TPU v7x, 32 devices: a whole 2x2x4 slice. The times are simulated.
32 devices in a mesh: groups: 2 (over y), row: 4 (over z), col: 2 (over x), sub: 2 (over core).
Axes of the slice: x: 2, y: 2, z: 4, core: 2. Of those that a mesh axis runs over, the one named last changes fastest.
Arguments:
- density: bfloat16 [4096, 2048], P(('groups', 'row'), ('col', 'sub')), parts along dimension 0, as said below
- margin: bfloat16 [4096, 2048], P(('groups', 'row'), ('col', 'sub')), parts along dimension 0, as said below
- pattern_d: int32 [32, 16], P(('groups', 'row'), ('col', 'sub')), parts along dimension 0, may hold values from 0 to 1, as said below
- pattern_s: int32 [32, 16], P(('groups', 'row'), ('col', 'sub')), parts along dimension 0, may hold values from 0 to 1, as said below
- dipole: bfloat16 [3, 4096], P(None, ('groups', 'col', 'sub')), parts along dimension 1, may hold values from -0.125 to 0.125
- owner: int32 [3, 32768], P(None, ('groups', 'row', 'col', 'sub')), parts along dimension 1, may hold values from 0 to 2047
- centres: float32 [3, 32768], P(None, ('groups', 'row', 'col', 'sub')), parts along dimension 1, may hold values from 0 to 3
- angles: float32 [3, 32768], P(None, ('groups', 'row', 'col', 'sub')), parts along dimension 1, may hold values from -3.140625 to 3.140625
- velocity: float32 [3, 32768], P(None, ('groups', 'row', 'col', 'sub')), parts along dimension 1, may hold values from -6 to 6
- angmom: float32 [3, 32768], P(None, ('groups', 'row', 'col', 'sub')), parts along dimension 1, may hold values from -6 to 6
- halo_list: int32 [2, 8192], P(None, ('groups', 'row', 'col', 'sub')), parts along dimension 1, may hold values from 0 to 1023
- neighbours: int32 [32, 32768], P(None, ('groups', 'row', 'col', 'sub')), parts along dimension 1, may hold values from 0 to 1535
Outputs:
- qm_out: bfloat16 [4096, 2048], P(('groups', 'row'), ('col', 'sub')), parts along dimension 0
- centres_new: float32 [3, 32768], P(None, ('groups', 'row', 'col', 'sub')), parts along dimension 1
- velocity_new: float32 [3, 32768], P(None, ('groups', 'row', 'col', 'sub')), parts along dimension 1
- angmom_new: float32 [3, 32768], P(None, ('groups', 'row', 'col', 'sub')), parts along dimension 1
- orient_new: float32 [4, 32768], P(None, ('groups', 'row', 'col', 'sub')), parts along dimension 1
There are 2 independent parts, one for each index of `groups`. A program takes and returns all parts, laid end to end along the dimension named above; each array names one. Nothing has to cross between parts.
Inputs may be any that keep to these rules, and one draw needn't show every extreme that they name: density is symmetric. margin is symmetric. `pattern_d`: symmetric, ones on the diagonal. `pattern_s`: every block row holds exactly 1 ones in each aligned run of 4 block columns.
All inputs are finite; a program needn't handle non-finite values.
Results may differ from a plain program's by a relative error of at most 0.0075.
Values may be sent and summed in bfloat16 or wider, within the bound.
No kernel may reach another device: no remote copies, remote signals or barrier semaphores. Data moves between devices by JAX's collectives and lax.ppermute only.
A program may use at most 128 MiB of HBM per device.

v0:
```python
import functools

import jax
import jax.numpy as jnp
from jax import lax
from jax.experimental import pallas as pl
from jax.experimental.pallas import tpu as pltpu
from jax.sharding import PartitionSpec as P

BLOCK = 128
LANES = 128

CHARGE = (-0.834, 0.417, 0.417)
UNIT = 0.417
MULTIPLE = (-2.0, 1.0, 1.0)
OFFSET = ((0.0, 0.0, -0.12), (0.76, 0.0, 0.47), (-0.76, 0.0, 0.47))
COUPLE = 0.1
STEP_DT = 0.5
WATER_MASS = 1.0
INERTIA = 0.5
SOFTEN = 1.0

SHIFT = 1.0
SCALE = 65535.0 / 5.0

F32 = jnp.float32
BF16 = jnp.bfloat16

SIN_TERMS = (-1 / 6, 1 / 120, -1 / 5040, 1 / 362880, -1 / 39916800, 1 / 6227020800)
COS_TERMS = (-1 / 2, 1 / 24, -1 / 720, 1 / 40320, -1 / 3628800, 1 / 479001600, -1 / 87178291200)


def at(tile):
    return slice(tile * LANES, (tile + 1) * LANES)


def position():
    return lax.axis_index("row"), lax.axis_index(("col", "sub"))


def pick(table, index):
    return jnp.take_along_axis(table, index, axis=1, mode="promise_in_bounds")


def contract(left, right, dims):
    return lax.dot_general(left, right, (dims, ((), ())), preferred_element_type=F32)


def series(square, terms):
    total = jnp.full_like(square, terms[-1])
    for term in terms[-2::-1]:
        total = total * square + term
    return total * square + 1.0


def line_of(row, comp):
    return 3 * row + comp


def round8(count):
    return -(-count // 8) * 8


def open_kernel(
    ways,
    hist_rows,
    pat_d,
    pat_s,
    marg,
    dip,
    owner,
    centres,
    angles,
    halo,
    message,
    small,
    again,
    sites,
    quat,
    moments,
):
    rows_b, cols_b = pat_d.shape
    waters = owner.shape[1]
    here_col = position()[1]
    message[...] = jnp.zeros(message.shape, F32)
    moments[...] = jnp.zeros(moments.shape, F32)
    for col in range(cols_b):
        moments[3 * col : 3 * col + 3, :] = dip[:, at(col)].astype(F32)
    lane = lax.broadcasted_iota(jnp.int32, (1, LANES), 1)
    patterns = jnp.zeros((1, LANES), F32)
    for row in range(rows_b):
        chosen = jnp.int32(0)
        lines = slice(row * BLOCK, (row + 1) * BLOCK)
        for col in range(cols_b):
            chosen = chosen + col * pat_s[row, col]
            line = row * cols_b + col
            patterns = jnp.where(lane == line, pat_s[row, col].astype(F32), patterns)
            patterns = jnp.where(lane == rows_b * cols_b + line, pat_d[row, col].astype(F32), patterns)
        span = pl.ds(pl.multiple_of(chosen * BLOCK, BLOCK), BLOCK)
        block = marg[lines, span]
        for copy in (small, again):
            copy[lines, :] = block
        product = contract(dip[:, span], block, ((1,), (1,)))
        place = hist_rows + line_of(row, 0)
        message[place : place + 3, :] = product
    message[pl.ds(hist_rows + 3 * rows_b + here_col, 1), :] = patterns
    total = jnp.zeros((hist_rows, LANES), F32)
    for source in range(3):
        line = owner[source : source + 1, :]
        high = lax.broadcasted_iota(jnp.int32, (hist_rows, waters), 0) == (line >> 7)
        low = lax.broadcasted_iota(jnp.int32, (LANES, waters), 0) == (line & 127)
        total = total + contract(
            jnp.where(high, MULTIPLE[source], 0.0).astype(BF16),
            jnp.where(low, 1.0, 0.0).astype(BF16),
            ((1,), (1,)),
        )
    message[0:hist_rows, :] = total
    halo_at = hist_rows + round8(3 * rows_b + ways)
    water_sites(centres, angles, halo, sites, quat, message.at[halo_at:, :])


def water_sites(centres, angles, halo, sites, quat, listed):
    half_angle = 0.5 * angles[...]
    square = half_angle * half_angle
    sine = half_angle * series(square, SIN_TERMS)
    cosine = series(square, COS_TERMS)
    sin_r, sin_p, sin_y = sine[0:1], sine[1:2], sine[2:3]
    cos_r, cos_p, cos_y = cosine[0:1], cosine[1:2], cosine[2:3]
    comp_w = cos_r * cos_p * cos_y + sin_r * sin_p * sin_y
    comp_x = sin_r * cos_p * cos_y - cos_r * sin_p * sin_y
    comp_y = cos_r * sin_p * cos_y + sin_r * cos_p * sin_y
    comp_z = cos_r * cos_p * sin_y - sin_r * sin_p * cos_y
    for place, comp in enumerate((comp_w, comp_x, comp_y, comp_z)):
        quat[place : place + 1, :] = comp
    first = (
        1.0 - 2.0 * (comp_y * comp_y + comp_z * comp_z),
        2.0 * (comp_x * comp_y + comp_w * comp_z),
        2.0 * (comp_x * comp_z - comp_w * comp_y),
    )
    third = (
        2.0 * (comp_x * comp_z + comp_w * comp_y),
        2.0 * (comp_y * comp_z - comp_w * comp_x),
        1.0 - 2.0 * (comp_x * comp_x + comp_y * comp_y),
    )
    sites[...] = jnp.zeros(sites.shape, F32)
    for source in range(3):
        for compo in range(3):
            place = 3 * source + compo
            position = centres[compo : compo + 1, :] + third[compo] * OFFSET[source][2]
            if OFFSET[source][0] != 0.0:
                position = position + first[compo] * OFFSET[source][0]
            sites[place : place + 1, :] = position
    waters, tiles = centres.shape[1], halo.shape[1] // LANES
    for which in range(2):
        for tile in range(tiles):
            index = jnp.broadcast_to(halo[which : which + 1, at(tile)], (8, LANES))
            low, high = index & 127, index >> 7
            for part in range(2):
                found = jnp.zeros((8, LANES), F32)
                for source in range(waters // LANES):
                    value = pick(sites[8 * part : 8 * part + 8, at(source)], low)
                    found = jnp.where(high == source, value, found)
                for comp in range(8 * part, min(8 * part + 8, 9)):
                    place = (which * 9 + comp) * tiles + tile
                    listed[place : place + 1, :] = found[comp - 8 * part : comp - 8 * part + 1]


def merge_kernel(summed, first, second, out):
    if summed > 0:
        out[0:summed, :] = first[0:summed, :] + second[0:summed, :]
    count = first.shape[0] - summed
    if count > 0:
        out[summed : summed + count, :] = first[summed:, :]
        out[summed + count :, :] = second[summed:, :]


def turn_kernel(summed, block_rows, halo_rows, first, second, moments, out, halos):
    out[0:summed, :] = first[0:summed, :] + second[0:summed, :]
    count = (first.shape[0] - summed) // (block_rows + halo_rows)
    for number, ref in enumerate((first, second)):
        for block in range(count):
            start = summed + block * (block_rows + halo_rows)
            place = number * count + block
            out[summed + place * block_rows : summed + (place + 1) * block_rows, :] = ref[
                start : start + block_rows, :
            ]
            halos[place * halo_rows : (place + 1) * halo_rows, :] = ref[
                start + block_rows : start + block_rows + halo_rows, :
            ]
    out[summed + 2 * count * block_rows :, :] = moments[...]


def pair_kernel(rows_n, sites, halos, neighbours, force, table):
    waters, slots = sites.shape[1], neighbours.shape[0]
    depth = halos.shape[0] // rows_n
    own_tiles = waters // LANES
    tiles = table.shape[1]
    halo_tiles = (tiles - own_tiles) // 2

    def store(tile, lines):
        fixed = [(line * SCALE + (SHIFT * SCALE + 0.5)).astype(jnp.int32) for line in lines]
        for word in range(5):
            value = fixed[2 * word]
            if word < 4:
                value = value | ((fixed[2 * word + 1] - 32768) << 16)
            table[word, tile] = jnp.broadcast_to(value, (8, LANES))

    for tile in range(own_tiles):
        store(tile, [sites[word : word + 1, at(tile)] for word in range(9)])
    for which in range(2):
        here_row = position()[0]
        other = lax.rem(here_row + (rows_n - 1, 1)[which], rows_n)
        start = pl.multiple_of((here_row ^ other) * depth, 8)
        lines = halos[pl.ds(start, depth), :]
        for tile in range(halo_tiles):
            places = [(which * 9 + word) * halo_tiles + tile for word in range(9)]
            store(own_tiles + which * halo_tiles + tile, [lines[place : place + 1] for place in places])

    def one_tile(tile, carry):
        span = pl.ds(pl.multiple_of(tile * LANES, LANES), LANES)
        lines = sites[:, span]
        own = []
        for word in range(9):
            line = jnp.broadcast_to(lines[word : word + 1] * SCALE + SHIFT * SCALE, (8, LANES))
            own.append((line, line - 32768.0))
        near = [jnp.zeros((8, LANES), F32) for _ in range(9)]
        far = [jnp.zeros((8, LANES), F32) for _ in range(9)]
        for pair in range(slots // 16):
            index = [neighbours[16 * pair + 8 * part : 16 * pair + 8 * part + 8, span] for part in range(2)]
            low = [value & 127 for value in index]
            high = [value >> 7 for value in index]
            found = [[None, None] for _ in range(5)]
            for source in range(tiles):
                here = [value == source for value in high]
                for word in range(5):
                    line = table[word, source]
                    for part in range(2):
                        value = pick(line, low[part])
                        found[word][part] = (
                            value if source == 0 else jnp.where(here[part], value, found[word][part])
                        )
            for part in range(2):
                places = []
                for word in range(9):
                    value = found[word // 2][part]
                    if word == 8:
                        places.append(value.astype(F32))
                    elif word % 2 == 0:
                        places.append((value & 65535).astype(F32))
                    else:
                        places.append((value >> 16).astype(F32))
                for source in range(3):
                    for target in range(3):
                        gap = []
                        for compo in range(3):
                            mine, other = 3 * source + compo, 3 * target + compo
                            gap.append(own[mine][other % 2] - places[other])
                        root = lax.rsqrt(
                            gap[0] * gap[0] + gap[1] * gap[1] + gap[2] * gap[2] + SOFTEN * SCALE * SCALE
                        )
                        weight = root * root * root
                        sums = near if target == 0 else far
                        for compo in range(3):
                            sums[3 * source + compo] = sums[3 * source + compo] + gap[compo] * weight
        for place in range(9):
            factor = CHARGE[place // 3] * UNIT * SCALE * SCALE
            total = factor * (far[place] - 2.0 * near[place])
            force[place : place + 1, span] = jnp.sum(total, axis=0, keepdims=True)
        return carry

    lax.fori_loop(0, own_tiles, one_tile, 0)


def pattern_flags(message, place):
    line = jnp.broadcast_to(message[pl.ds(place, 1), :], (8, LANES))
    return lambda block: pick(line, jnp.full((8, LANES), block, jnp.int32))[0:1].astype(BF16)


def field_kernel(ways, hist_rows, block_rows, summed, message, *refs):
    dens, out, masked, lines = refs[:ways], refs[ways], refs[ways + 1], refs[ways + 2]
    rows, cols = dens[0].shape
    rows_b, cols_b = rows // BLOCK, cols // BLOCK
    depth = (message.shape[0] - summed) // ways
    here_row, here_col = position()
    result = jnp.zeros((16, rows), F32)
    lines[...] = jnp.zeros(lines.shape, F32)
    for step in range(ways):
        device = here_col ^ step
        flag = pattern_flags(message, hist_rows + 3 * rows_b + device)
        for col in range(cols_b):
            other = device * (cols_b // rows_b) + col // rows_b
            place = hist_rows + (here_row ^ other) * block_rows + line_of(col % rows_b, 0)
            start = summed + step * depth + 3 * col
            moment = message[start : start + 3, :]
            pot = UNIT * COUPLE * message[pl.ds(device * cols_b + col, 1), :]
            for comp in range(3):
                product = message[pl.ds(place + comp, 1), :]
                lines[comp : comp + 1, at(col)] = product + pot * moment[comp : comp + 1]
            lines[3:6, at(col)] = moment
            for row in range(rows_b):
                spot = slice(row * BLOCK, (row + 1) * BLOCK)
                target = slice(step * cols + col * BLOCK, step * cols + (col + 1) * BLOCK)
                masked[spot, target] = dens[step][spot, at(col)] * flag(rows_b * cols_b + row * cols_b + col)
        whole = lines[...]
        first = whole.astype(BF16).astype(F32)
        both = jnp.concatenate([first, whole - first], axis=0).astype(BF16)
        result = result + contract(both, masked[:, step * cols : (step + 1) * cols], ((1,), (1,)))
    total = result[0:8] + result[8:16]
    out[...] = jnp.zeros(out.shape, F32)
    for row in range(rows_b):
        pot = UNIT * COUPLE * message[pl.ds(here_row * rows_b + row, 1), :]
        start = line_of(row, 0)
        out[start : start + 3, :] = total[0:3, at(row)] + pot * total[3:6, at(row)]


def advance_kernel(
    rows_n,
    rows_b,
    fields,
    owner,
    sites,
    quat,
    pair,
    centres,
    velocity,
    angmom,
    centres_new,
    velocity_new,
    angmom_new,
    orient_new,
    force,
    table,
):
    waters = owner.shape[1]
    depth = fields.shape[0] // rows_n
    here_row = position()[0]
    table[...] = jnp.zeros(table.shape, F32)
    for step in range(rows_n):
        for row in range(rows_b):
            start = step * depth + line_of(row, 0)
            place = 8 * (step * rows_b + row)
            table[place : place + 3, :] = fields[start : start + 3, :]
    for tile in range(waters // LANES):
        for source in range(3):
            index = jnp.broadcast_to(owner[source : source + 1, at(tile)], (8, LANES))
            low, high = index & 127, index >> 7
            found = jnp.zeros((8, LANES), F32)
            for step in range(rows_n):
                base = (here_row ^ step) * rows_b
                for row in range(rows_b):
                    place = 8 * (step * rows_b + row)
                    value = pick(table[place : place + 8, :], low)
                    found = jnp.where(high == base + row, value, found)
            lines = slice(3 * source, 3 * source + 3)
            force[lines, at(tile)] = pair[lines, at(tile)] + CHARGE[source] * found[0:3]

    def cross(left, right):
        return [
            left[1] * right[2] - left[2] * right[1],
            left[2] * right[0] - left[0] * right[2],
            left[0] * right[1] - left[1] * right[0],
        ]

    def split(array):
        return [array[compo : compo + 1, :] for compo in range(3)]

    total = force[0:3, :] + force[3:6, :] + force[6:9, :]
    torque = None
    centre = split(centres)
    for source in range(3):
        lever = [sites[3 * source + compo : 3 * source + compo + 1, :] - centre[compo] for compo in range(3)]
        push = [force[3 * source + compo : 3 * source + compo + 1, :] for compo in range(3)]
        turn = cross(lever, push)
        torque = turn if torque is None else [old + new for old, new in zip(torque, turn)]
    moving = velocity[...] + STEP_DT * total / WATER_MASS
    velocity_new[...] = moving
    centres_new[...] = centres[...] + STEP_DT * moving
    spin = [angmom[compo : compo + 1, :] + STEP_DT * torque[compo] for compo in range(3)]
    for compo in range(3):
        angmom_new[compo : compo + 1, :] = spin[compo]
    omega = [value * (1.0 / INERTIA) for value in spin]
    scalar = quat[0:1, :]
    vector = [quat[compo + 1 : compo + 2, :] for compo in range(3)]
    delta = [-(omega[0] * vector[0] + omega[1] * vector[1] + omega[2] * vector[2])]
    turned = cross(omega, vector)
    delta = delta + [scalar * omega[compo] + turned[compo] for compo in range(3)]
    moved = [old + 0.5 * STEP_DT * new for old, new in zip([scalar] + vector, delta)]
    length = jnp.sqrt(moved[0] * moved[0] + moved[1] * moved[1] + moved[2] * moved[2] + moved[3] * moved[3])
    for place in range(4):
        orient_new[place : place + 1, :] = moved[place] / length


def product_kernel(rows_n, hist_rows, block_rows, message, *refs):
    dens, small = refs[0], refs[1 : 1 + rows_n]
    out, panel = refs[1 + rows_n :]
    rows, cols = out.shape
    rows_b, cols_b = rows // BLOCK, cols // BLOCK
    here_row, here_col = position()
    for step in range(rows_n):
        other = here_row ^ step
        base = (here_col ^ (other * rows // cols)) * cols + lax.rem(other * rows, cols)
        flag = pattern_flags(message, hist_rows + step * block_rows + 3 * rows_b + here_col)
        for row in range(rows_b):
            block = small[step][row * BLOCK : (row + 1) * BLOCK, :]
            start = pl.multiple_of(base + row * BLOCK, BLOCK)
            for col in range(cols_b):
                panel[pl.ds(start, BLOCK), at(col)] = block * flag(row * cols_b + col)
    for row in range(rows_b):
        lines = slice(row * BLOCK, (row + 1) * BLOCK)
        own = UNIT * COUPLE * message[pl.ds(here_row * rows_b + row, 1), :]
        across = jnp.transpose(jnp.broadcast_to(own, (BLOCK, BLOCK)))
        value = contract(dens[lines, :], panel[...], ((1,), (0,)))
        for col in range(cols_b):
            pot = UNIT * COUPLE * message[pl.ds(here_col * cols_b + col, 1), :]
            sums = (across + pot) * dens[lines, at(col)].astype(F32)
            out[lines, at(col)] = (value[:, at(col)] + sums).astype(BF16)


def tie_kernel(first, second, out):
    pass


VMEM = pl.BlockSpec(memory_space=pltpu.VMEM)
SMEM = pl.BlockSpec(memory_space=pltpu.SMEM)


def fetching(kernel, places, *refs):
    refs, semaphore = list(refs[:-1]), refs[-1]
    held = refs[len(refs) - len(places) :]
    copies = [pltpu.make_async_copy(refs[at_], held[n], semaphore.at[n]) for n, at_ in enumerate(places)]
    for copy in copies:
        copy.start()
    for copy in copies:
        copy.wait()
    for n, at_ in enumerate(places):
        refs[at_] = held[n]
    kernel(*refs[: len(refs) - len(places)])


def call(
    kernel, name, outs, operands, scalars=0, scratch=(), cost=(0, 0), whole=VMEM, fetch=(), limit=48 << 20, **more
):
    in_specs = [SMEM] * scalars + [whole] * (len(operands) - scalars)
    scratch = list(scratch)
    if fetch:
        for place in fetch:
            memory = pltpu.SMEM if place < scalars else pltpu.VMEM
            scratch.append(memory(operands[place].shape, operands[place].dtype))
            in_specs[place] = pl.BlockSpec(memory_space=pltpu.HBM)
        scratch.append(pltpu.SemaphoreType.DMA((len(fetch),)))
        kernel = functools.partial(fetching, kernel, tuple(fetch))
    return pl.pallas_call(
        kernel,
        out_shape=[jax.ShapeDtypeStruct(shape, dtype) for shape, dtype in outs],
        in_specs=in_specs,
        out_specs=[whole] * len(outs),
        scratch_shapes=scratch,
        compiler_params=pltpu.CompilerParams(vmem_limit_bytes=limit),
        cost_estimate=pl.CostEstimate(flops=cost[0], bytes_accessed=cost[1], transcendentals=0),
        name=name,
        **more,
    )(*operands)


def doublings(count):
    step = 1
    while step < count:
        yield step
        step = 2 * step


def shards(
    density,
    margin,
    pattern_d,
    pattern_s,
    dipole,
    owner,
    centres,
    angles,
    velocity,
    angmom,
    halo_list,
    neighbours,
):
    rows, cols = density.shape
    rows_b, cols_b = pattern_d.shape
    rows_n = lax.axis_size("row")
    across = ("col", "sub")
    ways = lax.axis_size("col") * lax.axis_size("sub")
    hist_rows = rows * rows_n // LANES
    waters, listed = centres.shape[1], halo_list.shape[1]
    block_rows = round8(3 * rows_b + ways)
    halo_rows = round8(18 * (listed // LANES))
    summed = hist_rows + rows_n * block_rows
    field_rows = round8(3 * rows_b)
    moment_rows = round8(3 * cols_b)

    def swap(value, axis, count, step):
        return lax.ppermute(value, axis, [(i, i ^ step) for i in range(count)])

    def tie(value, later):
        (value,) = call(
            tie_kernel,
            "tie",
            [(value.shape, value.dtype)],
            [value, later],
            whole=pl.BlockSpec(memory_space=pl.ANY),
            input_output_aliases={0: 0},
        )
        return value

    def merge(first, second, count):
        total = 2 * first.shape[0] - count
        (out,) = call(functools.partial(merge_kernel, count), "merge", [((total, LANES), F32)], [first, second])
        return out

    def send(value, axis, count):
        held = [value] + [None] * (count - 1)
        for step in doublings(count):
            held[step] = swap(value, axis, count, step)
        return held

    def relay(held, axis, count, later):
        for step in range(1, count):
            lowest = step & -step
            if step != lowest:
                if (step - lowest) & (step - lowest - 1) == 0:
                    held[step - lowest] = tie(held[step - lowest], later)
                held[step] = swap(held[step - lowest], axis, count, lowest)
        return held

    dens_all = send(density, across, ways)
    message, small, again, sites, quat, moments = call(
        functools.partial(open_kernel, ways, hist_rows),
        "open",
        [
            ((hist_rows + block_rows + halo_rows, LANES), F32),
            ((rows, BLOCK), BF16),
            ((rows, BLOCK), BF16),
            ((16, waters), F32),
            ((4, waters), F32),
            ((moment_rows, LANES), F32),
        ],
        [pattern_d, pattern_s, margin, dipole, owner, centres, angles, halo_list],
        scalars=2,
        cost=(10**6, 12 * 10**6),
        fetch=range(8),
        limit=60 << 20,
    )
    small_all = [small] + [None] * (rows_n - 1)
    small_all[1] = swap(small, "row", rows_n, 1)
    steps = list(doublings(rows_n))
    for step in steps[:-1]:
        message = merge(message, swap(message, "row", rows_n, step), hist_rows)
    message, halos = call(
        functools.partial(turn_kernel, hist_rows, block_rows, halo_rows),
        "turn",
        [((summed + moment_rows, LANES), F32), ((rows_n * halo_rows, LANES), F32)],
        [message, swap(message, "row", rows_n, steps[-1]), moments],
    )
    dens_all = relay(dens_all, across, ways, message)
    for step in doublings(ways):
        message = merge(message, swap(message, across, ways, step), summed)
        if step == 1:
            later = tie(again, message)
            for further in steps[1:]:
                small_all[further] = swap(later, "row", rows_n, further)
    field, masked = call(
        functools.partial(field_kernel, ways, hist_rows, block_rows, summed),
        "field",
        [((field_rows, LANES), F32), ((rows, ways * cols), BF16)],
        [message] + dens_all,
        scratch=[pltpu.VMEM((8, cols), F32)],
        cost=(10**6, 5 * 10**6),
    )
    tiles = (waters + 2 * listed) // LANES
    (pair,) = call(
        functools.partial(pair_kernel, rows_n),
        "pair_forces",
        [((9, waters), F32)],
        [sites, halos, neighbours],
        scratch=[pltpu.VMEM((5, tiles, 8, LANES), jnp.int32)],
        cost=(10**6, 15 * 10**6),
    )
    for step in doublings(rows_n):
        field = merge(field, swap(field, "row", rows_n, step), 0)
        if step == 1:
            small_all = relay(small_all, "row", rows_n, field)
    (qm_out,) = call(
        functools.partial(product_kernel, rows_n, hist_rows, block_rows),
        "product",
        [((rows, cols), BF16)],
        [message, masked] + small_all,
        scratch=[pltpu.VMEM((rows * rows_n, cols), BF16)],
        cost=(10**6, 15 * 10**6),
    )
    centres_new, velocity_new, angmom_new, orient_new = call(
        functools.partial(advance_kernel, rows_n, rows_b),
        "advance",
        [((3, waters), F32), ((3, waters), F32), ((3, waters), F32), ((4, waters), F32)],
        [field, owner, sites, quat, pair, centres, velocity, angmom],
        scratch=[pltpu.VMEM((16, waters), F32), pltpu.VMEM((8 * hist_rows, LANES), F32)],
        cost=(10**6, 6 * 10**6),
    )
    return (qm_out, centres_new, velocity_new, angmom_new, orient_new)


def solution(mesh):
    square = P(("groups", "row"), ("col", "sub"))
    spread = P(None, ("groups", "row", "col", "sub"))
    return jax.shard_map(
        shards,
        mesh=mesh,
        in_specs=(square,) * 4 + (P(None, ("groups", "col", "sub")),) + (spread,) * 7,
        out_specs=(square,) + (spread,) * 4,
        check_vma=False,
    )
```

profile of v0, /device:TPU:0, one launch (start us, length us, event | category | flops | bytes accessed | tf_op | source)
XLA Modules:
  0.0 40.9 jit_solution(2210149948771791130)
XLA Ops:
  0.6 0.0 copy-start
  0.6 3.0 %collective-permute-start.5 = (bf16[512,512]{1,0:T(8,128)(2,1)}, bf16[512,512]{1,0:T(8,128)(2,1)S(1)}, u32[]{:S(2)}, u32[]{:S(2)}) collective-permute-start(bf16[512,512]{1,0:T(8,128)(2,1)} %refs_0_.3), channel_id=1, source_target_pairs={{0,2},{1,3},{2,0},{3,1},{4,6},{5,7},{6,4},{7,5},{8,10},{9,11},{10,... | collective-permute-start | bytes 1572872 | tf_op jit(solution)/shard_map/ppermute | solution.py:500
  3.6 2.2 %open.1 = (f32[72,128]{1,0:T(8,128)}, bf16[512,128]{1,0:T(8,128)(2,1)}, bf16[512,128]{1,0:T(8,128)(2,1)}, f32[16,1024]{1,0:T(8,128)}, f32[4,1024]{1,0:T(4,128)}, /*index=5*/f32[16,128]{1,0:T(8,128)}) custom-call(s32[4,4]{1,0:T(4,128)} %refs_0_.2, s32[4,4]{1,0:T(4,128)} %refs_1_.1, bf16[512,512]{1,0:T(8,128)(2,1)} %refs_2_.1, bf16[3,512]{1,0:T(4,128)(2,1)} %refs_3_.1, ...), custom_call_target="tpu_custom_call" | custom-call | flops 1000000 | bytes 12000000 | tf_op jit(solution)/shard_map/open/pallas_call | solution.py:452
  5.8 0.0 copy-start.2
  5.8 1.6 %collective-permute-start = (f32[72,128]{1,0:T(8,128)}, f32[72,128]{1,0:T(8,128)S(1)}, u32[]{:S(2)}, u32[]{:S(2)}) collective-permute-start(f32[72,128]{1,0:T(8,128)} %get-tuple-element.19.first), channel_id=1, source_target_pairs={{0,4},{4,0},{8,12},{12,8},{1,5},{5,1},{9,13},{13,9},{2,6},{6,2},{1... | collective-permute-start | bytes 110600 | tf_op jit(solution)/shard_map/ppermute | solution.py:500
  7.5 2.6 %collective-permute-done.second = f32[72,128]{1,0:T(8,128)S(1)} collective-permute-done((f32[72,128]{1,0:T(8,128)}, f32[72,128]{1,0:T(8,128)S(1)}, u32[]{:S(2)}, u32[]{:S(2)}) %collective-permute-start) | collective-permute-done | bytes 36896 | tf_op jit(solution)/shard_map/ppermute | solution.py:500
  10.1 0.0 copy-start.6
  10.1 0.8 %copy-done.6 = f32[72,128]{1,0:T(8,128)S(1)} copy-done((f32[72,128]{1,0:T(8,128)S(1)}, f32[72,128]{1,0:T(8,128)}, u32[]{:S(2)}) %copy-start.6) | copy-done | bytes 36888
  10.8 2.6 %collective-permute-start.1 = (f32[128,128]{1,0:T(8,128)S(1)}, f32[128,128]{1,0:T(8,128)S(1)}, u32[]{:S(2)}, u32[]{:S(2)}) collective-permute-start(f32[128,128]{1,0:T(8,128)S(1)} %merge.5.first), channel_id=1, source_target_pairs={{0,8},{4,12},{8,0},{12,4},{1,9},{5,13},{9,1},{13,5},{2,10},{6,14},... | collective-permute-start | bytes 196616 | tf_op jit(solution)/shard_map/ppermute | solution.py:500
  13.4 0.0 collective-permute-start.4
  13.4 2.6 %collective-permute-done.1.second = f32[128,128]{1,0:T(8,128)S(1)} collective-permute-done((f32[128,128]{1,0:T(8,128)S(1)}, f32[128,128]{1,0:T(8,128)S(1)}, u32[]{:S(2)}, u32[]{:S(2)}) %collective-permute-start.1) | collective-permute-done | bytes 65568 | tf_op jit(solution)/shard_map/ppermute | solution.py:500
  16.0 0.0 copy-start.10
  16.0 0.7 %copy-done.10 = f32[16,128]{1,0:T(8,128)S(1)} copy-done((f32[16,128]{1,0:T(8,128)S(1)}, f32[16,128]{1,0:T(8,128)}, u32[]{:S(2)}) %copy-start.10) | copy-done | bytes 8216
  16.7 0.0 collective-permute-done.5.first
  16.7 0.0 copy-start.1
  16.7 0.0 copy-start.3
  16.8 0.0 copy-start.4
  16.8 0.0 copy-start.5
  16.8 0.0 copy-start.7
  16.8 0.0 copy-start.8
  16.8 0.0 copy-start.9
  16.8 0.1 collective-permute-start.6
  16.9 0.5 %collective-permute-start.2 = (f32[96,128]{1,0:T(8,128)S(1)}, f32[96,128]{1,0:T(8,128)S(1)}, u32[]{:S(2)}, u32[]{:S(2)}) collective-permute-start(f32[96,128]{1,0:T(8,128)S(1)} %get-tuple-element.21.first.second), channel_id=1, source_target_pairs={{0,1},{1,0},{2,3},{3,2},{4,5},{5,4},{6,7},{7,6},{8,9},{9,8},{10,11... | collective-permute-start | bytes 147464 | tf_op jit(solution)/shard_map/ppermute | solution.py:500
  17.4 1.5 %collective-permute-done.2.second = f32[96,128]{1,0:T(8,128)S(1)} collective-permute-done((f32[96,128]{1,0:T(8,128)S(1)}, f32[96,128]{1,0:T(8,128)S(1)}, u32[]{:S(2)}, u32[]{:S(2)}) %collective-permute-start.2) | collective-permute-done | bytes 49184 | tf_op jit(solution)/shard_map/ppermute | solution.py:500
  18.9 2.7 %collective-permute-start.8 = (bf16[512,128]{1,0:T(8,128)(2,1)}, bf16[512,128]{1,0:T(8,128)(2,1)S(1)}, u32[]{:S(2)}, u32[]{:S(2)}) collective-permute-start(bf16[512,128]{1,0:T(8,128)(2,1)} %tie.4), channel_id=1, source_target_pairs={{0,8},{4,12},{8,0},{12,4},{1,9},{5,13},{9,1},{13,5},{2,10},{6,14},... | collective-permute-start | bytes 393224 | tf_op jit(solution)/shard_map/ppermute | solution.py:500
  21.6 0.7 %collective-permute-start.3 = (f32[112,128]{1,0:T(8,128)S(1)}, f32[112,128]{1,0:T(8,128)S(1)}, u32[]{:S(2)}, u32[]{:S(2)}) collective-permute-start(f32[112,128]{1,0:T(8,128)S(1)} %merge.6.first.second), channel_id=1, source_target_pairs={{0,2},{1,3},{2,0},{3,1},{4,6},{5,7},{6,4},{7,5},{8,10},{9,11},{10,... | collective-permute-start | bytes 172040 | tf_op jit(solution)/shard_map/ppermute | solution.py:500
  22.3 3.5 %collective-permute-done.3.second = f32[112,128]{1,0:T(8,128)S(1)} collective-permute-done((f32[112,128]{1,0:T(8,128)S(1)}, f32[112,128]{1,0:T(8,128)S(1)}, u32[]{:S(2)}, u32[]{:S(2)}) %collective-permute-start.3) | collective-permute-done | bytes 57376 | tf_op jit(solution)/shard_map/ppermute | solution.py:500
  25.8 0.0 collective-permute-done.4.refs_1_
  25.8 0.0 collective-permute-done.6.refs_3_
  25.8 0.0 copy-done
  25.8 0.8 %field.1 = (f32[16,128]{1,0:T(8,128)S(1)}, bf16[512,2048]{1,0:T(8,128)(2,1)S(1)}) custom-call(f32[144,128]{1,0:T(8,128)S(1)} %merge.7.message, bf16[512,512]{1,0:T(8,128)(2,1)S(1)} %copy-done, bf16[512,512]{1,0:T(8,128)(2,1)S(1)} %collective-permute-done.4.refs_1_, bf16[512,512]{1,0:T(8,128)(2,1)S(1)} %tie.3.refs_2_, ...), custom_call_target="tpu_custom_call" | custom-call | flops 1000000 | bytes 5000000 | tf_op jit(solution)/shard_map/field/pallas_call | solution.py:452
  26.6 2.1 %collective-permute-start.9 = (f32[16,128]{1,0:T(8,128)S(1)}, f32[16,128]{1,0:T(8,128)S(1)}, u32[]{:S(2)}, u32[]{:S(2)}) collective-permute-start(f32[16,128]{1,0:T(8,128)S(1)} %get-tuple-element.25.first), channel_id=1, source_target_pairs={{0,4},{4,0},{8,12},{12,8},{1,5},{5,1},{9,13},{13,9},{2,6},{6,2},{1... | collective-permute-start | bytes 24584 | tf_op jit(solution)/shard_map/ppermute | solution.py:500
  28.8 0.0 copy-done.2
  28.8 0.1 collective-permute-start.7
  28.9 1.6 %collective-permute-done.9.second = f32[16,128]{1,0:T(8,128)S(1)} collective-permute-done((f32[16,128]{1,0:T(8,128)S(1)}, f32[16,128]{1,0:T(8,128)S(1)}, u32[]{:S(2)}, u32[]{:S(2)}) %collective-permute-start.9) | collective-permute-done | bytes 8224 | tf_op jit(solution)/shard_map/ppermute | solution.py:500
  30.5 0.0 collective-permute-done.8.first
  30.5 1.9 %collective-permute-start.10 = (bf16[512,128]{1,0:T(8,128)(2,1)S(1)}, bf16[512,128]{1,0:T(8,128)(2,1)S(1)}, u32[]{:S(2)}, u32[]{:S(2)}) collective-permute-start(bf16[512,128]{1,0:T(8,128)(2,1)S(1)} %tie.5.refs_3_), channel_id=1, source_target_pairs={{0,4},{4,0},{8,12},{12,8},{1,5},{5,1},{9,13},{13,9},{2,6},{6,2},{1... | collective-permute-start | bytes 393224 | tf_op jit(solution)/shard_map/ppermute | solution.py:500
  32.4 0.4 collective-permute-start.11
  32.8 0.0 copy-done.1
  32.8 0.0 copy-done.3
  32.8 4.0 %pair_forces.1.pair = f32[9,1024]{1,0:T(8,128)S(1)} custom-call(f32[16,1024]{1,0:T(8,128)S(1)} %copy-done.1, f32[160,128]{1,0:T(8,128)S(1)} %get-tuple-element.28.halos, s32[32,1024]{1,0:T(8,128)S(1)} %copy-done.3), custom_call_target="tpu_custom_call" | custom-call | flops 1000000 | bytes 15000000 | tf_op jit(solution)/shard_map/pair_forces/pallas_call | solution.py:452
  36.8 0.3 collective-permute-done.11.second
  37.1 0.0 copy-done.4
  37.1 0.0 copy-done.5
  37.1 0.0 copy-done.7
  37.1 0.0 copy-done.8
  37.1 0.0 copy-done.9
  37.1 1.2 %advance.1 = (f32[3,1024]{1,0:T(4,128)}, f32[3,1024]{1,0:T(4,128)}, f32[3,1024]{1,0:T(4,128)}, f32[4,1024]{1,0:T(4,128)}) custom-call(f32[64,128]{1,0:T(8,128)S(1)} %merge.9.fields, s32[3,1024]{1,0:T(4,128)S(1)} %copy-done.4, f32[16,1024]{1,0:T(8,128)S(1)} %copy-done.1, f32[4,1024]{1,0:T(4,128)S(1)} %copy-done.9, f32[9,1024]{1,0:T(8,128)S(1)} %pair_forces.1.pair, ...), custom_call_target="tpu_custom_call" | custom-call | flops 1000000 | bytes 6000000 | tf_op jit(solution)/shard_map/advance/pallas_call | solution.py:452
  38.4 0.0 collective-permute-done.7.refs_2_
  38.4 0.0 collective-permute-done.10.refs_4_
  38.4 2.5 %product.1 = bf16[512,512]{1,0:T(8,128)(2,1)} custom-call(f32[144,128]{1,0:T(8,128)S(1)} %merge.7.message, bf16[512,2048]{1,0:T(8,128)(2,1)S(1)} %get-tuple-element.22.refs_0_, bf16[512,128]{1,0:T(8,128)(2,1)S(1)} %copy-done.2, bf16[512,128]{1,0:T(8,128)(2,1)S(1)} %collective-permute-done.7.refs_2_, bf16[512,128]{1,0:T(8,128)(2,1)S(1)} %tie.5.refs_3_, ...), custom_call_target="tpu_custom_call" | custom-call | flops 1000000 | bytes 15000000 | tf_op jit(solution)/shard_map/product/pallas_call | solution.py:452
  (9 shorter events, 0.0 us)
Async XLA Ops:
  0.6 25.2 %copy-start = (bf16[512,512]{1,0:T(8,128)(2,1)S(1)}, bf16[512,512]{1,0:T(8,128)(2,1)}, u32[]{:S(2)}) copy-start(bf16[512,512]{1,0:T(8,128)(2,1)} %refs_0_.3) | copy-start | bytes 1572868
  0.6 16.1 %collective-permute-start.5 = (bf16[512,512]{1,0:T(8,128)(2,1)}, bf16[512,512]{1,0:T(8,128)(2,1)S(1)}, u32[]{:S(2)}, u32[]{:S(2)}) collective-permute-start(bf16[512,512]{1,0:T(8,128)(2,1)} %refs_0_.3), channel_id=1, source_target_pairs={{0,2},{1,3},{2,0},{3,1},{4,6},{5,7},{6,4},{7,5},{8,10},{9,11},{10,... | collective-permute-start | bytes 1572872 | tf_op jit(solution)/shard_map/ppermute | solution.py:500
  5.8 23.0 %copy-start.2 = (bf16[512,128]{1,0:T(8,128)(2,1)S(1)}, bf16[512,128]{1,0:T(8,128)(2,1)}, u32[]{:S(2)}) copy-start(bf16[512,128]{1,0:T(8,128)(2,1)} %get-tuple-element.23.refs_1_) | copy-start | bytes 393220
  5.8 4.2 %collective-permute-start = (f32[72,128]{1,0:T(8,128)}, f32[72,128]{1,0:T(8,128)S(1)}, u32[]{:S(2)}, u32[]{:S(2)}) collective-permute-start(f32[72,128]{1,0:T(8,128)} %get-tuple-element.19.first), channel_id=1, source_target_pairs={{0,4},{4,0},{8,12},{12,8},{1,5},{5,1},{9,13},{13,9},{2,6},{6,2},{1... | collective-permute-start | bytes 110600 | tf_op jit(solution)/shard_map/ppermute | solution.py:500
  10.1 0.8 %copy-start.6 = (f32[72,128]{1,0:T(8,128)S(1)}, f32[72,128]{1,0:T(8,128)}, u32[]{:S(2)}) copy-start(f32[72,128]{1,0:T(8,128)} %get-tuple-element.19.first) | copy-start | bytes 110596
  10.8 5.2 %collective-permute-start.1 = (f32[128,128]{1,0:T(8,128)S(1)}, f32[128,128]{1,0:T(8,128)S(1)}, u32[]{:S(2)}, u32[]{:S(2)}) collective-permute-start(f32[128,128]{1,0:T(8,128)S(1)} %merge.5.first), channel_id=1, source_target_pairs={{0,8},{4,12},{8,0},{12,4},{1,9},{5,13},{9,1},{13,5},{2,10},{6,14},... | collective-permute-start | bytes 196616 | tf_op jit(solution)/shard_map/ppermute | solution.py:500
  13.4 12.4 %collective-permute-start.4 = (bf16[512,512]{1,0:T(8,128)(2,1)}, bf16[512,512]{1,0:T(8,128)(2,1)S(1)}, u32[]{:S(2)}, u32[]{:S(2)}) collective-permute-start(bf16[512,512]{1,0:T(8,128)(2,1)} %refs_0_.3), channel_id=1, source_target_pairs={{0,1},{1,0},{2,3},{3,2},{4,5},{5,4},{6,7},{7,6},{8,9},{9,8},{10,11... | collective-permute-start | bytes 1572872 | tf_op jit(solution)/shard_map/ppermute | solution.py:500
  16.0 0.7 %copy-start.10 = (f32[16,128]{1,0:T(8,128)S(1)}, f32[16,128]{1,0:T(8,128)}, u32[]{:S(2)}) copy-start(f32[16,128]{1,0:T(8,128)} %get-tuple-element.20.moments) | copy-start | bytes 24580
  16.7 16.1 %copy-start.1 = (f32[16,1024]{1,0:T(8,128)S(1)}, f32[16,1024]{1,0:T(8,128)}, u32[]{:S(2)}) copy-start(f32[16,1024]{1,0:T(8,128)} %get-tuple-element.26.sites) | copy-start | bytes 196612
  16.7 16.1 %copy-start.3 = (s32[32,1024]{1,0:T(8,128)S(1)}, s32[32,1024]{1,0:T(8,128)}, u32[]{:S(2)}) copy-start(s32[32,1024]{1,0:T(8,128)} %neighbours.1) | copy-start | bytes 393220
  16.8 20.3 %copy-start.4 = (s32[3,1024]{1,0:T(4,128)S(1)}, s32[3,1024]{1,0:T(4,128)}, u32[]{:S(2)}) copy-start(s32[3,1024]{1,0:T(4,128)} %owner.1) | copy-start | bytes 36868
  16.8 20.3 %copy-start.5 = (f32[3,1024]{1,0:T(4,128)S(1)}, f32[3,1024]{1,0:T(4,128)}, u32[]{:S(2)}) copy-start(f32[3,1024]{1,0:T(4,128)} %centres.1) | copy-start | bytes 36868
  16.8 20.3 %copy-start.7 = (f32[3,1024]{1,0:T(4,128)S(1)}, f32[3,1024]{1,0:T(4,128)}, u32[]{:S(2)}) copy-start(f32[3,1024]{1,0:T(4,128)} %velocity.1) | copy-start | bytes 36868
  16.8 20.3 %copy-start.8 = (f32[3,1024]{1,0:T(4,128)S(1)}, f32[3,1024]{1,0:T(4,128)}, u32[]{:S(2)}) copy-start(f32[3,1024]{1,0:T(4,128)} %angmom.1) | copy-start | bytes 36868
  16.8 20.3 %copy-start.9 = (f32[4,1024]{1,0:T(4,128)S(1)}, f32[4,1024]{1,0:T(4,128)}, u32[]{:S(2)}) copy-start(f32[4,1024]{1,0:T(4,128)} %get-tuple-element.27.quat) | copy-start | bytes 49156
  16.8 9.0 %collective-permute-start.6 = (bf16[512,512]{1,0:T(8,128)(2,1)S(1)}, bf16[512,512]{1,0:T(8,128)(2,1)S(1)}, u32[]{:S(2)}, u32[]{:S(2)}) collective-permute-start(bf16[512,512]{1,0:T(8,128)(2,1)S(1)} %tie.3.refs_2_), channel_id=1, source_target_pairs={{0,1},{1,0},{2,3},{3,2},{4,5},{5,4},{6,7},{7,6},{8,9},{9,8},{10,11... | collective-permute-start | bytes 1572872 | tf_op jit(solution)/shard_map/ppermute | solution.py:500
  16.9 2.0 %collective-permute-start.2 = (f32[96,128]{1,0:T(8,128)S(1)}, f32[96,128]{1,0:T(8,128)S(1)}, u32[]{:S(2)}, u32[]{:S(2)}) collective-permute-start(f32[96,128]{1,0:T(8,128)S(1)} %get-tuple-element.21.first.second), channel_id=1, source_target_pairs={{0,1},{1,0},{2,3},{3,2},{4,5},{5,4},{6,7},{7,6},{8,9},{9,8},{10,11... | collective-permute-start | bytes 147464 | tf_op jit(solution)/shard_map/ppermute | solution.py:500
  18.9 11.6 %collective-permute-start.8 = (bf16[512,128]{1,0:T(8,128)(2,1)}, bf16[512,128]{1,0:T(8,128)(2,1)S(1)}, u32[]{:S(2)}, u32[]{:S(2)}) collective-permute-start(bf16[512,128]{1,0:T(8,128)(2,1)} %tie.4), channel_id=1, source_target_pairs={{0,8},{4,12},{8,0},{12,4},{1,9},{5,13},{9,1},{13,5},{2,10},{6,14},... | collective-permute-start | bytes 393224 | tf_op jit(solution)/shard_map/ppermute | solution.py:500
  21.6 4.2 %collective-permute-start.3 = (f32[112,128]{1,0:T(8,128)S(1)}, f32[112,128]{1,0:T(8,128)S(1)}, u32[]{:S(2)}, u32[]{:S(2)}) collective-permute-start(f32[112,128]{1,0:T(8,128)S(1)} %merge.6.first.second), channel_id=1, source_target_pairs={{0,2},{1,3},{2,0},{3,1},{4,6},{5,7},{6,4},{7,5},{8,10},{9,11},{10,... | collective-permute-start | bytes 172040 | tf_op jit(solution)/shard_map/ppermute | solution.py:500
  26.6 3.8 %collective-permute-start.9 = (f32[16,128]{1,0:T(8,128)S(1)}, f32[16,128]{1,0:T(8,128)S(1)}, u32[]{:S(2)}, u32[]{:S(2)}) collective-permute-start(f32[16,128]{1,0:T(8,128)S(1)} %get-tuple-element.25.first), channel_id=1, source_target_pairs={{0,4},{4,0},{8,12},{12,8},{1,5},{5,1},{9,13},{13,9},{2,6},{6,2},{1... | collective-permute-start | bytes 24584 | tf_op jit(solution)/shard_map/ppermute | solution.py:500
  28.8 9.6 %collective-permute-start.7 = (bf16[512,128]{1,0:T(8,128)(2,1)S(1)}, bf16[512,128]{1,0:T(8,128)(2,1)S(1)}, u32[]{:S(2)}, u32[]{:S(2)}) collective-permute-start(bf16[512,128]{1,0:T(8,128)(2,1)S(1)} %copy-done.2), channel_id=1, source_target_pairs={{0,4},{4,0},{8,12},{12,8},{1,5},{5,1},{9,13},{13,9},{2,6},{6,2},{1... | collective-permute-start | bytes 393224 | tf_op jit(solution)/shard_map/ppermute | solution.py:500
  30.5 7.9 %collective-permute-start.10 = (bf16[512,128]{1,0:T(8,128)(2,1)S(1)}, bf16[512,128]{1,0:T(8,128)(2,1)S(1)}, u32[]{:S(2)}, u32[]{:S(2)}) collective-permute-start(bf16[512,128]{1,0:T(8,128)(2,1)S(1)} %tie.5.refs_3_), channel_id=1, source_target_pairs={{0,4},{4,0},{8,12},{12,8},{1,5},{5,1},{9,13},{13,9},{2,6},{6,2},{1... | collective-permute-start | bytes 393224 | tf_op jit(solution)/shard_map/ppermute | solution.py:500
  32.4 4.6 %collective-permute-start.11 = (f32[32,128]{1,0:T(8,128)S(1)}, f32[32,128]{1,0:T(8,128)S(1)}, u32[]{:S(2)}, u32[]{:S(2)}) collective-permute-start(f32[32,128]{1,0:T(8,128)S(1)} %merge.8.second.first), channel_id=1, source_target_pairs={{0,8},{4,12},{8,0},{12,4},{1,9},{5,13},{9,1},{13,5},{2,10},{6,14},... | collective-permute-start | bytes 49160 | tf_op jit(solution)/shard_map/ppermute | solution.py:500
where the time goes:
time: 41.1 us; the launch traced here: 40.9 us
  starting transfers between devices  15.7 us (38%)
  waiting for transfers between devices  12.1 us (29%)
  Pallas kernels  10.7 us (26%)
  local copies, waits for them, and re-layouts  1.52 us (4%)
  between operations  0.82 us (2%)
    ppermute x12, starting transfers between devices, swap(): return lax.ppermute(value, axis, [(i, i ^ step) for i in range(count)])  15.7 us
    ppermute x12, waiting for transfers between devices, swap(): return lax.ppermute(value, axis, [(i, i ^ step) for i in range(count)])  12.1 us
    pallas_call x14, Pallas kernels, call(): pl.pallas_call(kernel, out_shape=[jax.ShapeDtypeStruct(shape, dtype) for...  10.7 us
    unnamed x22, local copies, waits for them, and re-layouts  1.52 us
  transfers between devices with their start and end apart: 12, of which 6 were waited for; matrix products, arithmetic and copies ran while one was open for 0% of the time, Pallas kernels for 20%

commit v1 on v0

--- a/solution.py
+++ b/solution.py
@@ -77,15 +77,11 @@
     again,
     sites,
     quat,
-    moments,
 ):
     rows_b, cols_b = pat_d.shape
     waters = owner.shape[1]
     here_col = position()[1]
     message[...] = jnp.zeros(message.shape, F32)
-    moments[...] = jnp.zeros(moments.shape, F32)
-    for col in range(cols_b):
-        moments[3 * col : 3 * col + 3, :] = dip[:, at(col)].astype(F32)
     lane = lax.broadcasted_iota(jnp.int32, (1, LANES), 1)
     patterns = jnp.zeros((1, LANES), F32)
     for row in range(rows_b):
@@ -165,7 +161,8 @@
                     listed[place : place + 1, :] = found[comp - 8 * part : comp - 8 * part + 1]
 
 
-def merge_kernel(summed, first, second, out):
+def merge_kernel(summed, first, second, *refs):
+    out = refs[-1]
     if summed > 0:
         out[0:summed, :] = first[0:summed, :] + second[0:summed, :]
     count = first.shape[0] - summed
@@ -174,7 +171,7 @@
         out[summed + count :, :] = second[summed:, :]
 
 
-def turn_kernel(summed, block_rows, halo_rows, first, second, moments, out, halos):
+def turn_kernel(summed, block_rows, halo_rows, first, second, moments, done, out, halos):
     out[0:summed, :] = first[0:summed, :] + second[0:summed, :]
     count = (first.shape[0] - summed) // (block_rows + halo_rows)
     for number, ref in enumerate((first, second)):
@@ -190,31 +187,68 @@
     out[summed + 2 * count * block_rows :, :] = moments[...]
 
 
-def pair_kernel(rows_n, sites, halos, neighbours, force, table):
+def store_words(table, tile, lines):
+    fixed = [(line * SCALE + (SHIFT * SCALE + 0.5)).astype(jnp.int32) for line in lines]
+    for word in range(5):
+        value = fixed[2 * word]
+        if word < 4:
+            value = value | ((fixed[2 * word + 1] - 32768) << 16)
+        table[word, tile] = jnp.broadcast_to(value, (8, LANES))
+
+
+def gather_words(table, base, index, found):
+    low = [value & 127 for value in index]
+    high = [value >> 7 for value in index]
+    for source in range(table.shape[1]):
+        here = [value == base + source for value in high]
+        for word in range(5):
+            line = table[word, source]
+            for part in range(len(index)):
+                value = pick(line, low[part])
+                old = found[word][part]
+                found[word][part] = value if old is None else jnp.where(here[part], value, old)
+    return found
+
+
+def prepare_kernel(sites, dip, message, table, moments, held):
+    held[...] = message[...]
+    moments[...] = jnp.zeros(moments.shape, F32)
+    for col in range(dip.shape[1] // BLOCK):
+        moments[3 * col : 3 * col + 3, :] = dip[:, at(col)].astype(F32)
+    for tile in range(sites.shape[1] // LANES):
+        store_words(table, tile, [sites[word : word + 1, at(tile)] for word in range(9)])
+
+
+def own_kernel(table, neighbours, out):
+    slots, waters = neighbours.shape
+
+    def one_tile(tile, carry):
+        span = pl.ds(pl.multiple_of(tile * LANES, LANES), LANES)
+        for pair in range(slots // 16):
+            rows = [slice(16 * pair + 8 * part, 16 * pair + 8 * part + 8) for part in range(2)]
+            found = gather_words(table, 0, [neighbours[row, span] for row in rows], [[None, None] for _ in range(5)])
+            for word in range(5):
+                for part in range(2):
+                    start = word * slots + 16 * pair + 8 * part
+                    out[start : start + 8, span] = found[word][part]
+        return carry
+
+    lax.fori_loop(0, waters // LANES, one_tile, 0)
+
+
+def pair_kernel(rows_n, sites, own_words, halos, neighbours, force, table):
     waters, slots = sites.shape[1], neighbours.shape[0]
     depth = halos.shape[0] // rows_n
     own_tiles = waters // LANES
-    tiles = table.shape[1]
-    halo_tiles = (tiles - own_tiles) // 2
-
-    def store(tile, lines):
-        fixed = [(line * SCALE + (SHIFT * SCALE + 0.5)).astype(jnp.int32) for line in lines]
-        for word in range(5):
-            value = fixed[2 * word]
-            if word < 4:
-                value = value | ((fixed[2 * word + 1] - 32768) << 16)
-            table[word, tile] = jnp.broadcast_to(value, (8, LANES))
-
-    for tile in range(own_tiles):
-        store(tile, [sites[word : word + 1, at(tile)] for word in range(9)])
+    halo_tiles = table.shape[1] // 2
+    here_row = position()[0]
     for which in range(2):
-        here_row = position()[0]
         other = lax.rem(here_row + (rows_n - 1, 1)[which], rows_n)
         start = pl.multiple_of((here_row ^ other) * depth, 8)
         lines = halos[pl.ds(start, depth), :]
         for tile in range(halo_tiles):
             places = [(which * 9 + word) * halo_tiles + tile for word in range(9)]
-            store(own_tiles + which * halo_tiles + tile, [lines[place : place + 1] for place in places])
+            store_words(table, which * halo_tiles + tile, [lines[place : place + 1] for place in places])
 
     def one_tile(tile, carry):
         span = pl.ds(pl.multiple_of(tile * LANES, LANES), LANES)
@@ -226,19 +260,13 @@
         near = [jnp.zeros((8, LANES), F32) for _ in range(9)]
         far = [jnp.zeros((8, LANES), F32) for _ in range(9)]
         for pair in range(slots // 16):
-            index = [neighbours[16 * pair + 8 * part : 16 * pair + 8 * part + 8, span] for part in range(2)]
-            low = [value & 127 for value in index]
-            high = [value >> 7 for value in index]
-            found = [[None, None] for _ in range(5)]
-            for source in range(tiles):
-                here = [value == source for value in high]
-                for word in range(5):
-                    line = table[word, source]
-                    for part in range(2):
-                        value = pick(line, low[part])
-                        found[word][part] = (
-                            value if source == 0 else jnp.where(here[part], value, found[word][part])
-                        )
+            starts = [16 * pair + 8 * part for part in range(2)]
+            found = [
+                [own_words[word * slots + start : word * slots + start + 8, span] for start in starts]
+                for word in range(5)
+            ]
+            index = [neighbours[start : start + 8, span] for start in starts]
+            found = gather_words(table, own_tiles, index, found)
             for part in range(2):
                 places = []
                 for word in range(9):
@@ -405,8 +433,9 @@
             start = pl.multiple_of(base + row * BLOCK, BLOCK)
             for col in range(cols_b):
                 panel[pl.ds(start, BLOCK), at(col)] = block * flag(row * cols_b + col)
-    for row in range(rows_b):
-        lines = slice(row * BLOCK, (row + 1) * BLOCK)
+
+    def one_row(row, carry):
+        lines = pl.ds(pl.multiple_of(row * BLOCK, BLOCK), BLOCK)
         own = UNIT * COUPLE * message[pl.ds(here_row * rows_b + row, 1), :]
         across = jnp.transpose(jnp.broadcast_to(own, (BLOCK, BLOCK)))
         value = contract(dens[lines, :], panel[...], ((1,), (0,)))
@@ -414,6 +443,9 @@
             pot = UNIT * COUPLE * message[pl.ds(here_col * cols_b + col, 1), :]
             sums = (across + pot) * dens[lines, at(col)].astype(F32)
             out[lines, at(col)] = (value[:, at(col)] + sums).astype(BF16)
+        return carry
+
+    lax.fori_loop(0, rows_b, one_row, 0)
 
 
 def tie_kernel(first, second, out):
@@ -438,10 +470,12 @@
 
 
 def call(
-    kernel, name, outs, operands, scalars=0, scratch=(), cost=(0, 0), whole=VMEM, fetch=(), limit=48 << 20, **more
+    kernel, name, outs, operands, scalars=0, scratch=(), cost=(0, 0), whole=VMEM, fetch=(), unread=(), limit=48 << 20, **more
 ):
     in_specs = [SMEM] * scalars + [whole] * (len(operands) - scalars)
     scratch = list(scratch)
+    for place in unread:
+        in_specs[place] = pl.BlockSpec(memory_space=pl.ANY)
     if fetch:
         for place in fetch:
             memory = pltpu.SMEM if place < scalars else pltpu.VMEM
@@ -489,7 +523,7 @@
     across = ("col", "sub")
     ways = lax.axis_size("col") * lax.axis_size("sub")
     hist_rows = rows * rows_n // LANES
-    waters, listed = centres.shape[1], halo_list.shape[1]
+    waters, listed, slots = centres.shape[1], halo_list.shape[1], neighbours.shape[0]
     block_rows = round8(3 * rows_b + ways)
     halo_rows = round8(18 * (listed // LANES))
     summed = hist_rows + rows_n * block_rows
@@ -510,9 +544,16 @@
         )
         return value
 
-    def merge(first, second, count):
+    def merge(first, second, count, done=None):
         total = 2 * first.shape[0] - count
-        (out,) = call(functools.partial(merge_kernel, count), "merge", [((total, LANES), F32)], [first, second])
+        operands = [first, second] + ([] if done is None else [done])
+        (out,) = call(
+            functools.partial(merge_kernel, count),
+            "merge",
+            [((total, LANES), F32)],
+            operands,
+            unread=range(2, len(operands)),
+        )
         return out
 
     def send(value, axis, count):
@@ -531,7 +572,7 @@
         return held
 
     dens_all = send(density, across, ways)
-    message, small, again, sites, quat, moments = call(
+    message, small, again, sites, quat = call(
         functools.partial(open_kernel, ways, hist_rows),
         "open",
         [
@@ -540,7 +581,6 @@
             ((rows, BLOCK), BF16),
             ((16, waters), F32),
             ((4, waters), F32),
-            ((moment_rows, LANES), F32),
         ],
         [pattern_d, pattern_s, margin, dipole, owner, centres, angles, halo_list],
         scalars=2,
@@ -548,24 +588,42 @@
         fetch=range(8),
         limit=60 << 20,
     )
+    table, moments, held = call(
+        prepare_kernel,
+        "prepare",
+        [
+            ((5, waters // LANES, 8, LANES), jnp.int32),
+            ((moment_rows, LANES), F32),
+            (message.shape, F32),
+        ],
+        [sites, dipole, message],
+    )
+    (found,) = call(
+        own_kernel,
+        "own_gathers",
+        [((5 * slots, waters), jnp.int32)],
+        [table, neighbours],
+        cost=(10**6, 6 * 10**6),
+    )
     small_all = [small] + [None] * (rows_n - 1)
     small_all[1] = swap(small, "row", rows_n, 1)
     steps = list(doublings(rows_n))
     for step in steps[:-1]:
-        message = merge(message, swap(message, "row", rows_n, step), hist_rows)
+        message = merge(held, swap(message, "row", rows_n, step), hist_rows, moments)
+        held = message
+    later = tie(again, message)
     message, halos = call(
         functools.partial(turn_kernel, hist_rows, block_rows, halo_rows),
         "turn",
         [((summed + moment_rows, LANES), F32), ((rows_n * halo_rows, LANES), F32)],
-        [message, swap(message, "row", rows_n, steps[-1]), moments],
-    )
+        [message, swap(message, "row", rows_n, steps[-1]), moments, found],
+        unread=(3,),
+    )
+    for step in steps[1:]:
+        small_all[step] = swap(later, "row", rows_n, step)
     dens_all = relay(dens_all, across, ways, message)
     for step in doublings(ways):
         message = merge(message, swap(message, across, ways, step), summed)
-        if step == 1:
-            later = tie(again, message)
-            for further in steps[1:]:
-                small_all[further] = swap(later, "row", rows_n, further)
     field, masked = call(
         functools.partial(field_kernel, ways, hist_rows, block_rows, summed),
         "field",
@@ -574,13 +632,12 @@
         scratch=[pltpu.VMEM((8, cols), F32)],
         cost=(10**6, 5 * 10**6),
     )
-    tiles = (waters + 2 * listed) // LANES
     (pair,) = call(
         functools.partial(pair_kernel, rows_n),
         "pair_forces",
         [((9, waters), F32)],
-        [sites, halos, neighbours],
-        scratch=[pltpu.VMEM((5, tiles, 8, LANES), jnp.int32)],
+        [sites, found, halos, neighbours],
+        scratch=[pltpu.VMEM((5, 2 * listed // LANES, 8, LANES), jnp.int32)],
         cost=(10**6, 15 * 10**6),
     )
     for step in doublings(rows_n):

time: 41.1 us -> 39.7 us (0.966)
  waiting for transfers between devices: 12.1 us -> 7.22 us
  local copies, waits for them, and re-layouts: 1.52 us -> 3.24 us
  Pallas kernels: 10.7 us -> 12 us
  starting transfers between devices: 15.7 us -> 16.2 us
    ppermute x12, waiting for transfers between devices: 12.1 us -> 7.22 us  [swap(): return lax.ppermute(value, axis, [(i, i ^ step) for i in range(count)])]
    unnamed x22 -> x26, local copies, waits for them, and re-layouts: 1.52 us -> 3.24 us
    pallas_call x14 -> x16, Pallas kernels: 10.7 us -> 12 us  [call(): pl.pallas_call(kernel, out_shape=[jax.ShapeDtypeStruct(shape, dtype) for...]
    ppermute x12, starting transfers between devices: 15.7 us -> 16.2 us  [swap(): return lax.ppermute(value, axis, [(i, i ^ step) for i in range(count)])]
  transfers between devices with their start and end apart: 12 -> 12, of which waited for: 6 -> 5; matrix products, arithmetic and copies ran while one was open for 0% -> 0% of each run, Pallas kernels for 20% -> 23%
where the time goes in v1:
time: 39.7 us; the launch traced here: 39.4 us
  starting transfers between devices  16.2 us (41%)
  Pallas kernels  12 us (30%)
  waiting for transfers between devices  7.22 us (18%)
  local copies, waits for them, and re-layouts  3.24 us (8%)
  between operations  0.81 us (2%)
    ppermute x12, starting transfers between devices, swap(): return lax.ppermute(value, axis, [(i, i ^ step) for i in range(count)])  16.2 us
    pallas_call x16, Pallas kernels, call(): pl.pallas_call(kernel, out_shape=[jax.ShapeDtypeStruct(shape, dtype) for...  12 us
    ppermute x12, waiting for transfers between devices, swap(): return lax.ppermute(value, axis, [(i, i ^ step) for i in range(count)])  7.22 us
    unnamed x26, local copies, waits for them, and re-layouts  3.24 us
  transfers between devices with their start and end apart: 12, of which 5 were waited for; matrix products, arithmetic and copies ran while one was open for 0% of the time, Pallas kernels for 23%

profile of v1, /device:TPU:0, one launch (start us, length us, event | category | flops | bytes accessed | tf_op | source)
XLA Modules:
  0.0 39.4 jit_solution(6214572364034169519)
XLA Ops:
  0.6 0.0 copy-start.2
  0.6 3.0 %collective-permute-start.5 = (bf16[512,512]{1,0:T(8,128)(2,1)}, bf16[512,512]{1,0:T(8,128)(2,1)S(1)}, u32[]{:S(2)}, u32[]{:S(2)}) collective-permute-start(bf16[512,512]{1,0:T(8,128)(2,1)} %refs_0_.3), channel_id=1, source_target_pairs={{0,2},{1,3},{2,0},{3,1},{4,6},{5,7},{6,4},{7,5},{8,10},{9,11},{10,... | collective-permute-start | bytes 1572872 | tf_op jit(solution)/shard_map/ppermute | solution.py:534
  3.6 2.2 %open.1 = (f32[72,128]{1,0:T(8,128)}, bf16[512,128]{1,0:T(8,128)(2,1)}, bf16[512,128]{1,0:T(8,128)(2,1)}, f32[16,1024]{1,0:T(8,128)}, f32[4,1024]{1,0:T(4,128)}) custom-call(s32[4,4]{1,0:T(4,128)} %refs_0_.2, s32[4,4]{1,0:T(4,128)} %refs_1_.1, bf16[512,512]{1,0:T(8,128)(2,1)} %refs_2_.1, bf16[3,512]{1,0:T(4,128)(2,1)} %dip.1, s32[3,1024]{1,0:T(4,128)} %owner.1, ...), custom_call_target="tpu_custom_call" | custom-call | flops 1000000 | bytes 12000000 | tf_op jit(solution)/shard_map/open/pallas_call | solution.py:486
  5.8 1.6 %collective-permute-start = (f32[72,128]{1,0:T(8,128)}, f32[72,128]{1,0:T(8,128)S(1)}, u32[]{:S(2)}, u32[]{:S(2)}) collective-permute-start(f32[72,128]{1,0:T(8,128)} %get-tuple-element.22.message), channel_id=1, source_target_pairs={{0,4},{4,0},{8,12},{12,8},{1,5},{5,1},{9,13},{13,9},{2,6},{6,2},{1... | collective-permute-start | bytes 110600 | tf_op jit(solution)/shard_map/ppermute | solution.py:534
  7.5 0.0 copy-start
  7.5 0.8 %copy-done = f32[16,1024]{1,0:T(8,128)S(1)} copy-done((f32[16,1024]{1,0:T(8,128)S(1)}, f32[16,1024]{1,0:T(8,128)}, u32[]{:S(2)}) %copy-start) | copy-done | bytes 65560
  8.3 0.0 copy-start.8
  8.3 0.8 %copy-done.8 = f32[72,128]{1,0:T(8,128)S(1)} copy-done((f32[72,128]{1,0:T(8,128)S(1)}, f32[72,128]{1,0:T(8,128)}, u32[]{:S(2)}) %copy-start.8) | copy-done | bytes 36888
  9.1 0.0 copy-start.9
  9.1 0.7 %copy-done.9 = bf16[3,512]{1,0:T(4,128)(2,1)S(1)} copy-done((bf16[3,512]{1,0:T(4,128)(2,1)S(1)}, bf16[3,512]{1,0:T(4,128)(2,1)}, u32[]{:S(2)}) %copy-start.9) | copy-done | bytes 3096
  9.8 0.0 copy-start.5
  9.8 0.1 prepare.1
  9.8 0.2 collective-permute-done.second
  10.1 2.6 %collective-permute-start.1 = (f32[128,128]{1,0:T(8,128)S(1)}, f32[128,128]{1,0:T(8,128)S(1)}, u32[]{:S(2)}, u32[]{:S(2)}) collective-permute-start(f32[128,128]{1,0:T(8,128)S(1)} %merge.5.first.second), channel_id=1, source_target_pairs={{0,8},{4,12},{8,0},{12,4},{1,9},{5,13},{9,1},{13,5},{2,10},{6,14},... | collective-permute-start | bytes 196616 | tf_op jit(solution)/shard_map/ppermute | solution.py:534
  12.7 0.0 collective-permute-start.4
  12.7 0.0 copy-start.3
  12.7 0.9 %copy-done.3 = s32[32,1024]{1,0:T(8,128)S(1)} copy-done((s32[32,1024]{1,0:T(8,128)S(1)}, s32[32,1024]{1,0:T(8,128)}, u32[]{:S(2)}) %copy-start.3) | copy-done | bytes 131096
  13.6 2.6 %own_gathers.1.done.own_words = s32[160,1024]{1,0:T(8,128)S(1)} custom-call(s32[5,8,8,128]{3,2,1,0:T(8,128)S(1)} %get-tuple-element.25.table, s32[32,1024]{1,0:T(8,128)S(1)} %copy-done.3), custom_call_target="tpu_custom_call" | custom-call | flops 1000000 | bytes 6000000 | tf_op jit(solution)/shard_map/own_gathers/pallas_call | solution.py:486
  16.2 0.0 collective-permute-done.1.second
  16.2 0.0 copy-start.4
  16.3 0.0 collective-permute-done.5.first
  16.3 0.0 copy-start.1
  16.3 0.6 %collective-permute-start.6 = (bf16[512,512]{1,0:T(8,128)(2,1)S(1)}, bf16[512,512]{1,0:T(8,128)(2,1)S(1)}, u32[]{:S(2)}, u32[]{:S(2)}) collective-permute-start(bf16[512,512]{1,0:T(8,128)(2,1)S(1)} %tie.3.refs_2_), channel_id=1, source_target_pairs={{0,1},{1,0},{2,3},{3,2},{4,5},{5,4},{6,7},{7,6},{8,9},{9,8},{10,11... | collective-permute-start | bytes 1572872 | tf_op jit(solution)/shard_map/ppermute | solution.py:534
  16.9 0.0 copy-done.5
  16.9 0.0 copy-start.6
  16.9 0.0 copy-start.7
  16.9 0.0 copy-start.10
  16.9 0.0 copy-start.11
  16.9 0.0 copy-start.12
  16.9 1.9 %collective-permute-start.8 = (bf16[512,128]{1,0:T(8,128)(2,1)S(1)}, bf16[512,128]{1,0:T(8,128)(2,1)S(1)}, u32[]{:S(2)}, u32[]{:S(2)}) collective-permute-start(bf16[512,128]{1,0:T(8,128)(2,1)S(1)} %tie.4), channel_id=1, source_target_pairs={{0,8},{4,12},{8,0},{12,4},{1,9},{5,13},{9,1},{13,5},{2,10},{6,14},... | collective-permute-start | bytes 393224 | tf_op jit(solution)/shard_map/ppermute | solution.py:534
  18.8 0.2 collective-permute-start.2
  19.0 1.0 %collective-permute-done.2.second = f32[96,128]{1,0:T(8,128)S(1)} collective-permute-done((f32[96,128]{1,0:T(8,128)S(1)}, f32[96,128]{1,0:T(8,128)S(1)}, u32[]{:S(2)}, u32[]{:S(2)}) %collective-permute-start.2) | collective-permute-done | bytes 49184 | tf_op jit(solution)/shard_map/ppermute | solution.py:534
  20.0 1.6 %collective-permute-start.3 = (f32[112,128]{1,0:T(8,128)S(1)}, f32[112,128]{1,0:T(8,128)S(1)}, u32[]{:S(2)}, u32[]{:S(2)}) collective-permute-start(f32[112,128]{1,0:T(8,128)S(1)} %merge.6.first), channel_id=1, source_target_pairs={{0,2},{1,3},{2,0},{3,1},{4,6},{5,7},{6,4},{7,5},{8,10},{9,11},{10,... | collective-permute-start | bytes 172040 | tf_op jit(solution)/shard_map/ppermute | solution.py:534
  21.6 2.7 %collective-permute-done.3.second = f32[112,128]{1,0:T(8,128)S(1)} collective-permute-done((f32[112,128]{1,0:T(8,128)S(1)}, f32[112,128]{1,0:T(8,128)S(1)}, u32[]{:S(2)}, u32[]{:S(2)}) %collective-permute-start.3) | collective-permute-done | bytes 57376 | tf_op jit(solution)/shard_map/ppermute | solution.py:534
  24.3 0.0 collective-permute-done.4.refs_1_
  24.3 0.0 collective-permute-done.6.refs_3_
  24.3 0.0 copy-done.2
  24.3 0.8 %field.1 = (f32[16,128]{1,0:T(8,128)S(1)}, bf16[512,2048]{1,0:T(8,128)(2,1)S(1)}) custom-call(f32[144,128]{1,0:T(8,128)S(1)} %merge.7.message, bf16[512,512]{1,0:T(8,128)(2,1)S(1)} %copy-done.2, bf16[512,512]{1,0:T(8,128)(2,1)S(1)} %collective-permute-done.4.refs_1_, bf16[512,512]{1,0:T(8,128)(2,1)S(1)} %tie.3.refs_2_, ...), custom_call_target="tpu_custom_call" | custom-call | flops 1000000 | bytes 5000000 | tf_op jit(solution)/shard_map/field/pallas_call | solution.py:486
  25.1 1.6 %collective-permute-start.9 = (f32[16,128]{1,0:T(8,128)S(1)}, f32[16,128]{1,0:T(8,128)S(1)}, u32[]{:S(2)}, u32[]{:S(2)}) collective-permute-start(f32[16,128]{1,0:T(8,128)S(1)} %get-tuple-element.30.first), channel_id=1, source_target_pairs={{0,4},{4,0},{8,12},{12,8},{1,5},{5,1},{9,13},{13,9},{2,6},{6,2},{1... | collective-permute-start | bytes 24584 | tf_op jit(solution)/shard_map/ppermute | solution.py:534
  26.7 0.0 copy-done.4
  26.7 0.4 %collective-permute-start.7 = (bf16[512,128]{1,0:T(8,128)(2,1)S(1)}, bf16[512,128]{1,0:T(8,128)(2,1)S(1)}, u32[]{:S(2)}, u32[]{:S(2)}) collective-permute-start(bf16[512,128]{1,0:T(8,128)(2,1)S(1)} %copy-done.4), channel_id=1, source_target_pairs={{0,4},{4,0},{8,12},{12,8},{1,5},{5,1},{9,13},{13,9},{2,6},{6,2},{1... | collective-permute-start | bytes 393224 | tf_op jit(solution)/shard_map/ppermute | solution.py:534
  27.2 1.6 %collective-permute-done.9.second = f32[16,128]{1,0:T(8,128)S(1)} collective-permute-done((f32[16,128]{1,0:T(8,128)S(1)}, f32[16,128]{1,0:T(8,128)S(1)}, u32[]{:S(2)}, u32[]{:S(2)}) %collective-permute-start.9) | collective-permute-done | bytes 8224 | tf_op jit(solution)/shard_map/ppermute | solution.py:534
  28.8 0.0 collective-permute-done.8.first
  28.8 1.6 %collective-permute-start.10 = (bf16[512,128]{1,0:T(8,128)(2,1)S(1)}, bf16[512,128]{1,0:T(8,128)(2,1)S(1)}, u32[]{:S(2)}, u32[]{:S(2)}) collective-permute-start(bf16[512,128]{1,0:T(8,128)(2,1)S(1)} %tie.5.refs_3_), channel_id=1, source_target_pairs={{0,4},{4,0},{8,12},{12,8},{1,5},{5,1},{9,13},{13,9},{2,6},{6,2},{1... | collective-permute-start | bytes 393224 | tf_op jit(solution)/shard_map/ppermute | solution.py:534
  30.4 1.1 %collective-permute-start.11 = (f32[32,128]{1,0:T(8,128)S(1)}, f32[32,128]{1,0:T(8,128)S(1)}, u32[]{:S(2)}, u32[]{:S(2)}) collective-permute-start(f32[32,128]{1,0:T(8,128)S(1)} %merge.8.second.first), channel_id=1, source_target_pairs={{0,8},{4,12},{8,0},{12,4},{1,9},{5,13},{9,1},{13,5},{2,10},{6,14},... | collective-permute-start | bytes 49160 | tf_op jit(solution)/shard_map/ppermute | solution.py:534
  31.5 0.0 copy-done.1
  31.5 1.9 %pair_forces.1.pair = f32[9,1024]{1,0:T(8,128)S(1)} custom-call(f32[16,1024]{1,0:T(8,128)S(1)} %copy-done.1, s32[160,1024]{1,0:T(8,128)S(1)} %own_gathers.1.done.own_words, f32[160,128]{1,0:T(8,128)S(1)} %get-tuple-element.32.halos, s32[32,1024]{1,0:T(8,128)S(1)} %copy-done.3), custom_call_target="tpu_custom_call" | custom-call | flops 1000000 | bytes 15000000 | tf_op jit(solution)/shard_map/pair_forces/pallas_call | solution.py:486
  33.4 1.6 %collective-permute-done.11.second = f32[32,128]{1,0:T(8,128)S(1)} collective-permute-done((f32[32,128]{1,0:T(8,128)S(1)}, f32[32,128]{1,0:T(8,128)S(1)}, u32[]{:S(2)}, u32[]{:S(2)}) %collective-permute-start.11) | collective-permute-done | bytes 16416 | tf_op jit(solution)/shard_map/ppermute | solution.py:534
  35.1 0.0 copy-done.6
  35.1 0.0 copy-done.7
  35.1 0.0 copy-done.10
  35.1 0.0 copy-done.11
  35.1 0.0 copy-done.12
  35.1 1.2 %advance.1 = (f32[3,1024]{1,0:T(4,128)}, f32[3,1024]{1,0:T(4,128)}, f32[3,1024]{1,0:T(4,128)}, f32[4,1024]{1,0:T(4,128)}) custom-call(f32[64,128]{1,0:T(8,128)S(1)} %merge.9.fields, s32[3,1024]{1,0:T(4,128)S(1)} %copy-done.6, f32[16,1024]{1,0:T(8,128)S(1)} %copy-done.1, f32[4,1024]{1,0:T(4,128)S(1)} %copy-done.12, f32[9,1024]{1,0:T(8,128)S(1)} %pair_forces.1.pair, ...), custom_call_target="tpu_custom_call" | custom-call | flops 1000000 | bytes 6000000 | tf_op jit(solution)/shard_map/advance/pallas_call | solution.py:486
  36.4 0.0 collective-permute-done.7.refs_2_
  36.4 0.0 collective-permute-done.10.refs_4_
  36.4 3.0 %product.1 = bf16[512,512]{1,0:T(8,128)(2,1)} custom-call(f32[144,128]{1,0:T(8,128)S(1)} %merge.7.message, bf16[512,2048]{1,0:T(8,128)(2,1)S(1)} %get-tuple-element.27.refs_0_, bf16[512,128]{1,0:T(8,128)(2,1)S(1)} %copy-done.4, bf16[512,128]{1,0:T(8,128)(2,1)S(1)} %collective-permute-done.7.refs_2_, bf16[512,128]{1,0:T(8,128)(2,1)S(1)} %tie.5.refs_3_, ...), custom_call_target="tpu_custom_call" | custom-call | flops 1000000 | bytes 15000000 | tf_op jit(solution)/shard_map/product/pallas_call | solution.py:486
  (9 shorter events, 0.0 us)
Async XLA Ops:
  0.6 23.6 %copy-start.2 = (bf16[512,512]{1,0:T(8,128)(2,1)S(1)}, bf16[512,512]{1,0:T(8,128)(2,1)}, u32[]{:S(2)}) copy-start(bf16[512,512]{1,0:T(8,128)(2,1)} %refs_0_.3) | copy-start | bytes 1572868
  0.6 15.6 %collective-permute-start.5 = (bf16[512,512]{1,0:T(8,128)(2,1)}, bf16[512,512]{1,0:T(8,128)(2,1)S(1)}, u32[]{:S(2)}, u32[]{:S(2)}) collective-permute-start(bf16[512,512]{1,0:T(8,128)(2,1)} %refs_0_.3), channel_id=1, source_target_pairs={{0,2},{1,3},{2,0},{3,1},{4,6},{5,7},{6,4},{7,5},{8,10},{9,11},{10,... | collective-permute-start | bytes 1572872 | tf_op jit(solution)/shard_map/ppermute | solution.py:534
  5.8 4.2 %collective-permute-start = (f32[72,128]{1,0:T(8,128)}, f32[72,128]{1,0:T(8,128)S(1)}, u32[]{:S(2)}, u32[]{:S(2)}) collective-permute-start(f32[72,128]{1,0:T(8,128)} %get-tuple-element.22.message), channel_id=1, source_target_pairs={{0,4},{4,0},{8,12},{12,8},{1,5},{5,1},{9,13},{13,9},{2,6},{6,2},{1... | collective-permute-start | bytes 110600 | tf_op jit(solution)/shard_map/ppermute | solution.py:534
  7.5 0.8 %copy-start = (f32[16,1024]{1,0:T(8,128)S(1)}, f32[16,1024]{1,0:T(8,128)}, u32[]{:S(2)}) copy-start(f32[16,1024]{1,0:T(8,128)} %get-tuple-element.21.sites) | copy-start | bytes 196612
  8.3 0.8 %copy-start.8 = (f32[72,128]{1,0:T(8,128)S(1)}, f32[72,128]{1,0:T(8,128)}, u32[]{:S(2)}) copy-start(f32[72,128]{1,0:T(8,128)} %get-tuple-element.22.message) | copy-start | bytes 110596
  9.1 0.7 %copy-start.9 = (bf16[3,512]{1,0:T(4,128)(2,1)S(1)}, bf16[3,512]{1,0:T(4,128)(2,1)}, u32[]{:S(2)}) copy-start(bf16[3,512]{1,0:T(4,128)(2,1)} %dip.1) | copy-start | bytes 9220
  9.8 7.1 %copy-start.5 = (bf16[512,128]{1,0:T(8,128)(2,1)S(1)}, bf16[512,128]{1,0:T(8,128)(2,1)}, u32[]{:S(2)}) copy-start(bf16[512,128]{1,0:T(8,128)(2,1)} %get-tuple-element.29.first) | copy-start | bytes 393220
  10.1 6.1 %collective-permute-start.1 = (f32[128,128]{1,0:T(8,128)S(1)}, f32[128,128]{1,0:T(8,128)S(1)}, u32[]{:S(2)}, u32[]{:S(2)}) collective-permute-start(f32[128,128]{1,0:T(8,128)S(1)} %merge.5.first.second), channel_id=1, source_target_pairs={{0,8},{4,12},{8,0},{12,4},{1,9},{5,13},{9,1},{13,5},{2,10},{6,14},... | collective-permute-start | bytes 196616 | tf_op jit(solution)/shard_map/ppermute | solution.py:534
  12.7 11.6 %collective-permute-start.4 = (bf16[512,512]{1,0:T(8,128)(2,1)}, bf16[512,512]{1,0:T(8,128)(2,1)S(1)}, u32[]{:S(2)}, u32[]{:S(2)}) collective-permute-start(bf16[512,512]{1,0:T(8,128)(2,1)} %refs_0_.3), channel_id=1, source_target_pairs={{0,1},{1,0},{2,3},{3,2},{4,5},{5,4},{6,7},{7,6},{8,9},{9,8},{10,11... | collective-permute-start | bytes 1572872 | tf_op jit(solution)/shard_map/ppermute | solution.py:534
  12.7 0.9 %copy-start.3 = (s32[32,1024]{1,0:T(8,128)S(1)}, s32[32,1024]{1,0:T(8,128)}, u32[]{:S(2)}) copy-start(s32[32,1024]{1,0:T(8,128)} %neighbours.3) | copy-start | bytes 393220
  16.2 10.5 %copy-start.4 = (bf16[512,128]{1,0:T(8,128)(2,1)S(1)}, bf16[512,128]{1,0:T(8,128)(2,1)}, u32[]{:S(2)}) copy-start(bf16[512,128]{1,0:T(8,128)(2,1)} %get-tuple-element.28.refs_1_) | copy-start | bytes 393220
  16.3 15.2 %copy-start.1 = (f32[16,1024]{1,0:T(8,128)S(1)}, f32[16,1024]{1,0:T(8,128)}, u32[]{:S(2)}) copy-start(f32[16,1024]{1,0:T(8,128)} %get-tuple-element.21.sites) | copy-start | bytes 196612
  16.3 8.0 %collective-permute-start.6 = (bf16[512,512]{1,0:T(8,128)(2,1)S(1)}, bf16[512,512]{1,0:T(8,128)(2,1)S(1)}, u32[]{:S(2)}, u32[]{:S(2)}) collective-permute-start(bf16[512,512]{1,0:T(8,128)(2,1)S(1)} %tie.3.refs_2_), channel_id=1, source_target_pairs={{0,1},{1,0},{2,3},{3,2},{4,5},{5,4},{6,7},{7,6},{8,9},{9,8},{10,11... | collective-permute-start | bytes 1572872 | tf_op jit(solution)/shard_map/ppermute | solution.py:534
  16.9 18.2 %copy-start.6 = (s32[3,1024]{1,0:T(4,128)S(1)}, s32[3,1024]{1,0:T(4,128)}, u32[]{:S(2)}) copy-start(s32[3,1024]{1,0:T(4,128)} %owner.1) | copy-start | bytes 36868
  16.9 18.2 %copy-start.7 = (f32[3,1024]{1,0:T(4,128)S(1)}, f32[3,1024]{1,0:T(4,128)}, u32[]{:S(2)}) copy-start(f32[3,1024]{1,0:T(4,128)} %centres.1) | copy-start | bytes 36868
  16.9 18.2 %copy-start.10 = (f32[3,1024]{1,0:T(4,128)S(1)}, f32[3,1024]{1,0:T(4,128)}, u32[]{:S(2)}) copy-start(f32[3,1024]{1,0:T(4,128)} %velocity.1) | copy-start | bytes 36868
  16.9 18.2 %copy-start.11 = (f32[3,1024]{1,0:T(4,128)S(1)}, f32[3,1024]{1,0:T(4,128)}, u32[]{:S(2)}) copy-start(f32[3,1024]{1,0:T(4,128)} %angmom.1) | copy-start | bytes 36868
  16.9 18.2 %copy-start.12 = (f32[4,1024]{1,0:T(4,128)S(1)}, f32[4,1024]{1,0:T(4,128)}, u32[]{:S(2)}) copy-start(f32[4,1024]{1,0:T(4,128)} %get-tuple-element.31.quat) | copy-start | bytes 49156
  16.9 11.9 %collective-permute-start.8 = (bf16[512,128]{1,0:T(8,128)(2,1)S(1)}, bf16[512,128]{1,0:T(8,128)(2,1)S(1)}, u32[]{:S(2)}, u32[]{:S(2)}) collective-permute-start(bf16[512,128]{1,0:T(8,128)(2,1)S(1)} %tie.4), channel_id=1, source_target_pairs={{0,8},{4,12},{8,0},{12,4},{1,9},{5,13},{9,1},{13,5},{2,10},{6,14},... | collective-permute-start | bytes 393224 | tf_op jit(solution)/shard_map/ppermute | solution.py:534
  18.8 1.2 %collective-permute-start.2 = (f32[96,128]{1,0:T(8,128)S(1)}, f32[96,128]{1,0:T(8,128)S(1)}, u32[]{:S(2)}, u32[]{:S(2)}) collective-permute-start(f32[96,128]{1,0:T(8,128)S(1)} %get-tuple-element.26.first.second), channel_id=1, source_target_pairs={{0,1},{1,0},{2,3},{3,2},{4,5},{5,4},{6,7},{7,6},{8,9},{9,8},{10,11... | collective-permute-start | bytes 147464 | tf_op jit(solution)/shard_map/ppermute | solution.py:534
  20.0 4.2 %collective-permute-start.3 = (f32[112,128]{1,0:T(8,128)S(1)}, f32[112,128]{1,0:T(8,128)S(1)}, u32[]{:S(2)}, u32[]{:S(2)}) collective-permute-start(f32[112,128]{1,0:T(8,128)S(1)} %merge.6.first), channel_id=1, source_target_pairs={{0,2},{1,3},{2,0},{3,1},{4,6},{5,7},{6,4},{7,5},{8,10},{9,11},{10,... | collective-permute-start | bytes 172040 | tf_op jit(solution)/shard_map/ppermute | solution.py:534
  25.1 3.7 %collective-permute-start.9 = (f32[16,128]{1,0:T(8,128)S(1)}, f32[16,128]{1,0:T(8,128)S(1)}, u32[]{:S(2)}, u32[]{:S(2)}) collective-permute-start(f32[16,128]{1,0:T(8,128)S(1)} %get-tuple-element.30.first), channel_id=1, source_target_pairs={{0,4},{4,0},{8,12},{12,8},{1,5},{5,1},{9,13},{13,9},{2,6},{6,2},{1... | collective-permute-start | bytes 24584 | tf_op jit(solution)/shard_map/ppermute | solution.py:534
  26.7 9.6 %collective-permute-start.7 = (bf16[512,128]{1,0:T(8,128)(2,1)S(1)}, bf16[512,128]{1,0:T(8,128)(2,1)S(1)}, u32[]{:S(2)}, u32[]{:S(2)}) collective-permute-start(bf16[512,128]{1,0:T(8,128)(2,1)S(1)} %copy-done.4), channel_id=1, source_target_pairs={{0,4},{4,0},{8,12},{12,8},{1,5},{5,1},{9,13},{13,9},{2,6},{6,2},{1... | collective-permute-start | bytes 393224 | tf_op jit(solution)/shard_map/ppermute | solution.py:534
  28.8 7.6 %collective-permute-start.10 = (bf16[512,128]{1,0:T(8,128)(2,1)S(1)}, bf16[512,128]{1,0:T(8,128)(2,1)S(1)}, u32[]{:S(2)}, u32[]{:S(2)}) collective-permute-start(bf16[512,128]{1,0:T(8,128)(2,1)S(1)} %tie.5.refs_3_), channel_id=1, source_target_pairs={{0,4},{4,0},{8,12},{12,8},{1,5},{5,1},{9,13},{13,9},{2,6},{6,2},{1... | collective-permute-start | bytes 393224 | tf_op jit(solution)/shard_map/ppermute | solution.py:534
  30.4 4.7 %collective-permute-start.11 = (f32[32,128]{1,0:T(8,128)S(1)}, f32[32,128]{1,0:T(8,128)S(1)}, u32[]{:S(2)}, u32[]{:S(2)}) collective-permute-start(f32[32,128]{1,0:T(8,128)S(1)} %merge.8.second.first), channel_id=1, source_target_pairs={{0,8},{4,12},{8,0},{12,4},{1,9},{5,13},{9,1},{13,5},{2,10},{6,14},... | collective-permute-start | bytes 49160 | tf_op jit(solution)/shard_map/ppermute | solution.py:534

commit v2 on v1

--- a/solution.py
+++ b/solution.py
@@ -196,13 +196,13 @@
         table[word, tile] = jnp.broadcast_to(value, (8, LANES))
 
 
-def gather_words(table, base, index, found):
+def gather_words(sources, index, found):
     low = [value & 127 for value in index]
     high = [value >> 7 for value in index]
-    for source in range(table.shape[1]):
-        here = [value == base + source for value in high]
+    for number, table, place in sources:
+        here = [value == number for value in high]
         for word in range(5):
-            line = table[word, source]
+            line = table[word, place]
             for part in range(len(index)):
                 value = pick(line, low[part])
                 old = found[word][part]
@@ -219,14 +219,15 @@
         store_words(table, tile, [sites[word : word + 1, at(tile)] for word in range(9)])
 
 
-def own_kernel(table, neighbours, out):
+def own_kernel(first, table, neighbours, out):
     slots, waters = neighbours.shape
+    sources = [(tile, table, tile) for tile in range(first)]
 
     def one_tile(tile, carry):
         span = pl.ds(pl.multiple_of(tile * LANES, LANES), LANES)
         for pair in range(slots // 16):
             rows = [slice(16 * pair + 8 * part, 16 * pair + 8 * part + 8) for part in range(2)]
-            found = gather_words(table, 0, [neighbours[row, span] for row in rows], [[None, None] for _ in range(5)])
+            found = gather_words(sources, [neighbours[row, span] for row in rows], [[None, None] for _ in range(5)])
             for word in range(5):
                 for part in range(2):
                     start = word * slots + 16 * pair + 8 * part
@@ -236,7 +237,7 @@
     lax.fori_loop(0, waters // LANES, one_tile, 0)
 
 
-def pair_kernel(rows_n, sites, own_words, halos, neighbours, force, table):
+def pair_kernel(rows_n, first, sites, own_words, own_table, halos, neighbours, force, table):
     waters, slots = sites.shape[1], neighbours.shape[0]
     depth = halos.shape[0] // rows_n
     own_tiles = waters // LANES
@@ -249,6 +250,9 @@
         for tile in range(halo_tiles):
             places = [(which * 9 + word) * halo_tiles + tile for word in range(9)]
             store_words(table, which * halo_tiles + tile, [lines[place : place + 1] for place in places])
+
+    sources = [(tile, own_table, tile) for tile in range(first, own_tiles)]
+    sources = sources + [(own_tiles + tile, table, tile) for tile in range(2 * halo_tiles)]
 
     def one_tile(tile, carry):
         span = pl.ds(pl.multiple_of(tile * LANES, LANES), LANES)
@@ -266,7 +270,7 @@
                 for word in range(5)
             ]
             index = [neighbours[start : start + 8, span] for start in starts]
-            found = gather_words(table, own_tiles, index, found)
+            found = gather_words(sources, index, found)
             for part in range(2):
                 places = []
                 for word in range(9):
@@ -305,7 +309,7 @@
 
 
 def field_kernel(ways, hist_rows, block_rows, summed, message, *refs):
-    dens, out, masked, lines = refs[:ways], refs[ways], refs[ways + 1], refs[ways + 2]
+    dens, out, masked, lines = refs[:ways], refs[ways + 1], refs[ways + 2], refs[ways + 3]
     rows, cols = dens[0].shape
     rows_b, cols_b = rows // BLOCK, cols // BLOCK
     depth = (message.shape[0] - summed) // ways
@@ -418,31 +422,38 @@
         orient_new[place : place + 1, :] = moved[place] / length
 
 
-def product_kernel(rows_n, hist_rows, block_rows, message, *refs):
-    dens, small = refs[0], refs[1 : 1 + rows_n]
-    out, panel = refs[1 + rows_n :]
+def product_kernel(steps, hist_rows, block_rows, message, dens, *refs):
+    count = len(steps)
+    small, before = refs[:count], refs[count:-2]
+    out, panel = refs[-2:]
     rows, cols = out.shape
     rows_b, cols_b = rows // BLOCK, cols // BLOCK
     here_row, here_col = position()
-    for step in range(rows_n):
+    spans = []
+    for place, step in enumerate(steps):
         other = here_row ^ step
         base = (here_col ^ (other * rows // cols)) * cols + lax.rem(other * rows, cols)
+        spans.append(pl.ds(pl.multiple_of(base, BLOCK), rows))
         flag = pattern_flags(message, hist_rows + step * block_rows + 3 * rows_b + here_col)
         for row in range(rows_b):
-            block = small[step][row * BLOCK : (row + 1) * BLOCK, :]
-            start = pl.multiple_of(base + row * BLOCK, BLOCK)
+            block = small[place][row * BLOCK : (row + 1) * BLOCK, :]
             for col in range(cols_b):
-                panel[pl.ds(start, BLOCK), at(col)] = block * flag(row * cols_b + col)
+                panel[place, row * BLOCK : (row + 1) * BLOCK, at(col)] = block * flag(row * cols_b + col)
 
     def one_row(row, carry):
         lines = pl.ds(pl.multiple_of(row * BLOCK, BLOCK), BLOCK)
-        own = UNIT * COUPLE * message[pl.ds(here_row * rows_b + row, 1), :]
-        across = jnp.transpose(jnp.broadcast_to(own, (BLOCK, BLOCK)))
-        value = contract(dens[lines, :], panel[...], ((1,), (0,)))
-        for col in range(cols_b):
-            pot = UNIT * COUPLE * message[pl.ds(here_col * cols_b + col, 1), :]
-            sums = (across + pot) * dens[lines, at(col)].astype(F32)
-            out[lines, at(col)] = (value[:, at(col)] + sums).astype(BF16)
+        value = contract(dens[lines, spans[0]], panel[0], ((1,), (0,)))
+        for place in range(1, count):
+            value = value + contract(dens[lines, spans[place]], panel[place], ((1,), (0,)))
+        if before:
+            out[lines, :] = (value + before[0][lines, :]).astype(out.dtype)
+        else:
+            own = UNIT * COUPLE * message[pl.ds(here_row * rows_b + row, 1), :]
+            across = jnp.transpose(jnp.broadcast_to(own, (BLOCK, BLOCK)))
+            for col in range(cols_b):
+                pot = UNIT * COUPLE * message[pl.ds(here_col * cols_b + col, 1), :]
+                sums = (across + pot) * dens[lines, at(col)].astype(F32)
+                out[lines, at(col)] = (value[:, at(col)] + sums).astype(out.dtype)
         return carry
 
     lax.fori_loop(0, rows_b, one_row, 0)
@@ -598,8 +609,9 @@
         ],
         [sites, dipole, message],
     )
+    first = -(-5 * (waters // LANES) // 8)
     (found,) = call(
-        own_kernel,
+        functools.partial(own_kernel, first),
         "own_gathers",
         [((5 * slots, waters), jnp.int32)],
         [table, neighbours],
@@ -624,34 +636,40 @@
     dens_all = relay(dens_all, across, ways, message)
     for step in doublings(ways):
         message = merge(message, swap(message, across, ways, step), summed)
+    (pair,) = call(
+        functools.partial(pair_kernel, rows_n, first),
+        "pair_forces",
+        [((9, waters), F32)],
+        [sites, found, table, halos, neighbours],
+        scratch=[pltpu.VMEM((5, 2 * listed // LANES, 8, LANES), jnp.int32)],
+        cost=(10**6, 15 * 10**6),
+    )
     field, masked = call(
         functools.partial(field_kernel, ways, hist_rows, block_rows, summed),
         "field",
         [((field_rows, LANES), F32), ((rows, ways * cols), BF16)],
-        [message] + dens_all,
+        [message] + dens_all + [pair],
+        unread=(1 + ways,),
         scratch=[pltpu.VMEM((8, cols), F32)],
         cost=(10**6, 5 * 10**6),
-    )
-    (pair,) = call(
-        functools.partial(pair_kernel, rows_n),
-        "pair_forces",
-        [((9, waters), F32)],
-        [sites, found, halos, neighbours],
-        scratch=[pltpu.VMEM((5, 2 * listed // LANES, 8, LANES), jnp.int32)],
-        cost=(10**6, 15 * 10**6),
     )
     for step in doublings(rows_n):
         field = merge(field, swap(field, "row", rows_n, step), 0)
         if step == 1:
             small_all = relay(small_all, "row", rows_n, field)
-    (qm_out,) = call(
-        functools.partial(product_kernel, rows_n, hist_rows, block_rows),
-        "product",
-        [((rows, cols), BF16)],
-        [message, masked] + small_all,
-        scratch=[pltpu.VMEM((rows * rows_n, cols), BF16)],
-        cost=(10**6, 15 * 10**6),
-    )
+    early = [0] + list(steps)
+    late = [step for step in range(rows_n) if step not in early]
+    partial, kinds = [], [(early, F32 if late else BF16)] + ([(late, BF16)] if late else [])
+    for these, kind in kinds:
+        partial = call(
+            functools.partial(product_kernel, these, hist_rows, block_rows),
+            "product",
+            [((rows, cols), kind)],
+            [message, masked] + [small_all[step] for step in these] + list(partial),
+            scratch=[pltpu.VMEM((len(these), rows, cols), BF16)],
+            cost=(10**6, 10 * 10**6),
+        )
+    (qm_out,) = partial
     centres_new, velocity_new, angmom_new, orient_new = call(
         functools.partial(advance_kernel, rows_n, rows_b),
         "advance",

time: 39.7 us -> 38.7 us (0.975)
  waiting for transfers between devices: 7.22 us -> 5.39 us
  Pallas kernels: 12 us -> 12.6 us
    ppermute x12, waiting for transfers between devices: 7.22 us -> 5.39 us  [swap(): return lax.ppermute(value, axis, [(i, i ^ step) for i in range(count)])]
    pallas_call x16 -> x17, Pallas kernels: 12 us -> 12.6 us  [call(): pl.pallas_call(kernel, out_shape=[jax.ShapeDtypeStruct(shape, dtype) for...]
    unnamed x26 -> x28, local copies, waits for them, and re-layouts: 3.24 us -> 3.26 us
  transfers between devices with their start and end apart: 12 -> 12, of which waited for: 5 -> 5; matrix products, arithmetic and copies ran while one was open for 0% -> 0% of each run, Pallas kernels for 23% -> 28%
where the time goes in v2:
time: 38.7 us; the launch traced here: 38.4 us
  starting transfers between devices  16.3 us (42%)
  Pallas kernels  12.6 us (33%)
  waiting for transfers between devices  5.39 us (14%)
  local copies, waits for them, and re-layouts  3.26 us (8%)
  between operations  0.85 us (2%)
    ppermute x12, starting transfers between devices, swap(): return lax.ppermute(value, axis, [(i, i ^ step) for i in range(count)])  16.3 us
    pallas_call x17, Pallas kernels, call(): pl.pallas_call(kernel, out_shape=[jax.ShapeDtypeStruct(shape, dtype) for...  12.6 us
    ppermute x12, waiting for transfers between devices, swap(): return lax.ppermute(value, axis, [(i, i ^ step) for i in range(count)])  5.39 us
    unnamed x28, local copies, waits for them, and re-layouts  3.26 us
  transfers between devices with their start and end apart: 12, of which 5 were waited for; matrix products, arithmetic and copies ran while one was open for 0% of the time, Pallas kernels for 28%

profile of v2, /device:TPU:0, one launch (start us, length us, event | category | flops | bytes accessed | tf_op | source)
XLA Modules:
  0.0 38.4 jit_solution(12168217542983466322)
XLA Ops:
  0.6 0.0 copy-start.4
  0.6 3.0 %collective-permute-start.5 = (bf16[512,512]{1,0:T(8,128)(2,1)}, bf16[512,512]{1,0:T(8,128)(2,1)S(1)}, u32[]{:S(2)}, u32[]{:S(2)}) collective-permute-start(bf16[512,512]{1,0:T(8,128)(2,1)} %refs_0_.3), channel_id=1, source_target_pairs={{0,2},{1,3},{2,0},{3,1},{4,6},{5,7},{6,4},{7,5},{8,10},{9,11},{10,... | collective-permute-start | bytes 1572872 | tf_op jit(solution)/shard_map/ppermute | solution.py:545
  3.6 2.2 %open.1 = (f32[72,128]{1,0:T(8,128)}, bf16[512,128]{1,0:T(8,128)(2,1)}, bf16[512,128]{1,0:T(8,128)(2,1)}, f32[16,1024]{1,0:T(8,128)}, f32[4,1024]{1,0:T(4,128)}) custom-call(s32[4,4]{1,0:T(4,128)} %refs_0_.2, s32[4,4]{1,0:T(4,128)} %refs_1_.1, bf16[512,512]{1,0:T(8,128)(2,1)} %refs_2_.1, bf16[3,512]{1,0:T(4,128)(2,1)} %dip.1, s32[3,1024]{1,0:T(4,128)} %owner.1, ...), custom_call_target="tpu_custom_call" | custom-call | flops 1000000 | bytes 12000000 | tf_op jit(solution)/shard_map/open/pallas_call | solution.py:497
  5.8 1.6 %collective-permute-start = (f32[72,128]{1,0:T(8,128)}, f32[72,128]{1,0:T(8,128)S(1)}, u32[]{:S(2)}, u32[]{:S(2)}) collective-permute-start(f32[72,128]{1,0:T(8,128)} %get-tuple-element.22.message), channel_id=1, source_target_pairs={{0,4},{4,0},{8,12},{12,8},{1,5},{5,1},{9,13},{13,9},{2,6},{6,2},{1... | collective-permute-start | bytes 110600 | tf_op jit(solution)/shard_map/ppermute | solution.py:545
  7.5 0.0 copy-start
  7.5 0.8 %copy-done = f32[16,1024]{1,0:T(8,128)S(1)} copy-done((f32[16,1024]{1,0:T(8,128)S(1)}, f32[16,1024]{1,0:T(8,128)}, u32[]{:S(2)}) %copy-start) | copy-done | bytes 65560
  8.3 0.0 copy-start.9
  8.3 0.8 %copy-done.9 = f32[72,128]{1,0:T(8,128)S(1)} copy-done((f32[72,128]{1,0:T(8,128)S(1)}, f32[72,128]{1,0:T(8,128)}, u32[]{:S(2)}) %copy-start.9) | copy-done | bytes 36888
  9.1 0.0 copy-start.10
  9.1 0.7 %copy-done.10 = bf16[3,512]{1,0:T(4,128)(2,1)S(1)} copy-done((bf16[3,512]{1,0:T(4,128)(2,1)S(1)}, bf16[3,512]{1,0:T(4,128)(2,1)}, u32[]{:S(2)}) %copy-start.10) | copy-done | bytes 3096
  9.8 0.0 copy-start.6
  9.8 0.0 copy-start.1
  9.8 0.1 prepare.1
  9.8 0.2 collective-permute-done.second
  10.1 2.6 %collective-permute-start.1 = (f32[128,128]{1,0:T(8,128)S(1)}, f32[128,128]{1,0:T(8,128)S(1)}, u32[]{:S(2)}, u32[]{:S(2)}) collective-permute-start(f32[128,128]{1,0:T(8,128)S(1)} %merge.5.first.second), channel_id=1, source_target_pairs={{0,8},{4,12},{8,0},{12,4},{1,9},{5,13},{9,1},{13,5},{2,10},{6,14},... | collective-permute-start | bytes 196616 | tf_op jit(solution)/shard_map/ppermute | solution.py:545
  12.7 0.0 collective-permute-start.4
  12.7 0.0 copy-start.3
  12.7 0.9 %copy-done.3 = s32[32,1024]{1,0:T(8,128)S(1)} copy-done((s32[32,1024]{1,0:T(8,128)S(1)}, s32[32,1024]{1,0:T(8,128)}, u32[]{:S(2)}) %copy-start.3) | copy-done | bytes 131096
  13.6 1.9 %own_gathers.1.done.own_words = s32[160,1024]{1,0:T(8,128)S(1)} custom-call(s32[5,8,8,128]{3,2,1,0:T(8,128)S(1)} %get-tuple-element.25.table.own_table, s32[32,1024]{1,0:T(8,128)S(1)} %copy-done.3), custom_call_target="tpu_custom_call" | custom-call | flops 1000000 | bytes 6000000 | tf_op jit(solution)/shard_map/own_gathers/pallas_call | solution.py:497
  15.5 0.0 copy-start.2
  15.5 0.0 collective-permute-done.1.second
  15.5 0.3 collective-permute-done.5.first
  15.8 0.0 copy-start.5
  15.8 0.3 collective-permute-start.6
  16.1 0.0 copy-done.6
  16.1 2.6 %collective-permute-start.7 = (bf16[512,128]{1,0:T(8,128)(2,1)S(1)}, bf16[512,128]{1,0:T(8,128)(2,1)S(1)}, u32[]{:S(2)}, u32[]{:S(2)}) collective-permute-start(bf16[512,128]{1,0:T(8,128)(2,1)S(1)} %tie.4), channel_id=1, source_target_pairs={{0,8},{4,12},{8,0},{12,4},{1,9},{5,13},{9,1},{13,5},{2,10},{6,14},... | collective-permute-start | bytes 393224 | tf_op jit(solution)/shard_map/ppermute | solution.py:545
  18.7 0.2 collective-permute-start.2
  18.9 1.1 %collective-permute-done.2.second = f32[96,128]{1,0:T(8,128)S(1)} collective-permute-done((f32[96,128]{1,0:T(8,128)S(1)}, f32[96,128]{1,0:T(8,128)S(1)}, u32[]{:S(2)}, u32[]{:S(2)}) %collective-permute-start.2) | collective-permute-done | bytes 49184 | tf_op jit(solution)/shard_map/ppermute | solution.py:545
  19.9 1.6 %collective-permute-start.3 = (f32[112,128]{1,0:T(8,128)S(1)}, f32[112,128]{1,0:T(8,128)S(1)}, u32[]{:S(2)}, u32[]{:S(2)}) collective-permute-start(f32[112,128]{1,0:T(8,128)S(1)} %merge.6.first), channel_id=1, source_target_pairs={{0,2},{1,3},{2,0},{3,1},{4,6},{5,7},{6,4},{7,5},{8,10},{9,11},{10,... | collective-permute-start | bytes 172040 | tf_op jit(solution)/shard_map/ppermute | solution.py:545
  21.5 0.0 copy-done.4
  21.5 0.0 copy-done.1
  21.5 2.7 %pair_forces.1.refs_4_.pair = f32[9,1024]{1,0:T(8,128)S(1)} custom-call(f32[16,1024]{1,0:T(8,128)S(1)} %copy-done.1, s32[160,1024]{1,0:T(8,128)S(1)} %own_gathers.1.done.own_words, s32[5,8,8,128]{3,2,1,0:T(8,128)S(1)} %get-tuple-element.25.table.own_table, f32[160,128]{1,0:T(8,128)S(1)} %get-tuple-element.27.halos, s32[32,1024]{1,0:T(8,128)S(1)} %copy-done.4), custom_call_target="tpu_custom_call" | custom-call | flops 1000000 | bytes 15000000 | tf_op jit(solution)/shard_map/pair_forces/pallas_call | solution.py:497
  24.2 0.0 collective-permute-done.3.second
  24.2 0.0 collective-permute-done.4.refs_1_
  24.2 0.0 collective-permute-done.6.refs_3_
  24.2 0.0 copy-done.2
  24.3 0.8 %field.1 = (f32[16,128]{1,0:T(8,128)S(1)}, bf16[512,2048]{1,0:T(8,128)(2,1)S(1)}) custom-call(f32[144,128]{1,0:T(8,128)S(1)} %merge.7.message, bf16[512,512]{1,0:T(8,128)(2,1)S(1)} %copy-done.2, bf16[512,512]{1,0:T(8,128)(2,1)S(1)} %collective-permute-done.4.refs_1_, bf16[512,512]{1,0:T(8,128)(2,1)S(1)} %tie.3.refs_2_, ...), custom_call_target="tpu_custom_call" | custom-call | flops 1000000 | bytes 5000000 | tf_op jit(solution)/shard_map/field/pallas_call | solution.py:497
  25.1 0.0 copy-start.7
  25.1 0.0 copy-start.8
  25.1 0.0 copy-start.11
  25.1 0.0 copy-start.12
  25.1 0.0 copy-start.13
  25.1 1.6 %collective-permute-start.8 = (f32[16,128]{1,0:T(8,128)S(1)}, f32[16,128]{1,0:T(8,128)S(1)}, u32[]{:S(2)}, u32[]{:S(2)}) collective-permute-start(f32[16,128]{1,0:T(8,128)S(1)} %get-tuple-element.30.first), channel_id=1, source_target_pairs={{0,4},{4,0},{8,12},{12,8},{1,5},{5,1},{9,13},{13,9},{2,6},{6,2},{1... | collective-permute-start | bytes 24584 | tf_op jit(solution)/shard_map/ppermute | solution.py:545
  26.8 0.0 copy-done.5
  26.8 0.4 %collective-permute-start.10 = (bf16[512,128]{1,0:T(8,128)(2,1)S(1)}, bf16[512,128]{1,0:T(8,128)(2,1)S(1)}, u32[]{:S(2)}, u32[]{:S(2)}) collective-permute-start(bf16[512,128]{1,0:T(8,128)(2,1)S(1)} %copy-done.5), channel_id=1, source_target_pairs={{0,4},{4,0},{8,12},{12,8},{1,5},{5,1},{9,13},{13,9},{2,6},{6,2},{1... | collective-permute-start | bytes 393224 | tf_op jit(solution)/shard_map/ppermute | solution.py:545
  27.2 1.6 %collective-permute-done.8.second = f32[16,128]{1,0:T(8,128)S(1)} collective-permute-done((f32[16,128]{1,0:T(8,128)S(1)}, f32[16,128]{1,0:T(8,128)S(1)}, u32[]{:S(2)}, u32[]{:S(2)}) %collective-permute-start.8) | collective-permute-done | bytes 8224 | tf_op jit(solution)/shard_map/ppermute | solution.py:545
  28.9 0.0 collective-permute-done.7.first
  28.9 1.6 %collective-permute-start.9 = (bf16[512,128]{1,0:T(8,128)(2,1)S(1)}, bf16[512,128]{1,0:T(8,128)(2,1)S(1)}, u32[]{:S(2)}, u32[]{:S(2)}) collective-permute-start(bf16[512,128]{1,0:T(8,128)(2,1)S(1)} %tie.5.refs_2_), channel_id=1, source_target_pairs={{0,4},{4,0},{8,12},{12,8},{1,5},{5,1},{9,13},{13,9},{2,6},{6,2},{1... | collective-permute-start | bytes 393224 | tf_op jit(solution)/shard_map/ppermute | solution.py:545
  30.5 0.7 %collective-permute-start.11 = (f32[32,128]{1,0:T(8,128)S(1)}, f32[32,128]{1,0:T(8,128)S(1)}, u32[]{:S(2)}, u32[]{:S(2)}) collective-permute-start(f32[32,128]{1,0:T(8,128)S(1)} %merge.8.second.first), channel_id=1, source_target_pairs={{0,8},{4,12},{8,0},{12,4},{1,9},{5,13},{9,1},{13,5},{2,10},{6,14},... | collective-permute-start | bytes 49160 | tf_op jit(solution)/shard_map/ppermute | solution.py:545
  31.2 2.2 %collective-permute-done.10.refs_1_ = bf16[512,128]{1,0:T(8,128)(2,1)S(1)} collective-permute-done((bf16[512,128]{1,0:T(8,128)(2,1)S(1)}, bf16[512,128]{1,0:T(8,128)(2,1)S(1)}, u32[]{:S(2)}, u32[]{:S(2)}) %collective-permute-start.10) | collective-permute-done | bytes 131104 | tf_op jit(solution)/shard_map/ppermute | solution.py:545
  33.4 1.8 %product.2.refs_1_ = f32[512,512]{1,0:T(8,128)S(1)} custom-call(f32[144,128]{1,0:T(8,128)S(1)} %merge.7.message, bf16[512,2048]{1,0:T(8,128)(2,1)S(1)} %get-tuple-element.28.dens, bf16[512,128]{1,0:T(8,128)(2,1)S(1)} %copy-done.5, bf16[512,128]{1,0:T(8,128)(2,1)S(1)} %collective-permute-done.10.refs_1_, bf16[512,128]{1,0:T(8,128)(2,1)S(1)} %tie.5.refs_2_), custom_call_target="tpu_custom_call" | custom-call | flops 1000000 | bytes 10000000 | tf_op jit(solution)/shard_map/product/pallas_call | solution.py:497
  35.2 0.0 collective-permute-done.11.second
  35.2 0.0 copy-done.7
  35.2 0.0 copy-done.8
  35.3 0.0 copy-done.11
  35.3 0.0 copy-done.12
  35.3 0.0 copy-done.13
  35.3 1.2 %advance.1 = (f32[3,1024]{1,0:T(4,128)}, f32[3,1024]{1,0:T(4,128)}, f32[3,1024]{1,0:T(4,128)}, f32[4,1024]{1,0:T(4,128)}) custom-call(f32[64,128]{1,0:T(8,128)S(1)} %merge.9.fields, s32[3,1024]{1,0:T(4,128)S(1)} %copy-done.7, f32[16,1024]{1,0:T(8,128)S(1)} %copy-done.1, f32[4,1024]{1,0:T(4,128)S(1)} %copy-done.13, f32[9,1024]{1,0:T(8,128)S(1)} %pair_forces.1.refs_4_.pair, ...), custom_call_target="tpu_custom_call" | custom-call | flops 1000000 | bytes 6000000 | tf_op jit(solution)/shard_map/advance/pallas_call | solution.py:497
  36.5 0.0 collective-permute-done.9.refs_0_
  36.5 1.9 %product.3 = bf16[512,512]{1,0:T(8,128)(2,1)} custom-call(f32[144,128]{1,0:T(8,128)S(1)} %merge.7.message, bf16[512,2048]{1,0:T(8,128)(2,1)S(1)} %get-tuple-element.28.dens, bf16[512,128]{1,0:T(8,128)(2,1)S(1)} %collective-permute-done.9.refs_0_, f32[512,512]{1,0:T(8,128)S(1)} %product.2.refs_1_), custom_call_target="tpu_custom_call" | custom-call | flops 1000000 | bytes 10000000 | tf_op jit(solution)/shard_map/product/pallas_call | solution.py:497
  (9 shorter events, 0.0 us)
Async XLA Ops:
  0.6 20.9 %copy-start.4 = (s32[32,1024]{1,0:T(8,128)S(1)}, s32[32,1024]{1,0:T(8,128)}, u32[]{:S(2)}) copy-start(s32[32,1024]{1,0:T(8,128)} %neighbours.3) | copy-start | bytes 393220
  0.6 15.1 %collective-permute-start.5 = (bf16[512,512]{1,0:T(8,128)(2,1)}, bf16[512,512]{1,0:T(8,128)(2,1)S(1)}, u32[]{:S(2)}, u32[]{:S(2)}) collective-permute-start(bf16[512,512]{1,0:T(8,128)(2,1)} %refs_0_.3), channel_id=1, source_target_pairs={{0,2},{1,3},{2,0},{3,1},{4,6},{5,7},{6,4},{7,5},{8,10},{9,11},{10,... | collective-permute-start | bytes 1572872 | tf_op jit(solution)/shard_map/ppermute | solution.py:545
  5.8 4.2 %collective-permute-start = (f32[72,128]{1,0:T(8,128)}, f32[72,128]{1,0:T(8,128)S(1)}, u32[]{:S(2)}, u32[]{:S(2)}) collective-permute-start(f32[72,128]{1,0:T(8,128)} %get-tuple-element.22.message), channel_id=1, source_target_pairs={{0,4},{4,0},{8,12},{12,8},{1,5},{5,1},{9,13},{13,9},{2,6},{6,2},{1... | collective-permute-start | bytes 110600 | tf_op jit(solution)/shard_map/ppermute | solution.py:545
  7.5 0.8 %copy-start = (f32[16,1024]{1,0:T(8,128)S(1)}, f32[16,1024]{1,0:T(8,128)}, u32[]{:S(2)}) copy-start(f32[16,1024]{1,0:T(8,128)} %get-tuple-element.21.sites) | copy-start | bytes 196612
  8.3 0.8 %copy-start.9 = (f32[72,128]{1,0:T(8,128)S(1)}, f32[72,128]{1,0:T(8,128)}, u32[]{:S(2)}) copy-start(f32[72,128]{1,0:T(8,128)} %get-tuple-element.22.message) | copy-start | bytes 110596
  9.1 0.7 %copy-start.10 = (bf16[3,512]{1,0:T(4,128)(2,1)S(1)}, bf16[3,512]{1,0:T(4,128)(2,1)}, u32[]{:S(2)}) copy-start(bf16[3,512]{1,0:T(4,128)(2,1)} %dip.1) | copy-start | bytes 9220
  9.8 6.3 %copy-start.6 = (bf16[512,128]{1,0:T(8,128)(2,1)S(1)}, bf16[512,128]{1,0:T(8,128)(2,1)}, u32[]{:S(2)}) copy-start(bf16[512,128]{1,0:T(8,128)(2,1)} %get-tuple-element.29.first) | copy-start | bytes 393220
  9.8 11.7 %copy-start.1 = (f32[16,1024]{1,0:T(8,128)S(1)}, f32[16,1024]{1,0:T(8,128)}, u32[]{:S(2)}) copy-start(f32[16,1024]{1,0:T(8,128)} %get-tuple-element.21.sites) | copy-start | bytes 196612
  10.1 5.4 %collective-permute-start.1 = (f32[128,128]{1,0:T(8,128)S(1)}, f32[128,128]{1,0:T(8,128)S(1)}, u32[]{:S(2)}, u32[]{:S(2)}) collective-permute-start(f32[128,128]{1,0:T(8,128)S(1)} %merge.5.first.second), channel_id=1, source_target_pairs={{0,8},{4,12},{8,0},{12,4},{1,9},{5,13},{9,1},{13,5},{2,10},{6,14},... | collective-permute-start | bytes 196616 | tf_op jit(solution)/shard_map/ppermute | solution.py:545
  12.7 11.6 %collective-permute-start.4 = (bf16[512,512]{1,0:T(8,128)(2,1)}, bf16[512,512]{1,0:T(8,128)(2,1)S(1)}, u32[]{:S(2)}, u32[]{:S(2)}) collective-permute-start(bf16[512,512]{1,0:T(8,128)(2,1)} %refs_0_.3), channel_id=1, source_target_pairs={{0,1},{1,0},{2,3},{3,2},{4,5},{5,4},{6,7},{7,6},{8,9},{9,8},{10,11... | collective-permute-start | bytes 1572872 | tf_op jit(solution)/shard_map/ppermute | solution.py:545
  12.7 0.9 %copy-start.3 = (s32[32,1024]{1,0:T(8,128)S(1)}, s32[32,1024]{1,0:T(8,128)}, u32[]{:S(2)}) copy-start(s32[32,1024]{1,0:T(8,128)} %neighbours.3) | copy-start | bytes 393220
  15.5 8.8 %copy-start.2 = (bf16[512,512]{1,0:T(8,128)(2,1)S(1)}, bf16[512,512]{1,0:T(8,128)(2,1)}, u32[]{:S(2)}) copy-start(bf16[512,512]{1,0:T(8,128)(2,1)} %refs_0_.3) | copy-start | bytes 1572868
  15.8 11.0 %copy-start.5 = (bf16[512,128]{1,0:T(8,128)(2,1)S(1)}, bf16[512,128]{1,0:T(8,128)(2,1)}, u32[]{:S(2)}) copy-start(bf16[512,128]{1,0:T(8,128)(2,1)} %get-tuple-element.31.refs_0_) | copy-start | bytes 393220
  15.8 8.4 %collective-permute-start.6 = (bf16[512,512]{1,0:T(8,128)(2,1)S(1)}, bf16[512,512]{1,0:T(8,128)(2,1)S(1)}, u32[]{:S(2)}, u32[]{:S(2)}) collective-permute-start(bf16[512,512]{1,0:T(8,128)(2,1)S(1)} %tie.3.refs_2_), channel_id=1, source_target_pairs={{0,1},{1,0},{2,3},{3,2},{4,5},{5,4},{6,7},{7,6},{8,9},{9,8},{10,11... | collective-permute-start | bytes 1572872 | tf_op jit(solution)/shard_map/ppermute | solution.py:545
  16.1 12.8 %collective-permute-start.7 = (bf16[512,128]{1,0:T(8,128)(2,1)S(1)}, bf16[512,128]{1,0:T(8,128)(2,1)S(1)}, u32[]{:S(2)}, u32[]{:S(2)}) collective-permute-start(bf16[512,128]{1,0:T(8,128)(2,1)S(1)} %tie.4), channel_id=1, source_target_pairs={{0,8},{4,12},{8,0},{12,4},{1,9},{5,13},{9,1},{13,5},{2,10},{6,14},... | collective-permute-start | bytes 393224 | tf_op jit(solution)/shard_map/ppermute | solution.py:545
  18.7 1.2 %collective-permute-start.2 = (f32[96,128]{1,0:T(8,128)S(1)}, f32[96,128]{1,0:T(8,128)S(1)}, u32[]{:S(2)}, u32[]{:S(2)}) collective-permute-start(f32[96,128]{1,0:T(8,128)S(1)} %get-tuple-element.26.first.second), channel_id=1, source_target_pairs={{0,1},{1,0},{2,3},{3,2},{4,5},{5,4},{6,7},{7,6},{8,9},{9,8},{10,11... | collective-permute-start | bytes 147464 | tf_op jit(solution)/shard_map/ppermute | solution.py:545
  19.9 4.2 %collective-permute-start.3 = (f32[112,128]{1,0:T(8,128)S(1)}, f32[112,128]{1,0:T(8,128)S(1)}, u32[]{:S(2)}, u32[]{:S(2)}) collective-permute-start(f32[112,128]{1,0:T(8,128)S(1)} %merge.6.first), channel_id=1, source_target_pairs={{0,2},{1,3},{2,0},{3,1},{4,6},{5,7},{6,4},{7,5},{8,10},{9,11},{10,... | collective-permute-start | bytes 172040 | tf_op jit(solution)/shard_map/ppermute | solution.py:545
  25.1 10.2 %copy-start.7 = (s32[3,1024]{1,0:T(4,128)S(1)}, s32[3,1024]{1,0:T(4,128)}, u32[]{:S(2)}) copy-start(s32[3,1024]{1,0:T(4,128)} %owner.1) | copy-start | bytes 36868
  25.1 10.2 %copy-start.8 = (f32[3,1024]{1,0:T(4,128)S(1)}, f32[3,1024]{1,0:T(4,128)}, u32[]{:S(2)}) copy-start(f32[3,1024]{1,0:T(4,128)} %centres.1) | copy-start | bytes 36868
  25.1 10.1 %copy-start.11 = (f32[3,1024]{1,0:T(4,128)S(1)}, f32[3,1024]{1,0:T(4,128)}, u32[]{:S(2)}) copy-start(f32[3,1024]{1,0:T(4,128)} %velocity.1) | copy-start | bytes 36868
  25.1 10.1 %copy-start.12 = (f32[3,1024]{1,0:T(4,128)S(1)}, f32[3,1024]{1,0:T(4,128)}, u32[]{:S(2)}) copy-start(f32[3,1024]{1,0:T(4,128)} %angmom.1) | copy-start | bytes 36868
  25.1 10.1 %copy-start.13 = (f32[4,1024]{1,0:T(4,128)S(1)}, f32[4,1024]{1,0:T(4,128)}, u32[]{:S(2)}) copy-start(f32[4,1024]{1,0:T(4,128)} %get-tuple-element.32.quat) | copy-start | bytes 49156
  25.1 3.7 %collective-permute-start.8 = (f32[16,128]{1,0:T(8,128)S(1)}, f32[16,128]{1,0:T(8,128)S(1)}, u32[]{:S(2)}, u32[]{:S(2)}) collective-permute-start(f32[16,128]{1,0:T(8,128)S(1)} %get-tuple-element.30.first), channel_id=1, source_target_pairs={{0,4},{4,0},{8,12},{12,8},{1,5},{5,1},{9,13},{13,9},{2,6},{6,2},{1... | collective-permute-start | bytes 24584 | tf_op jit(solution)/shard_map/ppermute | solution.py:545
  26.8 6.6 %collective-permute-start.10 = (bf16[512,128]{1,0:T(8,128)(2,1)S(1)}, bf16[512,128]{1,0:T(8,128)(2,1)S(1)}, u32[]{:S(2)}, u32[]{:S(2)}) collective-permute-start(bf16[512,128]{1,0:T(8,128)(2,1)S(1)} %copy-done.5), channel_id=1, source_target_pairs={{0,4},{4,0},{8,12},{12,8},{1,5},{5,1},{9,13},{13,9},{2,6},{6,2},{1... | collective-permute-start | bytes 393224 | tf_op jit(solution)/shard_map/ppermute | solution.py:545
  28.9 7.7 %collective-permute-start.9 = (bf16[512,128]{1,0:T(8,128)(2,1)S(1)}, bf16[512,128]{1,0:T(8,128)(2,1)S(1)}, u32[]{:S(2)}, u32[]{:S(2)}) collective-permute-start(bf16[512,128]{1,0:T(8,128)(2,1)S(1)} %tie.5.refs_2_), channel_id=1, source_target_pairs={{0,4},{4,0},{8,12},{12,8},{1,5},{5,1},{9,13},{13,9},{2,6},{6,2},{1... | collective-permute-start | bytes 393224 | tf_op jit(solution)/shard_map/ppermute | solution.py:545
  30.5 4.7 %collective-permute-start.11 = (f32[32,128]{1,0:T(8,128)S(1)}, f32[32,128]{1,0:T(8,128)S(1)}, u32[]{:S(2)}, u32[]{:S(2)}) collective-permute-start(f32[32,128]{1,0:T(8,128)S(1)} %merge.8.second.first), channel_id=1, source_target_pairs={{0,8},{4,12},{8,0},{12,4},{1,9},{5,13},{9,1},{13,5},{2,10},{6,14},... | collective-permute-start | bytes 49160 | tf_op jit(solution)/shard_map/ppermute | solution.py:545

commit v3 on v2

--- a/solution.py
+++ b/solution.py
@@ -370,7 +370,7 @@
     for step in range(rows_n):
         for row in range(rows_b):
             start = step * depth + line_of(row, 0)
-            place = 8 * (step * rows_b + row)
+            place = 4 * (step * rows_b + row)
             table[place : place + 3, :] = fields[start : start + 3, :]
     for tile in range(waters // LANES):
         for source in range(3):
@@ -378,13 +378,15 @@
             low, high = index & 127, index >> 7
             found = jnp.zeros((8, LANES), F32)
             for step in range(rows_n):
-                base = (here_row ^ step) * rows_b
-                for row in range(rows_b):
-                    place = 8 * (step * rows_b + row)
+                base = (here_row ^ step) * (rows_b // 2)
+                for two in range(rows_b // 2):
+                    place = 8 * (step * (rows_b // 2) + two)
                     value = pick(table[place : place + 8, :], low)
-                    found = jnp.where(high == base + row, value, found)
+                    found = jnp.where((high >> 1) == base + two, value, found)
+            odd = (high[0:3] & 1) == 1
+            found = jnp.where(odd, found[4:7], found[0:3])
             lines = slice(3 * source, 3 * source + 3)
-            force[lines, at(tile)] = pair[lines, at(tile)] + CHARGE[source] * found[0:3]
+            force[lines, at(tile)] = pair[lines, at(tile)] + CHARGE[source] * found
 
     def cross(left, right):
         return [
@@ -657,7 +659,7 @@
         field = merge(field, swap(field, "row", rows_n, step), 0)
         if step == 1:
             small_all = relay(small_all, "row", rows_n, field)
-    early = [0] + list(steps)
+    early = [0] + steps[1:]
     late = [step for step in range(rows_n) if step not in early]
     partial, kinds = [], [(early, F32 if late else BF16)] + ([(late, BF16)] if late else [])
     for these, kind in kinds:
@@ -675,7 +677,7 @@
         "advance",
         [((3, waters), F32), ((3, waters), F32), ((3, waters), F32), ((4, waters), F32)],
         [field, owner, sites, quat, pair, centres, velocity, angmom],
-        scratch=[pltpu.VMEM((16, waters), F32), pltpu.VMEM((8 * hist_rows, LANES), F32)],
+        scratch=[pltpu.VMEM((16, waters), F32), pltpu.VMEM((4 * hist_rows, LANES), F32)],
         cost=(10**6, 6 * 10**6),
     )
     return (qm_out, centres_new, velocity_new, angmom_new, orient_new)

time: 38.7 us -> 38.9 us (level)
  transfers between devices with their start and end apart: 12 -> 12, of which waited for: 5 -> 5; matrix products, arithmetic and copies ran while one was open for 0% -> 0% of each run, Pallas kernels for 28% -> 26%
where the time goes in v3:
time: 38.9 us; the launch traced here: 38.6 us
  starting transfers between devices  16.3 us (42%)
  Pallas kernels  12.5 us (32%)
  waiting for transfers between devices  5.69 us (15%)
  local copies, waits for them, and re-layouts  3.26 us (8%)
  between operations  0.83 us (2%)
    ppermute x12, starting transfers between devices, swap(): return lax.ppermute(value, axis, [(i, i ^ step) for i in range(count)])  16.3 us
    pallas_call x17, Pallas kernels, call(): pl.pallas_call(kernel, out_shape=[jax.ShapeDtypeStruct(shape, dtype) for...  12.5 us
    ppermute x12, waiting for transfers between devices, swap(): return lax.ppermute(value, axis, [(i, i ^ step) for i in range(count)])  5.69 us
    unnamed x28, local copies, waits for them, and re-layouts  3.26 us
  transfers between devices with their start and end apart: 12, of which 5 were waited for; matrix products, arithmetic and copies ran while one was open for 0% of the time, Pallas kernels for 26%

profile of v3, /device:TPU:0, one launch (start us, length us, event | category | flops | bytes accessed | tf_op | source)
XLA Modules:
  0.0 38.6 jit_solution(1164735648481131480)
XLA Ops:
  0.6 0.0 copy-start.4
  0.6 3.0 %collective-permute-start.5 = (bf16[512,512]{1,0:T(8,128)(2,1)}, bf16[512,512]{1,0:T(8,128)(2,1)S(1)}, u32[]{:S(2)}, u32[]{:S(2)}) collective-permute-start(bf16[512,512]{1,0:T(8,128)(2,1)} %refs_0_.3), channel_id=1, source_target_pairs={{0,2},{1,3},{2,0},{3,1},{4,6},{5,7},{6,4},{7,5},{8,10},{9,11},{10,... | collective-permute-start | bytes 1572872 | tf_op jit(solution)/shard_map/ppermute | solution.py:547
  3.6 2.2 %open.1 = (f32[72,128]{1,0:T(8,128)}, bf16[512,128]{1,0:T(8,128)(2,1)}, bf16[512,128]{1,0:T(8,128)(2,1)}, f32[16,1024]{1,0:T(8,128)}, f32[4,1024]{1,0:T(4,128)}) custom-call(s32[4,4]{1,0:T(4,128)} %refs_0_.2, s32[4,4]{1,0:T(4,128)} %refs_1_.1, bf16[512,512]{1,0:T(8,128)(2,1)} %refs_2_.1, bf16[3,512]{1,0:T(4,128)(2,1)} %dip.1, s32[3,1024]{1,0:T(4,128)} %owner.1, ...), custom_call_target="tpu_custom_call" | custom-call | flops 1000000 | bytes 12000000 | tf_op jit(solution)/shard_map/open/pallas_call | solution.py:499
  5.8 1.6 %collective-permute-start = (f32[72,128]{1,0:T(8,128)}, f32[72,128]{1,0:T(8,128)S(1)}, u32[]{:S(2)}, u32[]{:S(2)}) collective-permute-start(f32[72,128]{1,0:T(8,128)} %get-tuple-element.22.message), channel_id=1, source_target_pairs={{0,4},{4,0},{8,12},{12,8},{1,5},{5,1},{9,13},{13,9},{2,6},{6,2},{1... | collective-permute-start | bytes 110600 | tf_op jit(solution)/shard_map/ppermute | solution.py:547
  7.5 0.0 copy-start
  7.5 0.8 %copy-done = f32[16,1024]{1,0:T(8,128)S(1)} copy-done((f32[16,1024]{1,0:T(8,128)S(1)}, f32[16,1024]{1,0:T(8,128)}, u32[]{:S(2)}) %copy-start) | copy-done | bytes 65560
  8.3 0.0 copy-start.9
  8.3 0.8 %copy-done.9 = f32[72,128]{1,0:T(8,128)S(1)} copy-done((f32[72,128]{1,0:T(8,128)S(1)}, f32[72,128]{1,0:T(8,128)}, u32[]{:S(2)}) %copy-start.9) | copy-done | bytes 36888
  9.1 0.0 copy-start.10
  9.1 0.7 %copy-done.10 = bf16[3,512]{1,0:T(4,128)(2,1)S(1)} copy-done((bf16[3,512]{1,0:T(4,128)(2,1)S(1)}, bf16[3,512]{1,0:T(4,128)(2,1)}, u32[]{:S(2)}) %copy-start.10) | copy-done | bytes 3096
  9.8 0.0 copy-start.5
  9.8 0.0 copy-start.1
  9.8 0.1 prepare.1
  9.8 0.2 collective-permute-done.second
  10.1 2.6 %collective-permute-start.1 = (f32[128,128]{1,0:T(8,128)S(1)}, f32[128,128]{1,0:T(8,128)S(1)}, u32[]{:S(2)}, u32[]{:S(2)}) collective-permute-start(f32[128,128]{1,0:T(8,128)S(1)} %merge.5.first.second), channel_id=1, source_target_pairs={{0,8},{4,12},{8,0},{12,4},{1,9},{5,13},{9,1},{13,5},{2,10},{6,14},... | collective-permute-start | bytes 196616 | tf_op jit(solution)/shard_map/ppermute | solution.py:547
  12.7 0.0 collective-permute-start.4
  12.7 0.0 copy-start.3
  12.7 0.9 %copy-done.3 = s32[32,1024]{1,0:T(8,128)S(1)} copy-done((s32[32,1024]{1,0:T(8,128)S(1)}, s32[32,1024]{1,0:T(8,128)}, u32[]{:S(2)}) %copy-start.3) | copy-done | bytes 131096
  13.6 1.9 %own_gathers.1.done.own_words = s32[160,1024]{1,0:T(8,128)S(1)} custom-call(s32[5,8,8,128]{3,2,1,0:T(8,128)S(1)} %get-tuple-element.25.table.own_table, s32[32,1024]{1,0:T(8,128)S(1)} %copy-done.3), custom_call_target="tpu_custom_call" | custom-call | flops 1000000 | bytes 6000000 | tf_op jit(solution)/shard_map/own_gathers/pallas_call | solution.py:499
  15.5 0.0 copy-start.2
  15.5 0.0 collective-permute-done.1.second
  15.5 0.3 collective-permute-done.5.first
  15.8 0.0 copy-start.6
  15.8 0.3 collective-permute-start.6
  16.1 0.0 copy-done.5
  16.1 2.6 %collective-permute-start.8 = (bf16[512,128]{1,0:T(8,128)(2,1)S(1)}, bf16[512,128]{1,0:T(8,128)(2,1)S(1)}, u32[]{:S(2)}, u32[]{:S(2)}) collective-permute-start(bf16[512,128]{1,0:T(8,128)(2,1)S(1)} %tie.4), channel_id=1, source_target_pairs={{0,8},{4,12},{8,0},{12,4},{1,9},{5,13},{9,1},{13,5},{2,10},{6,14},... | collective-permute-start | bytes 393224 | tf_op jit(solution)/shard_map/ppermute | solution.py:547
  18.7 0.2 collective-permute-start.2
  18.9 1.1 %collective-permute-done.2.second = f32[96,128]{1,0:T(8,128)S(1)} collective-permute-done((f32[96,128]{1,0:T(8,128)S(1)}, f32[96,128]{1,0:T(8,128)S(1)}, u32[]{:S(2)}, u32[]{:S(2)}) %collective-permute-start.2) | collective-permute-done | bytes 49184 | tf_op jit(solution)/shard_map/ppermute | solution.py:547
  19.9 1.6 %collective-permute-start.3 = (f32[112,128]{1,0:T(8,128)S(1)}, f32[112,128]{1,0:T(8,128)S(1)}, u32[]{:S(2)}, u32[]{:S(2)}) collective-permute-start(f32[112,128]{1,0:T(8,128)S(1)} %merge.6.first), channel_id=1, source_target_pairs={{0,2},{1,3},{2,0},{3,1},{4,6},{5,7},{6,4},{7,5},{8,10},{9,11},{10,... | collective-permute-start | bytes 172040 | tf_op jit(solution)/shard_map/ppermute | solution.py:547
  21.5 0.0 copy-done.4
  21.5 0.0 copy-done.1
  21.5 2.7 %pair_forces.1.refs_4_.pair = f32[9,1024]{1,0:T(8,128)S(1)} custom-call(f32[16,1024]{1,0:T(8,128)S(1)} %copy-done.1, s32[160,1024]{1,0:T(8,128)S(1)} %own_gathers.1.done.own_words, s32[5,8,8,128]{3,2,1,0:T(8,128)S(1)} %get-tuple-element.25.table.own_table, f32[160,128]{1,0:T(8,128)S(1)} %get-tuple-element.27.halos, s32[32,1024]{1,0:T(8,128)S(1)} %copy-done.4), custom_call_target="tpu_custom_call" | custom-call | flops 1000000 | bytes 15000000 | tf_op jit(solution)/shard_map/pair_forces/pallas_call | solution.py:499
  24.2 0.0 collective-permute-done.3.second
  24.2 0.0 collective-permute-done.4.refs_1_
  24.2 0.0 collective-permute-done.6.refs_3_
  24.2 0.0 copy-done.2
  24.3 0.8 %field.1 = (f32[16,128]{1,0:T(8,128)S(1)}, bf16[512,2048]{1,0:T(8,128)(2,1)S(1)}) custom-call(f32[144,128]{1,0:T(8,128)S(1)} %merge.7.message, bf16[512,512]{1,0:T(8,128)(2,1)S(1)} %copy-done.2, bf16[512,512]{1,0:T(8,128)(2,1)S(1)} %collective-permute-done.4.refs_1_, bf16[512,512]{1,0:T(8,128)(2,1)S(1)} %tie.3.refs_2_, ...), custom_call_target="tpu_custom_call" | custom-call | flops 1000000 | bytes 5000000 | tf_op jit(solution)/shard_map/field/pallas_call | solution.py:499
  25.1 0.0 copy-start.7
  25.1 0.0 copy-start.8
  25.1 0.0 copy-start.11
  25.1 0.0 copy-start.12
  25.1 0.0 copy-start.13
  25.1 1.6 %collective-permute-start.9 = (f32[16,128]{1,0:T(8,128)S(1)}, f32[16,128]{1,0:T(8,128)S(1)}, u32[]{:S(2)}, u32[]{:S(2)}) collective-permute-start(f32[16,128]{1,0:T(8,128)S(1)} %get-tuple-element.31.first), channel_id=1, source_target_pairs={{0,4},{4,0},{8,12},{12,8},{1,5},{5,1},{9,13},{13,9},{2,6},{6,2},{1... | collective-permute-start | bytes 24584 | tf_op jit(solution)/shard_map/ppermute | solution.py:547
  26.8 0.0 copy-done.6
  26.8 0.4 %collective-permute-start.7 = (bf16[512,128]{1,0:T(8,128)(2,1)S(1)}, bf16[512,128]{1,0:T(8,128)(2,1)S(1)}, u32[]{:S(2)}, u32[]{:S(2)}) collective-permute-start(bf16[512,128]{1,0:T(8,128)(2,1)S(1)} %copy-done.6), channel_id=1, source_target_pairs={{0,4},{4,0},{8,12},{12,8},{1,5},{5,1},{9,13},{13,9},{2,6},{6,2},{1... | collective-permute-start | bytes 393224 | tf_op jit(solution)/shard_map/ppermute | solution.py:547
  27.2 1.6 %collective-permute-done.9.second = f32[16,128]{1,0:T(8,128)S(1)} collective-permute-done((f32[16,128]{1,0:T(8,128)S(1)}, f32[16,128]{1,0:T(8,128)S(1)}, u32[]{:S(2)}, u32[]{:S(2)}) %collective-permute-start.9) | collective-permute-done | bytes 8224 | tf_op jit(solution)/shard_map/ppermute | solution.py:547
  28.9 0.0 collective-permute-done.8.first
  28.9 1.6 %collective-permute-start.10 = (bf16[512,128]{1,0:T(8,128)(2,1)S(1)}, bf16[512,128]{1,0:T(8,128)(2,1)S(1)}, u32[]{:S(2)}, u32[]{:S(2)}) collective-permute-start(bf16[512,128]{1,0:T(8,128)(2,1)S(1)} %tie.5.refs_1_), channel_id=1, source_target_pairs={{0,4},{4,0},{8,12},{12,8},{1,5},{5,1},{9,13},{13,9},{2,6},{6,2},{1... | collective-permute-start | bytes 393224 | tf_op jit(solution)/shard_map/ppermute | solution.py:547
  30.5 0.7 %collective-permute-start.11 = (f32[32,128]{1,0:T(8,128)S(1)}, f32[32,128]{1,0:T(8,128)S(1)}, u32[]{:S(2)}, u32[]{:S(2)}) collective-permute-start(f32[32,128]{1,0:T(8,128)S(1)} %merge.8.second.first), channel_id=1, source_target_pairs={{0,8},{4,12},{8,0},{12,4},{1,9},{5,13},{9,1},{13,5},{2,10},{6,14},... | collective-permute-start | bytes 49160 | tf_op jit(solution)/shard_map/ppermute | solution.py:547
  31.2 1.5 %product.2.refs_2_ = f32[512,512]{1,0:T(8,128)S(1)} custom-call(f32[144,128]{1,0:T(8,128)S(1)} %merge.7.message, bf16[512,2048]{1,0:T(8,128)(2,1)S(1)} %get-tuple-element.28.dens, bf16[512,128]{1,0:T(8,128)(2,1)S(1)} %copy-done.6, bf16[512,128]{1,0:T(8,128)(2,1)S(1)} %tie.5.refs_1_), custom_call_target="tpu_custom_call" | custom-call | flops 1000000 | bytes 10000000 | tf_op jit(solution)/shard_map/product/pallas_call | solution.py:499
  32.7 2.5 %collective-permute-done.11.second = f32[32,128]{1,0:T(8,128)S(1)} collective-permute-done((f32[32,128]{1,0:T(8,128)S(1)}, f32[32,128]{1,0:T(8,128)S(1)}, u32[]{:S(2)}, u32[]{:S(2)}) %collective-permute-start.11) | collective-permute-done | bytes 16416 | tf_op jit(solution)/shard_map/ppermute | solution.py:547
  35.2 0.0 copy-done.7
  35.2 0.0 copy-done.8
  35.2 0.0 copy-done.11
  35.2 0.0 copy-done.12
  35.2 0.0 copy-done.13
  35.2 1.1 %advance.1 = (f32[3,1024]{1,0:T(4,128)}, f32[3,1024]{1,0:T(4,128)}, f32[3,1024]{1,0:T(4,128)}, f32[4,1024]{1,0:T(4,128)}) custom-call(f32[64,128]{1,0:T(8,128)S(1)} %merge.9.fields, s32[3,1024]{1,0:T(4,128)S(1)} %copy-done.7, f32[16,1024]{1,0:T(8,128)S(1)} %copy-done.1, f32[4,1024]{1,0:T(4,128)S(1)} %copy-done.13, f32[9,1024]{1,0:T(8,128)S(1)} %pair_forces.1.refs_4_.pair, ...), custom_call_target="tpu_custom_call" | custom-call | flops 1000000 | bytes 6000000 | tf_op jit(solution)/shard_map/advance/pallas_call | solution.py:499
  36.3 0.0 collective-permute-done.7.refs_0_
  36.3 0.0 collective-permute-done.10.refs_1_
  36.3 2.3 %product.3 = bf16[512,512]{1,0:T(8,128)(2,1)} custom-call(f32[144,128]{1,0:T(8,128)S(1)} %merge.7.message, bf16[512,2048]{1,0:T(8,128)(2,1)S(1)} %get-tuple-element.28.dens, bf16[512,128]{1,0:T(8,128)(2,1)S(1)} %collective-permute-done.7.refs_0_, bf16[512,128]{1,0:T(8,128)(2,1)S(1)} %collective-permute-done.10.refs_1_, f32[512,512]{1,0:T(8,128)S(1)} %product.2.refs_2_), custom_call_target="tpu_custom_call" | custom-call | flops 1000000 | bytes 10000000 | tf_op jit(solution)/shard_map/product/pallas_call | solution.py:499
  (9 shorter events, 0.0 us)
Async XLA Ops:
  0.6 20.9 %copy-start.4 = (s32[32,1024]{1,0:T(8,128)S(1)}, s32[32,1024]{1,0:T(8,128)}, u32[]{:S(2)}) copy-start(s32[32,1024]{1,0:T(8,128)} %neighbours.3) | copy-start | bytes 393220
  0.6 15.1 %collective-permute-start.5 = (bf16[512,512]{1,0:T(8,128)(2,1)}, bf16[512,512]{1,0:T(8,128)(2,1)S(1)}, u32[]{:S(2)}, u32[]{:S(2)}) collective-permute-start(bf16[512,512]{1,0:T(8,128)(2,1)} %refs_0_.3), channel_id=1, source_target_pairs={{0,2},{1,3},{2,0},{3,1},{4,6},{5,7},{6,4},{7,5},{8,10},{9,11},{10,... | collective-permute-start | bytes 1572872 | tf_op jit(solution)/shard_map/ppermute | solution.py:547
  5.8 4.2 %collective-permute-start = (f32[72,128]{1,0:T(8,128)}, f32[72,128]{1,0:T(8,128)S(1)}, u32[]{:S(2)}, u32[]{:S(2)}) collective-permute-start(f32[72,128]{1,0:T(8,128)} %get-tuple-element.22.message), channel_id=1, source_target_pairs={{0,4},{4,0},{8,12},{12,8},{1,5},{5,1},{9,13},{13,9},{2,6},{6,2},{1... | collective-permute-start | bytes 110600 | tf_op jit(solution)/shard_map/ppermute | solution.py:547
  7.5 0.8 %copy-start = (f32[16,1024]{1,0:T(8,128)S(1)}, f32[16,1024]{1,0:T(8,128)}, u32[]{:S(2)}) copy-start(f32[16,1024]{1,0:T(8,128)} %get-tuple-element.21.sites) | copy-start | bytes 196612
  8.3 0.8 %copy-start.9 = (f32[72,128]{1,0:T(8,128)S(1)}, f32[72,128]{1,0:T(8,128)}, u32[]{:S(2)}) copy-start(f32[72,128]{1,0:T(8,128)} %get-tuple-element.22.message) | copy-start | bytes 110596
  9.1 0.7 %copy-start.10 = (bf16[3,512]{1,0:T(4,128)(2,1)S(1)}, bf16[3,512]{1,0:T(4,128)(2,1)}, u32[]{:S(2)}) copy-start(bf16[3,512]{1,0:T(4,128)(2,1)} %dip.1) | copy-start | bytes 9220
  9.8 6.3 %copy-start.5 = (bf16[512,128]{1,0:T(8,128)(2,1)S(1)}, bf16[512,128]{1,0:T(8,128)(2,1)}, u32[]{:S(2)}) copy-start(bf16[512,128]{1,0:T(8,128)(2,1)} %get-tuple-element.30.first) | copy-start | bytes 393220
  9.8 11.7 %copy-start.1 = (f32[16,1024]{1,0:T(8,128)S(1)}, f32[16,1024]{1,0:T(8,128)}, u32[]{:S(2)}) copy-start(f32[16,1024]{1,0:T(8,128)} %get-tuple-element.21.sites) | copy-start | bytes 196612
  10.1 5.4 %collective-permute-start.1 = (f32[128,128]{1,0:T(8,128)S(1)}, f32[128,128]{1,0:T(8,128)S(1)}, u32[]{:S(2)}, u32[]{:S(2)}) collective-permute-start(f32[128,128]{1,0:T(8,128)S(1)} %merge.5.first.second), channel_id=1, source_target_pairs={{0,8},{4,12},{8,0},{12,4},{1,9},{5,13},{9,1},{13,5},{2,10},{6,14},... | collective-permute-start | bytes 196616 | tf_op jit(solution)/shard_map/ppermute | solution.py:547
  12.7 11.6 %collective-permute-start.4 = (bf16[512,512]{1,0:T(8,128)(2,1)}, bf16[512,512]{1,0:T(8,128)(2,1)S(1)}, u32[]{:S(2)}, u32[]{:S(2)}) collective-permute-start(bf16[512,512]{1,0:T(8,128)(2,1)} %refs_0_.3), channel_id=1, source_target_pairs={{0,1},{1,0},{2,3},{3,2},{4,5},{5,4},{6,7},{7,6},{8,9},{9,8},{10,11... | collective-permute-start | bytes 1572872 | tf_op jit(solution)/shard_map/ppermute | solution.py:547
  12.7 0.9 %copy-start.3 = (s32[32,1024]{1,0:T(8,128)S(1)}, s32[32,1024]{1,0:T(8,128)}, u32[]{:S(2)}) copy-start(s32[32,1024]{1,0:T(8,128)} %neighbours.3) | copy-start | bytes 393220
  15.5 8.8 %copy-start.2 = (bf16[512,512]{1,0:T(8,128)(2,1)S(1)}, bf16[512,512]{1,0:T(8,128)(2,1)}, u32[]{:S(2)}) copy-start(bf16[512,512]{1,0:T(8,128)(2,1)} %refs_0_.3) | copy-start | bytes 1572868
  15.8 11.0 %copy-start.6 = (bf16[512,128]{1,0:T(8,128)(2,1)S(1)}, bf16[512,128]{1,0:T(8,128)(2,1)}, u32[]{:S(2)}) copy-start(bf16[512,128]{1,0:T(8,128)(2,1)} %get-tuple-element.29.refs_0_) | copy-start | bytes 393220
  15.8 8.4 %collective-permute-start.6 = (bf16[512,512]{1,0:T(8,128)(2,1)S(1)}, bf16[512,512]{1,0:T(8,128)(2,1)S(1)}, u32[]{:S(2)}, u32[]{:S(2)}) collective-permute-start(bf16[512,512]{1,0:T(8,128)(2,1)S(1)} %tie.3.refs_2_), channel_id=1, source_target_pairs={{0,1},{1,0},{2,3},{3,2},{4,5},{5,4},{6,7},{7,6},{8,9},{9,8},{10,11... | collective-permute-start | bytes 1572872 | tf_op jit(solution)/shard_map/ppermute | solution.py:547
  16.1 12.8 %collective-permute-start.8 = (bf16[512,128]{1,0:T(8,128)(2,1)S(1)}, bf16[512,128]{1,0:T(8,128)(2,1)S(1)}, u32[]{:S(2)}, u32[]{:S(2)}) collective-permute-start(bf16[512,128]{1,0:T(8,128)(2,1)S(1)} %tie.4), channel_id=1, source_target_pairs={{0,8},{4,12},{8,0},{12,4},{1,9},{5,13},{9,1},{13,5},{2,10},{6,14},... | collective-permute-start | bytes 393224 | tf_op jit(solution)/shard_map/ppermute | solution.py:547
  18.7 1.2 %collective-permute-start.2 = (f32[96,128]{1,0:T(8,128)S(1)}, f32[96,128]{1,0:T(8,128)S(1)}, u32[]{:S(2)}, u32[]{:S(2)}) collective-permute-start(f32[96,128]{1,0:T(8,128)S(1)} %get-tuple-element.26.first.second), channel_id=1, source_target_pairs={{0,1},{1,0},{2,3},{3,2},{4,5},{5,4},{6,7},{7,6},{8,9},{9,8},{10,11... | collective-permute-start | bytes 147464 | tf_op jit(solution)/shard_map/ppermute | solution.py:547
  19.9 4.2 %collective-permute-start.3 = (f32[112,128]{1,0:T(8,128)S(1)}, f32[112,128]{1,0:T(8,128)S(1)}, u32[]{:S(2)}, u32[]{:S(2)}) collective-permute-start(f32[112,128]{1,0:T(8,128)S(1)} %merge.6.first), channel_id=1, source_target_pairs={{0,2},{1,3},{2,0},{3,1},{4,6},{5,7},{6,4},{7,5},{8,10},{9,11},{10,... | collective-permute-start | bytes 172040 | tf_op jit(solution)/shard_map/ppermute | solution.py:547
  25.1 10.1 %copy-start.7 = (s32[3,1024]{1,0:T(4,128)S(1)}, s32[3,1024]{1,0:T(4,128)}, u32[]{:S(2)}) copy-start(s32[3,1024]{1,0:T(4,128)} %owner.1) | copy-start | bytes 36868
  25.1 10.1 %copy-start.8 = (f32[3,1024]{1,0:T(4,128)S(1)}, f32[3,1024]{1,0:T(4,128)}, u32[]{:S(2)}) copy-start(f32[3,1024]{1,0:T(4,128)} %centres.1) | copy-start | bytes 36868
  25.1 10.1 %copy-start.11 = (f32[3,1024]{1,0:T(4,128)S(1)}, f32[3,1024]{1,0:T(4,128)}, u32[]{:S(2)}) copy-start(f32[3,1024]{1,0:T(4,128)} %velocity.1) | copy-start | bytes 36868
  25.1 10.1 %copy-start.12 = (f32[3,1024]{1,0:T(4,128)S(1)}, f32[3,1024]{1,0:T(4,128)}, u32[]{:S(2)}) copy-start(f32[3,1024]{1,0:T(4,128)} %angmom.1) | copy-start | bytes 36868
  25.1 10.1 %copy-start.13 = (f32[4,1024]{1,0:T(4,128)S(1)}, f32[4,1024]{1,0:T(4,128)}, u32[]{:S(2)}) copy-start(f32[4,1024]{1,0:T(4,128)} %get-tuple-element.32.quat) | copy-start | bytes 49156
  25.1 3.7 %collective-permute-start.9 = (f32[16,128]{1,0:T(8,128)S(1)}, f32[16,128]{1,0:T(8,128)S(1)}, u32[]{:S(2)}, u32[]{:S(2)}) collective-permute-start(f32[16,128]{1,0:T(8,128)S(1)} %get-tuple-element.31.first), channel_id=1, source_target_pairs={{0,4},{4,0},{8,12},{12,8},{1,5},{5,1},{9,13},{13,9},{2,6},{6,2},{1... | collective-permute-start | bytes 24584 | tf_op jit(solution)/shard_map/ppermute | solution.py:547
  26.8 9.5 %collective-permute-start.7 = (bf16[512,128]{1,0:T(8,128)(2,1)S(1)}, bf16[512,128]{1,0:T(8,128)(2,1)S(1)}, u32[]{:S(2)}, u32[]{:S(2)}) collective-permute-start(bf16[512,128]{1,0:T(8,128)(2,1)S(1)} %copy-done.6), channel_id=1, source_target_pairs={{0,4},{4,0},{8,12},{12,8},{1,5},{5,1},{9,13},{13,9},{2,6},{6,2},{1... | collective-permute-start | bytes 393224 | tf_op jit(solution)/shard_map/ppermute | solution.py:547
  28.9 7.4 %collective-permute-start.10 = (bf16[512,128]{1,0:T(8,128)(2,1)S(1)}, bf16[512,128]{1,0:T(8,128)(2,1)S(1)}, u32[]{:S(2)}, u32[]{:S(2)}) collective-permute-start(bf16[512,128]{1,0:T(8,128)(2,1)S(1)} %tie.5.refs_1_), channel_id=1, source_target_pairs={{0,4},{4,0},{8,12},{12,8},{1,5},{5,1},{9,13},{13,9},{2,6},{6,2},{1... | collective-permute-start | bytes 393224 | tf_op jit(solution)/shard_map/ppermute | solution.py:547
  30.5 4.6 %collective-permute-start.11 = (f32[32,128]{1,0:T(8,128)S(1)}, f32[32,128]{1,0:T(8,128)S(1)}, u32[]{:S(2)}, u32[]{:S(2)}) collective-permute-start(f32[32,128]{1,0:T(8,128)S(1)} %merge.8.second.first), channel_id=1, source_target_pairs={{0,8},{4,12},{8,0},{12,4},{1,9},{5,13},{9,1},{13,5},{2,10},{6,14},... | collective-permute-start | bytes 49160 | tf_op jit(solution)/shard_map/ppermute | solution.py:547

commit v4 on v3

--- a/solution.py
+++ b/solution.py
@@ -442,23 +442,24 @@
             for col in range(cols_b):
                 panel[place, row * BLOCK : (row + 1) * BLOCK, at(col)] = block * flag(row * cols_b + col)
 
-    def one_row(row, carry):
-        lines = pl.ds(pl.multiple_of(row * BLOCK, BLOCK), BLOCK)
+    chunk = 2 * BLOCK
+    for part in range(rows // chunk):
+        lines = slice(part * chunk, (part + 1) * chunk)
         value = contract(dens[lines, spans[0]], panel[0], ((1,), (0,)))
         for place in range(1, count):
             value = value + contract(dens[lines, spans[place]], panel[place], ((1,), (0,)))
         if before:
             out[lines, :] = (value + before[0][lines, :]).astype(out.dtype)
-        else:
+            continue
+        for half in range(2):
+            row = 2 * part + half
+            lines = slice(row * BLOCK, (row + 1) * BLOCK)
             own = UNIT * COUPLE * message[pl.ds(here_row * rows_b + row, 1), :]
             across = jnp.transpose(jnp.broadcast_to(own, (BLOCK, BLOCK)))
             for col in range(cols_b):
                 pot = UNIT * COUPLE * message[pl.ds(here_col * cols_b + col, 1), :]
                 sums = (across + pot) * dens[lines, at(col)].astype(F32)
-                out[lines, at(col)] = (value[:, at(col)] + sums).astype(out.dtype)
-        return carry
-
-    lax.fori_loop(0, rows_b, one_row, 0)
+                out[lines, at(col)] = (value[half * BLOCK : (half + 1) * BLOCK, at(col)] + sums).astype(out.dtype)
 
 
 def tie_kernel(first, second, out):
@@ -655,23 +656,24 @@
         scratch=[pltpu.VMEM((8, cols), F32)],
         cost=(10**6, 5 * 10**6),
     )
-    for step in doublings(rows_n):
-        field = merge(field, swap(field, "row", rows_n, step), 0)
-        if step == 1:
-            small_all = relay(small_all, "row", rows_n, field)
-    early = [0] + steps[1:]
-    late = [step for step in range(rows_n) if step not in early]
-    partial, kinds = [], [(early, F32 if late else BF16)] + ([(late, BF16)] if late else [])
-    for these, kind in kinds:
-        partial = call(
+    small_all = relay(small_all, "row", rows_n, field)
+
+    def product(these, kind, before):
+        return call(
             functools.partial(product_kernel, these, hist_rows, block_rows),
             "product",
             [((rows, cols), kind)],
-            [message, masked] + [small_all[step] for step in these] + list(partial),
+            [message, masked] + [small_all[step] for step in these] + before,
             scratch=[pltpu.VMEM((len(these), rows, cols), BF16)],
             cost=(10**6, 10 * 10**6),
         )
-    (qm_out,) = partial
+
+    early = [0] + steps[1:]
+    late = [step for step in range(rows_n) if step not in early]
+    (partial,) = product(early, F32, [])
+    (qm_out,) = product(late, BF16, [partial])
+    for step in steps:
+        field = merge(field, swap(field, "row", rows_n, step), 0, {1: partial, steps[-1]: qm_out}.get(step))
     centres_new, velocity_new, angmom_new, orient_new = call(
         functools.partial(advance_kernel, rows_n, rows_b),
         "advance",

time: 38.9 us -> 39.3 us (1.010)
  Pallas kernels: 12.5 us -> 11.2 us
  local copies, waits for them, and re-layouts: 3.26 us -> 4.29 us
  starting transfers between devices: 16.3 us -> 17.3 us
    pallas_call x17, Pallas kernels: 12.5 us -> 11.2 us  [call(): pl.pallas_call(kernel, out_shape=[jax.ShapeDtypeStruct(shape, dtype) for...]
    ppermute x12, starting transfers between devices: 16.3 us -> 17.3 us  [swap(): return lax.ppermute(value, axis, [(i, i ^ step) for i in range(count)])]
    unnamed x28 -> x30, local copies, waits for them, and re-layouts: 3.26 us -> 4.29 us
where the time goes in v4:
time: 39.3 us; the launch traced here: 39 us
  starting transfers between devices  17.3 us (44%)
  Pallas kernels  11.2 us (28%)
  waiting for transfers between devices  5.38 us (14%)
  local copies, waits for them, and re-layouts  4.29 us (11%)
  between operations  0.82 us (2%)
    ppermute x12, starting transfers between devices, swap(): return lax.ppermute(value, axis, [(i, i ^ step) for i in range(count)])  17.3 us
    pallas_call x17, Pallas kernels, call(): pl.pallas_call(kernel, out_shape=[jax.ShapeDtypeStruct(shape, dtype) for...  11.2 us
    ppermute x12, waiting for transfers between devices, swap(): return lax.ppermute(value, axis, [(i, i ^ step) for i in range(count)])  5.38 us
    unnamed x30, local copies, waits for them, and re-layouts  4.29 us
  transfers between devices with their start and end apart: 12, of which 5 were waited for; matrix products, arithmetic and copies ran while one was open for 0% of the time, Pallas kernels for 26%

profile of v4, /device:TPU:0, one launch (start us, length us, event | category | flops | bytes accessed | tf_op | source)
XLA Modules:
  0.0 39.0 jit_solution(13126204138834657353)
XLA Ops:
  0.6 0.0 copy-start.5
  0.6 3.0 %collective-permute-start.5 = (bf16[512,512]{1,0:T(8,128)(2,1)}, bf16[512,512]{1,0:T(8,128)(2,1)S(1)}, u32[]{:S(2)}, u32[]{:S(2)}) collective-permute-start(bf16[512,512]{1,0:T(8,128)(2,1)} %refs_0_.3), channel_id=1, source_target_pairs={{0,2},{1,3},{2,0},{3,1},{4,6},{5,7},{6,4},{7,5},{8,10},{9,11},{10,... | collective-permute-start | bytes 1572872 | tf_op jit(solution)/shard_map/ppermute | solution.py:548
  3.6 2.2 %open.1 = (f32[72,128]{1,0:T(8,128)}, bf16[512,128]{1,0:T(8,128)(2,1)}, bf16[512,128]{1,0:T(8,128)(2,1)}, f32[16,1024]{1,0:T(8,128)}, f32[4,1024]{1,0:T(4,128)}) custom-call(s32[4,4]{1,0:T(4,128)} %refs_0_.2, s32[4,4]{1,0:T(4,128)} %refs_1_.1, bf16[512,512]{1,0:T(8,128)(2,1)} %refs_2_.1, bf16[3,512]{1,0:T(4,128)(2,1)} %dip.1, s32[3,1024]{1,0:T(4,128)} %owner.1, ...), custom_call_target="tpu_custom_call" | custom-call | flops 1000000 | bytes 12000000 | tf_op jit(solution)/shard_map/open/pallas_call | solution.py:500
  5.8 1.6 %collective-permute-start = (f32[72,128]{1,0:T(8,128)}, f32[72,128]{1,0:T(8,128)S(1)}, u32[]{:S(2)}, u32[]{:S(2)}) collective-permute-start(f32[72,128]{1,0:T(8,128)} %get-tuple-element.22.message), channel_id=1, source_target_pairs={{0,4},{4,0},{8,12},{12,8},{1,5},{5,1},{9,13},{13,9},{2,6},{6,2},{1... | collective-permute-start | bytes 110600 | tf_op jit(solution)/shard_map/ppermute | solution.py:548
  7.5 0.0 copy-start.1
  7.5 0.8 %copy-done.1 = f32[16,1024]{1,0:T(8,128)S(1)} copy-done((f32[16,1024]{1,0:T(8,128)S(1)}, f32[16,1024]{1,0:T(8,128)}, u32[]{:S(2)}) %copy-start.1) | copy-done | bytes 65560
  8.3 0.0 copy-start.10
  8.3 0.8 %copy-done.10 = f32[72,128]{1,0:T(8,128)S(1)} copy-done((f32[72,128]{1,0:T(8,128)S(1)}, f32[72,128]{1,0:T(8,128)}, u32[]{:S(2)}) %copy-start.10) | copy-done | bytes 36888
  9.1 0.0 copy-start.11
  9.1 0.7 %copy-done.11 = bf16[3,512]{1,0:T(4,128)(2,1)S(1)} copy-done((bf16[3,512]{1,0:T(4,128)(2,1)S(1)}, bf16[3,512]{1,0:T(4,128)(2,1)}, u32[]{:S(2)}) %copy-start.11) | copy-done | bytes 3096
  9.7 0.0 copy-start.6
  9.7 0.0 copy-start.2
  9.8 0.1 prepare.1
  9.8 0.2 collective-permute-done.second
  10.0 2.6 %collective-permute-start.1 = (f32[128,128]{1,0:T(8,128)S(1)}, f32[128,128]{1,0:T(8,128)S(1)}, u32[]{:S(2)}, u32[]{:S(2)}) collective-permute-start(f32[128,128]{1,0:T(8,128)S(1)} %merge.5.first.second), channel_id=1, source_target_pairs={{0,8},{4,12},{8,0},{12,4},{1,9},{5,13},{9,1},{13,5},{2,10},{6,14},... | collective-permute-start | bytes 196616 | tf_op jit(solution)/shard_map/ppermute | solution.py:548
  12.6 0.0 collective-permute-start.4
  12.6 0.0 copy-start.4
  12.6 0.9 %copy-done.4 = s32[32,1024]{1,0:T(8,128)S(1)} copy-done((s32[32,1024]{1,0:T(8,128)S(1)}, s32[32,1024]{1,0:T(8,128)}, u32[]{:S(2)}) %copy-start.4) | copy-done | bytes 131096
  13.5 0.0 copy-start.7
  13.5 1.9 %own_gathers.1.done.own_words = s32[160,1024]{1,0:T(8,128)S(1)} custom-call(s32[5,8,8,128]{3,2,1,0:T(8,128)S(1)} %get-tuple-element.25.table.own_table, s32[32,1024]{1,0:T(8,128)S(1)} %copy-done.4), custom_call_target="tpu_custom_call" | custom-call | flops 1000000 | bytes 6000000 | tf_op jit(solution)/shard_map/own_gathers/pallas_call | solution.py:500
  15.4 0.0 copy-start.3
  15.4 0.0 collective-permute-done.1.second
  15.5 0.3 collective-permute-done.5.first
  15.8 0.3 collective-permute-start.6
  16.1 0.0 copy-done.6
  16.1 2.6 %collective-permute-start.8 = (bf16[512,128]{1,0:T(8,128)(2,1)S(1)}, bf16[512,128]{1,0:T(8,128)(2,1)S(1)}, u32[]{:S(2)}, u32[]{:S(2)}) collective-permute-start(bf16[512,128]{1,0:T(8,128)(2,1)S(1)} %tie.4), channel_id=1, source_target_pairs={{0,8},{4,12},{8,0},{12,4},{1,9},{5,13},{9,1},{13,5},{2,10},{6,14},... | collective-permute-start | bytes 393224 | tf_op jit(solution)/shard_map/ppermute | solution.py:548
  18.7 0.2 collective-permute-start.2
  18.9 1.1 %collective-permute-done.2.second = f32[96,128]{1,0:T(8,128)S(1)} collective-permute-done((f32[96,128]{1,0:T(8,128)S(1)}, f32[96,128]{1,0:T(8,128)S(1)}, u32[]{:S(2)}, u32[]{:S(2)}) %collective-permute-start.2) | collective-permute-done | bytes 49184 | tf_op jit(solution)/shard_map/ppermute | solution.py:548
  19.9 1.6 %collective-permute-start.3 = (f32[112,128]{1,0:T(8,128)S(1)}, f32[112,128]{1,0:T(8,128)S(1)}, u32[]{:S(2)}, u32[]{:S(2)}) collective-permute-start(f32[112,128]{1,0:T(8,128)S(1)} %merge.6.first), channel_id=1, source_target_pairs={{0,2},{1,3},{2,0},{3,1},{4,6},{5,7},{6,4},{7,5},{8,10},{9,11},{10,... | collective-permute-start | bytes 172040 | tf_op jit(solution)/shard_map/ppermute | solution.py:548
  21.5 0.0 copy-done.7
  21.5 1.6 %collective-permute-start.7 = (bf16[512,128]{1,0:T(8,128)(2,1)S(1)}, bf16[512,128]{1,0:T(8,128)(2,1)S(1)}, u32[]{:S(2)}, u32[]{:S(2)}) collective-permute-start(bf16[512,128]{1,0:T(8,128)(2,1)S(1)} %copy-done.7), channel_id=1, source_target_pairs={{0,4},{4,0},{8,12},{12,8},{1,5},{5,1},{9,13},{13,9},{2,6},{6,2},{1... | collective-permute-start | bytes 393224 | tf_op jit(solution)/shard_map/ppermute | solution.py:548
  23.1 0.0 copy-done.5
  23.1 0.0 copy-done.2
  23.1 2.7 %pair_forces.1.refs_4_.pair = f32[9,1024]{1,0:T(8,128)S(1)} custom-call(f32[16,1024]{1,0:T(8,128)S(1)} %copy-done.2, s32[160,1024]{1,0:T(8,128)S(1)} %own_gathers.1.done.own_words, s32[5,8,8,128]{3,2,1,0:T(8,128)S(1)} %get-tuple-element.25.table.own_table, f32[160,128]{1,0:T(8,128)S(1)} %get-tuple-element.27.halos, s32[32,1024]{1,0:T(8,128)S(1)} %copy-done.5), custom_call_target="tpu_custom_call" | custom-call | flops 1000000 | bytes 15000000 | tf_op jit(solution)/shard_map/pair_forces/pallas_call | solution.py:500
  25.8 0.0 collective-permute-done.3.second
  25.8 0.0 collective-permute-done.4.refs_1_
  25.8 0.0 collective-permute-done.6.refs_3_
  25.8 0.0 copy-done.3
  25.8 0.8 %field.1 = (f32[16,128]{1,0:T(8,128)S(1)}, bf16[512,2048]{1,0:T(8,128)(2,1)S(1)}) custom-call(f32[144,128]{1,0:T(8,128)S(1)} %merge.7.message, bf16[512,512]{1,0:T(8,128)(2,1)S(1)} %copy-done.3, bf16[512,512]{1,0:T(8,128)(2,1)S(1)} %collective-permute-done.4.refs_1_, bf16[512,512]{1,0:T(8,128)(2,1)S(1)} %tie.3.refs_2_, ...), custom_call_target="tpu_custom_call" | custom-call | flops 1000000 | bytes 5000000 | tf_op jit(solution)/shard_map/field/pallas_call | solution.py:500
  26.6 0.0 collective-permute-done.8.first
  26.7 0.5 %collective-permute-start.9 = (bf16[512,128]{1,0:T(8,128)(2,1)S(1)}, bf16[512,128]{1,0:T(8,128)(2,1)S(1)}, u32[]{:S(2)}, u32[]{:S(2)}) collective-permute-start(bf16[512,128]{1,0:T(8,128)(2,1)S(1)} %tie.5.refs_1_), channel_id=1, source_target_pairs={{0,4},{4,0},{8,12},{12,8},{1,5},{5,1},{9,13},{13,9},{2,6},{6,2},{1... | collective-permute-start | bytes 393224 | tf_op jit(solution)/shard_map/ppermute | solution.py:548
  27.2 1.6 %collective-permute-start.10 = (f32[16,128]{1,0:T(8,128)S(1)}, f32[16,128]{1,0:T(8,128)S(1)}, u32[]{:S(2)}, u32[]{:S(2)}) collective-permute-start(f32[16,128]{1,0:T(8,128)S(1)} %get-tuple-element.31.second.first), channel_id=1, source_target_pairs={{0,4},{4,0},{8,12},{12,8},{1,5},{5,1},{9,13},{13,9},{2,6},{6,2},{1... | collective-permute-start | bytes 24584 | tf_op jit(solution)/shard_map/ppermute | solution.py:548
  28.8 0.8 %product.2.refs_2_.refs_0_ = f32[512,512]{1,0:T(8,128)S(1)} custom-call(f32[144,128]{1,0:T(8,128)S(1)} %merge.7.message, bf16[512,2048]{1,0:T(8,128)(2,1)S(1)} %get-tuple-element.28.dens, bf16[512,128]{1,0:T(8,128)(2,1)S(1)} %copy-done.7, bf16[512,128]{1,0:T(8,128)(2,1)S(1)} %tie.5.refs_1_), custom_call_target="tpu_custom_call" | custom-call | flops 1000000 | bytes 10000000 | tf_op jit(solution)/shard_map/product/pallas_call | solution.py:500
  29.6 2.3 %collective-permute-done.10.second = f32[16,128]{1,0:T(8,128)S(1)} collective-permute-done((f32[16,128]{1,0:T(8,128)S(1)}, f32[16,128]{1,0:T(8,128)S(1)}, u32[]{:S(2)}, u32[]{:S(2)}) %collective-permute-start.10) | collective-permute-done | bytes 8224 | tf_op jit(solution)/shard_map/ppermute | solution.py:548
  31.9 0.0 copy-start.8
  31.9 0.0 copy-start.9
  31.9 0.0 copy-start.12
  31.9 0.0 copy-start.13
  31.9 0.0 copy-start.14
  32.0 1.8 %collective-permute-start.11 = (f32[32,128]{1,0:T(8,128)S(1)}, f32[32,128]{1,0:T(8,128)S(1)}, u32[]{:S(2)}, u32[]{:S(2)}) collective-permute-start(f32[32,128]{1,0:T(8,128)S(1)} %merge.8.first), channel_id=1, source_target_pairs={{0,8},{4,12},{8,0},{12,4},{1,9},{5,13},{9,1},{13,5},{2,10},{6,14},... | collective-permute-start | bytes 49160 | tf_op jit(solution)/shard_map/ppermute | solution.py:548
  33.8 0.0 collective-permute-done.7.refs_0_
  33.8 0.0 collective-permute-done.9.refs_1_
  33.8 1.6 %product.3.refs_0_ = bf16[512,512]{1,0:T(8,128)(2,1)} custom-call(f32[144,128]{1,0:T(8,128)S(1)} %merge.7.message, bf16[512,2048]{1,0:T(8,128)(2,1)S(1)} %get-tuple-element.28.dens, bf16[512,128]{1,0:T(8,128)(2,1)S(1)} %collective-permute-done.7.refs_0_, bf16[512,128]{1,0:T(8,128)(2,1)S(1)} %collective-permute-done.9.refs_1_, ...), custom_call_target="tpu_custom_call" | custom-call | flops 1000000 | bytes 10000000 | tf_op jit(solution)/shard_map/product/pallas_call | solution.py:500
  35.4 1.4 %collective-permute-done.11.second = f32[32,128]{1,0:T(8,128)S(1)} collective-permute-done((f32[32,128]{1,0:T(8,128)S(1)}, f32[32,128]{1,0:T(8,128)S(1)}, u32[]{:S(2)}, u32[]{:S(2)}) %collective-permute-start.11) | collective-permute-done | bytes 16416 | tf_op jit(solution)/shard_map/ppermute | solution.py:548
  36.8 0.0 copy-start
  36.8 1.0 %copy-done = bf16[512,512]{1,0:T(8,128)(2,1)S(1)} copy-done((bf16[512,512]{1,0:T(8,128)(2,1)S(1)}, bf16[512,512]{1,0:T(8,128)(2,1)}, u32[]{:S(2)}) %copy-start) | copy-done | bytes 524312
  37.9 0.0 copy-done.8
  37.9 0.0 copy-done.9
  37.9 0.0 copy-done.12
  37.9 0.0 copy-done.13
  37.9 0.0 copy-done.14
  37.9 1.1 %advance.1 = (f32[3,1024]{1,0:T(4,128)}, f32[3,1024]{1,0:T(4,128)}, f32[3,1024]{1,0:T(4,128)}, f32[4,1024]{1,0:T(4,128)}) custom-call(f32[64,128]{1,0:T(8,128)S(1)} %merge.9.fields, s32[3,1024]{1,0:T(4,128)S(1)} %copy-done.8, f32[16,1024]{1,0:T(8,128)S(1)} %copy-done.2, f32[4,1024]{1,0:T(4,128)S(1)} %copy-done.14, f32[9,1024]{1,0:T(8,128)S(1)} %pair_forces.1.refs_4_.pair, ...), custom_call_target="tpu_custom_call" | custom-call | flops 1000000 | bytes 6000000 | tf_op jit(solution)/shard_map/advance/pallas_call | solution.py:500
  (9 shorter events, 0.0 us)
Async XLA Ops:
  0.6 22.4 %copy-start.5 = (s32[32,1024]{1,0:T(8,128)S(1)}, s32[32,1024]{1,0:T(8,128)}, u32[]{:S(2)}) copy-start(s32[32,1024]{1,0:T(8,128)} %neighbours.3) | copy-start | bytes 393220
  0.6 15.1 %collective-permute-start.5 = (bf16[512,512]{1,0:T(8,128)(2,1)}, bf16[512,512]{1,0:T(8,128)(2,1)S(1)}, u32[]{:S(2)}, u32[]{:S(2)}) collective-permute-start(bf16[512,512]{1,0:T(8,128)(2,1)} %refs_0_.3), channel_id=1, source_target_pairs={{0,2},{1,3},{2,0},{3,1},{4,6},{5,7},{6,4},{7,5},{8,10},{9,11},{10,... | collective-permute-start | bytes 1572872 | tf_op jit(solution)/shard_map/ppermute | solution.py:548
  5.8 4.2 %collective-permute-start = (f32[72,128]{1,0:T(8,128)}, f32[72,128]{1,0:T(8,128)S(1)}, u32[]{:S(2)}, u32[]{:S(2)}) collective-permute-start(f32[72,128]{1,0:T(8,128)} %get-tuple-element.22.message), channel_id=1, source_target_pairs={{0,4},{4,0},{8,12},{12,8},{1,5},{5,1},{9,13},{13,9},{2,6},{6,2},{1... | collective-permute-start | bytes 110600 | tf_op jit(solution)/shard_map/ppermute | solution.py:548
  7.5 0.8 %copy-start.1 = (f32[16,1024]{1,0:T(8,128)S(1)}, f32[16,1024]{1,0:T(8,128)}, u32[]{:S(2)}) copy-start(f32[16,1024]{1,0:T(8,128)} %get-tuple-element.21.sites) | copy-start | bytes 196612
  8.3 0.8 %copy-start.10 = (f32[72,128]{1,0:T(8,128)S(1)}, f32[72,128]{1,0:T(8,128)}, u32[]{:S(2)}) copy-start(f32[72,128]{1,0:T(8,128)} %get-tuple-element.22.message) | copy-start | bytes 110596
  9.1 0.7 %copy-start.11 = (bf16[3,512]{1,0:T(4,128)(2,1)S(1)}, bf16[3,512]{1,0:T(4,128)(2,1)}, u32[]{:S(2)}) copy-start(bf16[3,512]{1,0:T(4,128)(2,1)} %dip.1) | copy-start | bytes 9220
  9.7 6.3 %copy-start.6 = (bf16[512,128]{1,0:T(8,128)(2,1)S(1)}, bf16[512,128]{1,0:T(8,128)(2,1)}, u32[]{:S(2)}) copy-start(bf16[512,128]{1,0:T(8,128)(2,1)} %get-tuple-element.30.first) | copy-start | bytes 393220
  9.7 13.3 %copy-start.2 = (f32[16,1024]{1,0:T(8,128)S(1)}, f32[16,1024]{1,0:T(8,128)}, u32[]{:S(2)}) copy-start(f32[16,1024]{1,0:T(8,128)} %get-tuple-element.21.sites) | copy-start | bytes 196612
  10.0 5.4 %collective-permute-start.1 = (f32[128,128]{1,0:T(8,128)S(1)}, f32[128,128]{1,0:T(8,128)S(1)}, u32[]{:S(2)}, u32[]{:S(2)}) collective-permute-start(f32[128,128]{1,0:T(8,128)S(1)} %merge.5.first.second), channel_id=1, source_target_pairs={{0,8},{4,12},{8,0},{12,4},{1,9},{5,13},{9,1},{13,5},{2,10},{6,14},... | collective-permute-start | bytes 196616 | tf_op jit(solution)/shard_map/ppermute | solution.py:548
  12.6 13.2 %collective-permute-start.4 = (bf16[512,512]{1,0:T(8,128)(2,1)}, bf16[512,512]{1,0:T(8,128)(2,1)S(1)}, u32[]{:S(2)}, u32[]{:S(2)}) collective-permute-start(bf16[512,512]{1,0:T(8,128)(2,1)} %refs_0_.3), channel_id=1, source_target_pairs={{0,1},{1,0},{2,3},{3,2},{4,5},{5,4},{6,7},{7,6},{8,9},{9,8},{10,11... | collective-permute-start | bytes 1572872 | tf_op jit(solution)/shard_map/ppermute | solution.py:548
  12.6 0.9 %copy-start.4 = (s32[32,1024]{1,0:T(8,128)S(1)}, s32[32,1024]{1,0:T(8,128)}, u32[]{:S(2)}) copy-start(s32[32,1024]{1,0:T(8,128)} %neighbours.3) | copy-start | bytes 393220
  13.5 7.9 %copy-start.7 = (bf16[512,128]{1,0:T(8,128)(2,1)S(1)}, bf16[512,128]{1,0:T(8,128)(2,1)}, u32[]{:S(2)}) copy-start(bf16[512,128]{1,0:T(8,128)(2,1)} %get-tuple-element.29.refs_0_) | copy-start | bytes 393220
  15.4 10.4 %copy-start.3 = (bf16[512,512]{1,0:T(8,128)(2,1)S(1)}, bf16[512,512]{1,0:T(8,128)(2,1)}, u32[]{:S(2)}) copy-start(bf16[512,512]{1,0:T(8,128)(2,1)} %refs_0_.3) | copy-start | bytes 1572868
  15.8 10.0 %collective-permute-start.6 = (bf16[512,512]{1,0:T(8,128)(2,1)S(1)}, bf16[512,512]{1,0:T(8,128)(2,1)S(1)}, u32[]{:S(2)}, u32[]{:S(2)}) collective-permute-start(bf16[512,512]{1,0:T(8,128)(2,1)S(1)} %tie.3.refs_2_), channel_id=1, source_target_pairs={{0,1},{1,0},{2,3},{3,2},{4,5},{5,4},{6,7},{7,6},{8,9},{9,8},{10,11... | collective-permute-start | bytes 1572872 | tf_op jit(solution)/shard_map/ppermute | solution.py:548
  16.1 10.6 %collective-permute-start.8 = (bf16[512,128]{1,0:T(8,128)(2,1)S(1)}, bf16[512,128]{1,0:T(8,128)(2,1)S(1)}, u32[]{:S(2)}, u32[]{:S(2)}) collective-permute-start(bf16[512,128]{1,0:T(8,128)(2,1)S(1)} %tie.4), channel_id=1, source_target_pairs={{0,8},{4,12},{8,0},{12,4},{1,9},{5,13},{9,1},{13,5},{2,10},{6,14},... | collective-permute-start | bytes 393224 | tf_op jit(solution)/shard_map/ppermute | solution.py:548
  18.7 1.2 %collective-permute-start.2 = (f32[96,128]{1,0:T(8,128)S(1)}, f32[96,128]{1,0:T(8,128)S(1)}, u32[]{:S(2)}, u32[]{:S(2)}) collective-permute-start(f32[96,128]{1,0:T(8,128)S(1)} %get-tuple-element.26.first.second), channel_id=1, source_target_pairs={{0,1},{1,0},{2,3},{3,2},{4,5},{5,4},{6,7},{7,6},{8,9},{9,8},{10,11... | collective-permute-start | bytes 147464 | tf_op jit(solution)/shard_map/ppermute | solution.py:548
  19.9 5.8 %collective-permute-start.3 = (f32[112,128]{1,0:T(8,128)S(1)}, f32[112,128]{1,0:T(8,128)S(1)}, u32[]{:S(2)}, u32[]{:S(2)}) collective-permute-start(f32[112,128]{1,0:T(8,128)S(1)} %merge.6.first), channel_id=1, source_target_pairs={{0,2},{1,3},{2,0},{3,1},{4,6},{5,7},{6,4},{7,5},{8,10},{9,11},{10,... | collective-permute-start | bytes 172040 | tf_op jit(solution)/shard_map/ppermute | solution.py:548
  21.5 12.3 %collective-permute-start.7 = (bf16[512,128]{1,0:T(8,128)(2,1)S(1)}, bf16[512,128]{1,0:T(8,128)(2,1)S(1)}, u32[]{:S(2)}, u32[]{:S(2)}) collective-permute-start(bf16[512,128]{1,0:T(8,128)(2,1)S(1)} %copy-done.7), channel_id=1, source_target_pairs={{0,4},{4,0},{8,12},{12,8},{1,5},{5,1},{9,13},{13,9},{2,6},{6,2},{1... | collective-permute-start | bytes 393224 | tf_op jit(solution)/shard_map/ppermute | solution.py:548
  26.7 7.1 %collective-permute-start.9 = (bf16[512,128]{1,0:T(8,128)(2,1)S(1)}, bf16[512,128]{1,0:T(8,128)(2,1)S(1)}, u32[]{:S(2)}, u32[]{:S(2)}) collective-permute-start(bf16[512,128]{1,0:T(8,128)(2,1)S(1)} %tie.5.refs_1_), channel_id=1, source_target_pairs={{0,4},{4,0},{8,12},{12,8},{1,5},{5,1},{9,13},{13,9},{2,6},{6,2},{1... | collective-permute-start | bytes 393224 | tf_op jit(solution)/shard_map/ppermute | solution.py:548
  27.2 4.7 %collective-permute-start.10 = (f32[16,128]{1,0:T(8,128)S(1)}, f32[16,128]{1,0:T(8,128)S(1)}, u32[]{:S(2)}, u32[]{:S(2)}) collective-permute-start(f32[16,128]{1,0:T(8,128)S(1)} %get-tuple-element.31.second.first), channel_id=1, source_target_pairs={{0,4},{4,0},{8,12},{12,8},{1,5},{5,1},{9,13},{13,9},{2,6},{6,2},{1... | collective-permute-start | bytes 24584 | tf_op jit(solution)/shard_map/ppermute | solution.py:548
  31.9 6.0 %copy-start.8 = (s32[3,1024]{1,0:T(4,128)S(1)}, s32[3,1024]{1,0:T(4,128)}, u32[]{:S(2)}) copy-start(s32[3,1024]{1,0:T(4,128)} %owner.1) | copy-start | bytes 36868
  31.9 6.0 %copy-start.9 = (f32[3,1024]{1,0:T(4,128)S(1)}, f32[3,1024]{1,0:T(4,128)}, u32[]{:S(2)}) copy-start(f32[3,1024]{1,0:T(4,128)} %centres.1) | copy-start | bytes 36868
  31.9 6.0 %copy-start.12 = (f32[3,1024]{1,0:T(4,128)S(1)}, f32[3,1024]{1,0:T(4,128)}, u32[]{:S(2)}) copy-start(f32[3,1024]{1,0:T(4,128)} %velocity.1) | copy-start | bytes 36868
  31.9 6.0 %copy-start.13 = (f32[3,1024]{1,0:T(4,128)S(1)}, f32[3,1024]{1,0:T(4,128)}, u32[]{:S(2)}) copy-start(f32[3,1024]{1,0:T(4,128)} %angmom.1) | copy-start | bytes 36868
  31.9 6.0 %copy-start.14 = (f32[4,1024]{1,0:T(4,128)S(1)}, f32[4,1024]{1,0:T(4,128)}, u32[]{:S(2)}) copy-start(f32[4,1024]{1,0:T(4,128)} %get-tuple-element.32.quat) | copy-start | bytes 49156
  32.0 4.9 %collective-permute-start.11 = (f32[32,128]{1,0:T(8,128)S(1)}, f32[32,128]{1,0:T(8,128)S(1)}, u32[]{:S(2)}, u32[]{:S(2)}) collective-permute-start(f32[32,128]{1,0:T(8,128)S(1)} %merge.8.first), channel_id=1, source_target_pairs={{0,8},{4,12},{8,0},{12,4},{1,9},{5,13},{9,1},{13,5},{2,10},{6,14},... | collective-permute-start | bytes 49160 | tf_op jit(solution)/shard_map/ppermute | solution.py:548
  36.8 1.0 %copy-start = (bf16[512,512]{1,0:T(8,128)(2,1)S(1)}, bf16[512,512]{1,0:T(8,128)(2,1)}, u32[]{:S(2)}) copy-start(bf16[512,512]{1,0:T(8,128)(2,1)} %product.3.refs_0_) | copy-start | bytes 1572868

commit v5 on v3

--- a/solution.py
+++ b/solution.py
@@ -442,23 +442,24 @@
             for col in range(cols_b):
                 panel[place, row * BLOCK : (row + 1) * BLOCK, at(col)] = block * flag(row * cols_b + col)
 
-    def one_row(row, carry):
-        lines = pl.ds(pl.multiple_of(row * BLOCK, BLOCK), BLOCK)
+    chunk = 2 * BLOCK
+    for part in range(rows // chunk):
+        lines = slice(part * chunk, (part + 1) * chunk)
         value = contract(dens[lines, spans[0]], panel[0], ((1,), (0,)))
         for place in range(1, count):
             value = value + contract(dens[lines, spans[place]], panel[place], ((1,), (0,)))
         if before:
             out[lines, :] = (value + before[0][lines, :]).astype(out.dtype)
-        else:
+            continue
+        for half in range(2):
+            row = 2 * part + half
+            lines = slice(row * BLOCK, (row + 1) * BLOCK)
             own = UNIT * COUPLE * message[pl.ds(here_row * rows_b + row, 1), :]
             across = jnp.transpose(jnp.broadcast_to(own, (BLOCK, BLOCK)))
             for col in range(cols_b):
                 pot = UNIT * COUPLE * message[pl.ds(here_col * cols_b + col, 1), :]
                 sums = (across + pot) * dens[lines, at(col)].astype(F32)
-                out[lines, at(col)] = (value[:, at(col)] + sums).astype(out.dtype)
-        return carry
-
-    lax.fori_loop(0, rows_b, one_row, 0)
+                out[lines, at(col)] = (value[half * BLOCK : (half + 1) * BLOCK, at(col)] + sums).astype(out.dtype)
 
 
 def tie_kernel(first, second, out):

time: 38.9 us -> 38.2 us (0.982)
  Pallas kernels: 12.5 us -> 11.2 us
  waiting for transfers between devices: 5.69 us -> 6.34 us
    pallas_call x17, Pallas kernels: 12.5 us -> 11.2 us  [call(): pl.pallas_call(kernel, out_shape=[jax.ShapeDtypeStruct(shape, dtype) for...]
    ppermute x12, waiting for transfers between devices: 5.69 us -> 6.34 us  [swap(): return lax.ppermute(value, axis, [(i, i ^ step) for i in range(count)])]
  transfers between devices with their start and end apart: 12 -> 12, of which waited for: 5 -> 5; matrix products, arithmetic and copies ran while one was open for 0% -> 0% of each run, Pallas kernels for 26% -> 25%
where the time goes in v5:
time: 38.2 us; the launch traced here: 37.9 us
  starting transfers between devices  16.3 us (43%)
  Pallas kernels  11.2 us (29%)
  waiting for transfers between devices  6.34 us (17%)
  local copies, waits for them, and re-layouts  3.26 us (9%)
  between operations  0.82 us (2%)
    ppermute x12, starting transfers between devices, swap(): return lax.ppermute(value, axis, [(i, i ^ step) for i in range(count)])  16.3 us
    pallas_call x17, Pallas kernels, call(): pl.pallas_call(kernel, out_shape=[jax.ShapeDtypeStruct(shape, dtype) for...  11.2 us
    ppermute x12, waiting for transfers between devices, swap(): return lax.ppermute(value, axis, [(i, i ^ step) for i in range(count)])  6.34 us
    unnamed x28, local copies, waits for them, and re-layouts  3.26 us
  transfers between devices with their start and end apart: 12, of which 5 were waited for; matrix products, arithmetic and copies ran while one was open for 0% of the time, Pallas kernels for 25%

profile of v5, /device:TPU:0, one launch (start us, length us, event | category | flops | bytes accessed | tf_op | source)
XLA Modules:
  0.0 37.9 jit_solution(17175685777836390034)
XLA Ops:
  0.6 0.0 copy-start.4
  0.6 3.0 %collective-permute-start.5 = (bf16[512,512]{1,0:T(8,128)(2,1)}, bf16[512,512]{1,0:T(8,128)(2,1)S(1)}, u32[]{:S(2)}, u32[]{:S(2)}) collective-permute-start(bf16[512,512]{1,0:T(8,128)(2,1)} %refs_0_.3), channel_id=1, source_target_pairs={{0,2},{1,3},{2,0},{3,1},{4,6},{5,7},{6,4},{7,5},{8,10},{9,11},{10,... | collective-permute-start | bytes 1572872 | tf_op jit(solution)/shard_map/ppermute | solution.py:548
  3.6 2.2 %open.1 = (f32[72,128]{1,0:T(8,128)}, bf16[512,128]{1,0:T(8,128)(2,1)}, bf16[512,128]{1,0:T(8,128)(2,1)}, f32[16,1024]{1,0:T(8,128)}, f32[4,1024]{1,0:T(4,128)}) custom-call(s32[4,4]{1,0:T(4,128)} %refs_0_.2, s32[4,4]{1,0:T(4,128)} %refs_1_.1, bf16[512,512]{1,0:T(8,128)(2,1)} %refs_2_.1, bf16[3,512]{1,0:T(4,128)(2,1)} %dip.1, s32[3,1024]{1,0:T(4,128)} %owner.1, ...), custom_call_target="tpu_custom_call" | custom-call | flops 1000000 | bytes 12000000 | tf_op jit(solution)/shard_map/open/pallas_call | solution.py:500
  5.8 1.6 %collective-permute-start = (f32[72,128]{1,0:T(8,128)}, f32[72,128]{1,0:T(8,128)S(1)}, u32[]{:S(2)}, u32[]{:S(2)}) collective-permute-start(f32[72,128]{1,0:T(8,128)} %get-tuple-element.22.message), channel_id=1, source_target_pairs={{0,4},{4,0},{8,12},{12,8},{1,5},{5,1},{9,13},{13,9},{2,6},{6,2},{1... | collective-permute-start | bytes 110600 | tf_op jit(solution)/shard_map/ppermute | solution.py:548
  7.5 0.0 copy-start
  7.5 0.8 %copy-done = f32[16,1024]{1,0:T(8,128)S(1)} copy-done((f32[16,1024]{1,0:T(8,128)S(1)}, f32[16,1024]{1,0:T(8,128)}, u32[]{:S(2)}) %copy-start) | copy-done | bytes 65560
  8.3 0.0 copy-start.9
  8.3 0.8 %copy-done.9 = f32[72,128]{1,0:T(8,128)S(1)} copy-done((f32[72,128]{1,0:T(8,128)S(1)}, f32[72,128]{1,0:T(8,128)}, u32[]{:S(2)}) %copy-start.9) | copy-done | bytes 36888
  9.1 0.0 copy-start.10
  9.1 0.7 %copy-done.10 = bf16[3,512]{1,0:T(4,128)(2,1)S(1)} copy-done((bf16[3,512]{1,0:T(4,128)(2,1)S(1)}, bf16[3,512]{1,0:T(4,128)(2,1)}, u32[]{:S(2)}) %copy-start.10) | copy-done | bytes 3096
  9.8 0.0 copy-start.5
  9.8 0.0 copy-start.1
  9.8 0.1 prepare.1
  9.8 0.2 collective-permute-done.second
  10.1 2.6 %collective-permute-start.1 = (f32[128,128]{1,0:T(8,128)S(1)}, f32[128,128]{1,0:T(8,128)S(1)}, u32[]{:S(2)}, u32[]{:S(2)}) collective-permute-start(f32[128,128]{1,0:T(8,128)S(1)} %merge.5.first.second), channel_id=1, source_target_pairs={{0,8},{4,12},{8,0},{12,4},{1,9},{5,13},{9,1},{13,5},{2,10},{6,14},... | collective-permute-start | bytes 196616 | tf_op jit(solution)/shard_map/ppermute | solution.py:548
  12.7 0.0 collective-permute-start.4
  12.7 0.0 copy-start.3
  12.7 0.9 %copy-done.3 = s32[32,1024]{1,0:T(8,128)S(1)} copy-done((s32[32,1024]{1,0:T(8,128)S(1)}, s32[32,1024]{1,0:T(8,128)}, u32[]{:S(2)}) %copy-start.3) | copy-done | bytes 131096
  13.6 1.9 %own_gathers.1.done.own_words = s32[160,1024]{1,0:T(8,128)S(1)} custom-call(s32[5,8,8,128]{3,2,1,0:T(8,128)S(1)} %get-tuple-element.25.table.own_table, s32[32,1024]{1,0:T(8,128)S(1)} %copy-done.3), custom_call_target="tpu_custom_call" | custom-call | flops 1000000 | bytes 6000000 | tf_op jit(solution)/shard_map/own_gathers/pallas_call | solution.py:500
  15.5 0.0 copy-start.2
  15.5 0.0 collective-permute-done.1.second
  15.5 0.3 collective-permute-done.5.first
  15.8 0.0 copy-start.6
  15.8 0.3 collective-permute-start.6
  16.1 0.0 copy-done.5
  16.1 2.6 %collective-permute-start.8 = (bf16[512,128]{1,0:T(8,128)(2,1)S(1)}, bf16[512,128]{1,0:T(8,128)(2,1)S(1)}, u32[]{:S(2)}, u32[]{:S(2)}) collective-permute-start(bf16[512,128]{1,0:T(8,128)(2,1)S(1)} %tie.4), channel_id=1, source_target_pairs={{0,8},{4,12},{8,0},{12,4},{1,9},{5,13},{9,1},{13,5},{2,10},{6,14},... | collective-permute-start | bytes 393224 | tf_op jit(solution)/shard_map/ppermute | solution.py:548
  18.7 0.2 collective-permute-start.2
  18.9 1.1 %collective-permute-done.2.second = f32[96,128]{1,0:T(8,128)S(1)} collective-permute-done((f32[96,128]{1,0:T(8,128)S(1)}, f32[96,128]{1,0:T(8,128)S(1)}, u32[]{:S(2)}, u32[]{:S(2)}) %collective-permute-start.2) | collective-permute-done | bytes 49184 | tf_op jit(solution)/shard_map/ppermute | solution.py:548
  19.9 1.6 %collective-permute-start.3 = (f32[112,128]{1,0:T(8,128)S(1)}, f32[112,128]{1,0:T(8,128)S(1)}, u32[]{:S(2)}, u32[]{:S(2)}) collective-permute-start(f32[112,128]{1,0:T(8,128)S(1)} %merge.6.first), channel_id=1, source_target_pairs={{0,2},{1,3},{2,0},{3,1},{4,6},{5,7},{6,4},{7,5},{8,10},{9,11},{10,... | collective-permute-start | bytes 172040 | tf_op jit(solution)/shard_map/ppermute | solution.py:548
  21.5 0.0 copy-done.4
  21.5 0.0 copy-done.1
  21.5 2.7 %pair_forces.1.refs_4_.pair = f32[9,1024]{1,0:T(8,128)S(1)} custom-call(f32[16,1024]{1,0:T(8,128)S(1)} %copy-done.1, s32[160,1024]{1,0:T(8,128)S(1)} %own_gathers.1.done.own_words, s32[5,8,8,128]{3,2,1,0:T(8,128)S(1)} %get-tuple-element.25.table.own_table, f32[160,128]{1,0:T(8,128)S(1)} %get-tuple-element.27.halos, s32[32,1024]{1,0:T(8,128)S(1)} %copy-done.4), custom_call_target="tpu_custom_call" | custom-call | flops 1000000 | bytes 15000000 | tf_op jit(solution)/shard_map/pair_forces/pallas_call | solution.py:500
  24.2 0.0 collective-permute-done.3.second
  24.2 0.0 collective-permute-done.4.refs_1_
  24.2 0.0 collective-permute-done.6.refs_3_
  24.2 0.0 copy-done.2
  24.3 0.8 %field.1 = (f32[16,128]{1,0:T(8,128)S(1)}, bf16[512,2048]{1,0:T(8,128)(2,1)S(1)}) custom-call(f32[144,128]{1,0:T(8,128)S(1)} %merge.7.message, bf16[512,512]{1,0:T(8,128)(2,1)S(1)} %copy-done.2, bf16[512,512]{1,0:T(8,128)(2,1)S(1)} %collective-permute-done.4.refs_1_, bf16[512,512]{1,0:T(8,128)(2,1)S(1)} %tie.3.refs_2_, ...), custom_call_target="tpu_custom_call" | custom-call | flops 1000000 | bytes 5000000 | tf_op jit(solution)/shard_map/field/pallas_call | solution.py:500
  25.1 0.0 copy-start.7
  25.1 0.0 copy-start.8
  25.1 0.0 copy-start.11
  25.1 0.0 copy-start.12
  25.1 0.0 copy-start.13
  25.1 1.6 %collective-permute-start.9 = (f32[16,128]{1,0:T(8,128)S(1)}, f32[16,128]{1,0:T(8,128)S(1)}, u32[]{:S(2)}, u32[]{:S(2)}) collective-permute-start(f32[16,128]{1,0:T(8,128)S(1)} %get-tuple-element.31.first), channel_id=1, source_target_pairs={{0,4},{4,0},{8,12},{12,8},{1,5},{5,1},{9,13},{13,9},{2,6},{6,2},{1... | collective-permute-start | bytes 24584 | tf_op jit(solution)/shard_map/ppermute | solution.py:548
  26.8 0.0 copy-done.6
  26.8 0.4 %collective-permute-start.7 = (bf16[512,128]{1,0:T(8,128)(2,1)S(1)}, bf16[512,128]{1,0:T(8,128)(2,1)S(1)}, u32[]{:S(2)}, u32[]{:S(2)}) collective-permute-start(bf16[512,128]{1,0:T(8,128)(2,1)S(1)} %copy-done.6), channel_id=1, source_target_pairs={{0,4},{4,0},{8,12},{12,8},{1,5},{5,1},{9,13},{13,9},{2,6},{6,2},{1... | collective-permute-start | bytes 393224 | tf_op jit(solution)/shard_map/ppermute | solution.py:548
  27.2 1.6 %collective-permute-done.9.second = f32[16,128]{1,0:T(8,128)S(1)} collective-permute-done((f32[16,128]{1,0:T(8,128)S(1)}, f32[16,128]{1,0:T(8,128)S(1)}, u32[]{:S(2)}, u32[]{:S(2)}) %collective-permute-start.9) | collective-permute-done | bytes 8224 | tf_op jit(solution)/shard_map/ppermute | solution.py:548
  28.9 0.0 collective-permute-done.8.first
  28.9 1.6 %collective-permute-start.10 = (bf16[512,128]{1,0:T(8,128)(2,1)S(1)}, bf16[512,128]{1,0:T(8,128)(2,1)S(1)}, u32[]{:S(2)}, u32[]{:S(2)}) collective-permute-start(bf16[512,128]{1,0:T(8,128)(2,1)S(1)} %tie.5.refs_1_), channel_id=1, source_target_pairs={{0,4},{4,0},{8,12},{12,8},{1,5},{5,1},{9,13},{13,9},{2,6},{6,2},{1... | collective-permute-start | bytes 393224 | tf_op jit(solution)/shard_map/ppermute | solution.py:548
  30.5 0.7 %collective-permute-start.11 = (f32[32,128]{1,0:T(8,128)S(1)}, f32[32,128]{1,0:T(8,128)S(1)}, u32[]{:S(2)}, u32[]{:S(2)}) collective-permute-start(f32[32,128]{1,0:T(8,128)S(1)} %merge.8.second.first), channel_id=1, source_target_pairs={{0,8},{4,12},{8,0},{12,4},{1,9},{5,13},{9,1},{13,5},{2,10},{6,14},... | collective-permute-start | bytes 49160 | tf_op jit(solution)/shard_map/ppermute | solution.py:548
  31.2 0.8 %product.2.refs_2_ = f32[512,512]{1,0:T(8,128)S(1)} custom-call(f32[144,128]{1,0:T(8,128)S(1)} %merge.7.message, bf16[512,2048]{1,0:T(8,128)(2,1)S(1)} %get-tuple-element.28.dens, bf16[512,128]{1,0:T(8,128)(2,1)S(1)} %copy-done.6, bf16[512,128]{1,0:T(8,128)(2,1)S(1)} %tie.5.refs_1_), custom_call_target="tpu_custom_call" | custom-call | flops 1000000 | bytes 10000000 | tf_op jit(solution)/shard_map/product/pallas_call | solution.py:500
  32.0 3.1 %collective-permute-done.11.second = f32[32,128]{1,0:T(8,128)S(1)} collective-permute-done((f32[32,128]{1,0:T(8,128)S(1)}, f32[32,128]{1,0:T(8,128)S(1)}, u32[]{:S(2)}, u32[]{:S(2)}) %collective-permute-start.11) | collective-permute-done | bytes 16416 | tf_op jit(solution)/shard_map/ppermute | solution.py:548
  35.2 0.0 copy-done.7
  35.2 0.0 copy-done.8
  35.2 0.0 copy-done.11
  35.2 0.0 copy-done.12
  35.2 0.0 copy-done.13
  35.2 1.1 %advance.1 = (f32[3,1024]{1,0:T(4,128)}, f32[3,1024]{1,0:T(4,128)}, f32[3,1024]{1,0:T(4,128)}, f32[4,1024]{1,0:T(4,128)}) custom-call(f32[64,128]{1,0:T(8,128)S(1)} %merge.9.fields, s32[3,1024]{1,0:T(4,128)S(1)} %copy-done.7, f32[16,1024]{1,0:T(8,128)S(1)} %copy-done.1, f32[4,1024]{1,0:T(4,128)S(1)} %copy-done.13, f32[9,1024]{1,0:T(8,128)S(1)} %pair_forces.1.refs_4_.pair, ...), custom_call_target="tpu_custom_call" | custom-call | flops 1000000 | bytes 6000000 | tf_op jit(solution)/shard_map/advance/pallas_call | solution.py:500
  36.3 0.0 collective-permute-done.7.refs_0_
  36.3 0.0 collective-permute-done.10.refs_1_
  36.3 1.6 %product.3 = bf16[512,512]{1,0:T(8,128)(2,1)} custom-call(f32[144,128]{1,0:T(8,128)S(1)} %merge.7.message, bf16[512,2048]{1,0:T(8,128)(2,1)S(1)} %get-tuple-element.28.dens, bf16[512,128]{1,0:T(8,128)(2,1)S(1)} %collective-permute-done.7.refs_0_, bf16[512,128]{1,0:T(8,128)(2,1)S(1)} %collective-permute-done.10.refs_1_, f32[512,512]{1,0:T(8,128)S(1)} %product.2.refs_2_), custom_call_target="tpu_custom_call" | custom-call | flops 1000000 | bytes 10000000 | tf_op jit(solution)/shard_map/product/pallas_call | solution.py:500
  (9 shorter events, 0.0 us)
Async XLA Ops:
  0.6 20.9 %copy-start.4 = (s32[32,1024]{1,0:T(8,128)S(1)}, s32[32,1024]{1,0:T(8,128)}, u32[]{:S(2)}) copy-start(s32[32,1024]{1,0:T(8,128)} %neighbours.3) | copy-start | bytes 393220
  0.6 15.1 %collective-permute-start.5 = (bf16[512,512]{1,0:T(8,128)(2,1)}, bf16[512,512]{1,0:T(8,128)(2,1)S(1)}, u32[]{:S(2)}, u32[]{:S(2)}) collective-permute-start(bf16[512,512]{1,0:T(8,128)(2,1)} %refs_0_.3), channel_id=1, source_target_pairs={{0,2},{1,3},{2,0},{3,1},{4,6},{5,7},{6,4},{7,5},{8,10},{9,11},{10,... | collective-permute-start | bytes 1572872 | tf_op jit(solution)/shard_map/ppermute | solution.py:548
  5.8 4.2 %collective-permute-start = (f32[72,128]{1,0:T(8,128)}, f32[72,128]{1,0:T(8,128)S(1)}, u32[]{:S(2)}, u32[]{:S(2)}) collective-permute-start(f32[72,128]{1,0:T(8,128)} %get-tuple-element.22.message), channel_id=1, source_target_pairs={{0,4},{4,0},{8,12},{12,8},{1,5},{5,1},{9,13},{13,9},{2,6},{6,2},{1... | collective-permute-start | bytes 110600 | tf_op jit(solution)/shard_map/ppermute | solution.py:548
  7.5 0.8 %copy-start = (f32[16,1024]{1,0:T(8,128)S(1)}, f32[16,1024]{1,0:T(8,128)}, u32[]{:S(2)}) copy-start(f32[16,1024]{1,0:T(8,128)} %get-tuple-element.21.sites) | copy-start | bytes 196612
  8.3 0.8 %copy-start.9 = (f32[72,128]{1,0:T(8,128)S(1)}, f32[72,128]{1,0:T(8,128)}, u32[]{:S(2)}) copy-start(f32[72,128]{1,0:T(8,128)} %get-tuple-element.22.message) | copy-start | bytes 110596
  9.1 0.7 %copy-start.10 = (bf16[3,512]{1,0:T(4,128)(2,1)S(1)}, bf16[3,512]{1,0:T(4,128)(2,1)}, u32[]{:S(2)}) copy-start(bf16[3,512]{1,0:T(4,128)(2,1)} %dip.1) | copy-start | bytes 9220
  9.8 6.3 %copy-start.5 = (bf16[512,128]{1,0:T(8,128)(2,1)S(1)}, bf16[512,128]{1,0:T(8,128)(2,1)}, u32[]{:S(2)}) copy-start(bf16[512,128]{1,0:T(8,128)(2,1)} %get-tuple-element.30.first) | copy-start | bytes 393220
  9.8 11.7 %copy-start.1 = (f32[16,1024]{1,0:T(8,128)S(1)}, f32[16,1024]{1,0:T(8,128)}, u32[]{:S(2)}) copy-start(f32[16,1024]{1,0:T(8,128)} %get-tuple-element.21.sites) | copy-start | bytes 196612
  10.1 5.4 %collective-permute-start.1 = (f32[128,128]{1,0:T(8,128)S(1)}, f32[128,128]{1,0:T(8,128)S(1)}, u32[]{:S(2)}, u32[]{:S(2)}) collective-permute-start(f32[128,128]{1,0:T(8,128)S(1)} %merge.5.first.second), channel_id=1, source_target_pairs={{0,8},{4,12},{8,0},{12,4},{1,9},{5,13},{9,1},{13,5},{2,10},{6,14},... | collective-permute-start | bytes 196616 | tf_op jit(solution)/shard_map/ppermute | solution.py:548
  12.7 11.6 %collective-permute-start.4 = (bf16[512,512]{1,0:T(8,128)(2,1)}, bf16[512,512]{1,0:T(8,128)(2,1)S(1)}, u32[]{:S(2)}, u32[]{:S(2)}) collective-permute-start(bf16[512,512]{1,0:T(8,128)(2,1)} %refs_0_.3), channel_id=1, source_target_pairs={{0,1},{1,0},{2,3},{3,2},{4,5},{5,4},{6,7},{7,6},{8,9},{9,8},{10,11... | collective-permute-start | bytes 1572872 | tf_op jit(solution)/shard_map/ppermute | solution.py:548
  12.7 0.9 %copy-start.3 = (s32[32,1024]{1,0:T(8,128)S(1)}, s32[32,1024]{1,0:T(8,128)}, u32[]{:S(2)}) copy-start(s32[32,1024]{1,0:T(8,128)} %neighbours.3) | copy-start | bytes 393220
  15.5 8.8 %copy-start.2 = (bf16[512,512]{1,0:T(8,128)(2,1)S(1)}, bf16[512,512]{1,0:T(8,128)(2,1)}, u32[]{:S(2)}) copy-start(bf16[512,512]{1,0:T(8,128)(2,1)} %refs_0_.3) | copy-start | bytes 1572868
  15.8 11.0 %copy-start.6 = (bf16[512,128]{1,0:T(8,128)(2,1)S(1)}, bf16[512,128]{1,0:T(8,128)(2,1)}, u32[]{:S(2)}) copy-start(bf16[512,128]{1,0:T(8,128)(2,1)} %get-tuple-element.29.refs_0_) | copy-start | bytes 393220
  15.8 8.4 %collective-permute-start.6 = (bf16[512,512]{1,0:T(8,128)(2,1)S(1)}, bf16[512,512]{1,0:T(8,128)(2,1)S(1)}, u32[]{:S(2)}, u32[]{:S(2)}) collective-permute-start(bf16[512,512]{1,0:T(8,128)(2,1)S(1)} %tie.3.refs_2_), channel_id=1, source_target_pairs={{0,1},{1,0},{2,3},{3,2},{4,5},{5,4},{6,7},{7,6},{8,9},{9,8},{10,11... | collective-permute-start | bytes 1572872 | tf_op jit(solution)/shard_map/ppermute | solution.py:548
  16.1 12.8 %collective-permute-start.8 = (bf16[512,128]{1,0:T(8,128)(2,1)S(1)}, bf16[512,128]{1,0:T(8,128)(2,1)S(1)}, u32[]{:S(2)}, u32[]{:S(2)}) collective-permute-start(bf16[512,128]{1,0:T(8,128)(2,1)S(1)} %tie.4), channel_id=1, source_target_pairs={{0,8},{4,12},{8,0},{12,4},{1,9},{5,13},{9,1},{13,5},{2,10},{6,14},... | collective-permute-start | bytes 393224 | tf_op jit(solution)/shard_map/ppermute | solution.py:548
  18.7 1.2 %collective-permute-start.2 = (f32[96,128]{1,0:T(8,128)S(1)}, f32[96,128]{1,0:T(8,128)S(1)}, u32[]{:S(2)}, u32[]{:S(2)}) collective-permute-start(f32[96,128]{1,0:T(8,128)S(1)} %get-tuple-element.26.first.second), channel_id=1, source_target_pairs={{0,1},{1,0},{2,3},{3,2},{4,5},{5,4},{6,7},{7,6},{8,9},{9,8},{10,11... | collective-permute-start | bytes 147464 | tf_op jit(solution)/shard_map/ppermute | solution.py:548
  19.9 4.2 %collective-permute-start.3 = (f32[112,128]{1,0:T(8,128)S(1)}, f32[112,128]{1,0:T(8,128)S(1)}, u32[]{:S(2)}, u32[]{:S(2)}) collective-permute-start(f32[112,128]{1,0:T(8,128)S(1)} %merge.6.first), channel_id=1, source_target_pairs={{0,2},{1,3},{2,0},{3,1},{4,6},{5,7},{6,4},{7,5},{8,10},{9,11},{10,... | collective-permute-start | bytes 172040 | tf_op jit(solution)/shard_map/ppermute | solution.py:548
  25.1 10.1 %copy-start.7 = (s32[3,1024]{1,0:T(4,128)S(1)}, s32[3,1024]{1,0:T(4,128)}, u32[]{:S(2)}) copy-start(s32[3,1024]{1,0:T(4,128)} %owner.1) | copy-start | bytes 36868
  25.1 10.1 %copy-start.8 = (f32[3,1024]{1,0:T(4,128)S(1)}, f32[3,1024]{1,0:T(4,128)}, u32[]{:S(2)}) copy-start(f32[3,1024]{1,0:T(4,128)} %centres.1) | copy-start | bytes 36868
  25.1 10.1 %copy-start.11 = (f32[3,1024]{1,0:T(4,128)S(1)}, f32[3,1024]{1,0:T(4,128)}, u32[]{:S(2)}) copy-start(f32[3,1024]{1,0:T(4,128)} %velocity.1) | copy-start | bytes 36868
  25.1 10.1 %copy-start.12 = (f32[3,1024]{1,0:T(4,128)S(1)}, f32[3,1024]{1,0:T(4,128)}, u32[]{:S(2)}) copy-start(f32[3,1024]{1,0:T(4,128)} %angmom.1) | copy-start | bytes 36868
  25.1 10.1 %copy-start.13 = (f32[4,1024]{1,0:T(4,128)S(1)}, f32[4,1024]{1,0:T(4,128)}, u32[]{:S(2)}) copy-start(f32[4,1024]{1,0:T(4,128)} %get-tuple-element.32.quat) | copy-start | bytes 49156
  25.1 3.7 %collective-permute-start.9 = (f32[16,128]{1,0:T(8,128)S(1)}, f32[16,128]{1,0:T(8,128)S(1)}, u32[]{:S(2)}, u32[]{:S(2)}) collective-permute-start(f32[16,128]{1,0:T(8,128)S(1)} %get-tuple-element.31.first), channel_id=1, source_target_pairs={{0,4},{4,0},{8,12},{12,8},{1,5},{5,1},{9,13},{13,9},{2,6},{6,2},{1... | collective-permute-start | bytes 24584 | tf_op jit(solution)/shard_map/ppermute | solution.py:548
  26.8 9.5 %collective-permute-start.7 = (bf16[512,128]{1,0:T(8,128)(2,1)S(1)}, bf16[512,128]{1,0:T(8,128)(2,1)S(1)}, u32[]{:S(2)}, u32[]{:S(2)}) collective-permute-start(bf16[512,128]{1,0:T(8,128)(2,1)S(1)} %copy-done.6), channel_id=1, source_target_pairs={{0,4},{4,0},{8,12},{12,8},{1,5},{5,1},{9,13},{13,9},{2,6},{6,2},{1... | collective-permute-start | bytes 393224 | tf_op jit(solution)/shard_map/ppermute | solution.py:548
  28.9 7.4 %collective-permute-start.10 = (bf16[512,128]{1,0:T(8,128)(2,1)S(1)}, bf16[512,128]{1,0:T(8,128)(2,1)S(1)}, u32[]{:S(2)}, u32[]{:S(2)}) collective-permute-start(bf16[512,128]{1,0:T(8,128)(2,1)S(1)} %tie.5.refs_1_), channel_id=1, source_target_pairs={{0,4},{4,0},{8,12},{12,8},{1,5},{5,1},{9,13},{13,9},{2,6},{6,2},{1... | collective-permute-start | bytes 393224 | tf_op jit(solution)/shard_map/ppermute | solution.py:548
  30.5 4.6 %collective-permute-start.11 = (f32[32,128]{1,0:T(8,128)S(1)}, f32[32,128]{1,0:T(8,128)S(1)}, u32[]{:S(2)}, u32[]{:S(2)}) collective-permute-start(f32[32,128]{1,0:T(8,128)S(1)} %merge.8.second.first), channel_id=1, source_target_pairs={{0,8},{4,12},{8,0},{12,4},{1,9},{5,13},{9,1},{13,5},{2,10},{6,14},... | collective-permute-start | bytes 49160 | tf_op jit(solution)/shard_map/ppermute | solution.py:548

commit v6 on v5

--- a/solution.py
+++ b/solution.py
@@ -660,7 +660,7 @@
         field = merge(field, swap(field, "row", rows_n, step), 0)
         if step == 1:
             small_all = relay(small_all, "row", rows_n, field)
-    early = [0] + steps[1:]
+    early = [0] + steps
     late = [step for step in range(rows_n) if step not in early]
     partial, kinds = [], [(early, F32 if late else BF16)] + ([(late, BF16)] if late else [])
     for these, kind in kinds:

time: 38.2 us -> 37.9 us (level)
  transfers between devices with their start and end apart: 12 -> 12, of which waited for: 5 -> 6; matrix products, arithmetic and copies ran while one was open for 0% -> 0% of each run, Pallas kernels for 25% -> 26%
where the time goes in v6:
time: 37.9 us; the launch traced here: 37.6 us
  starting transfers between devices  16.3 us (43%)
  Pallas kernels  11.2 us (30%)
  waiting for transfers between devices  6.06 us (16%)
  local copies, waits for them, and re-layouts  3.26 us (9%)
  between operations  0.82 us (2%)
    ppermute x12, starting transfers between devices, swap(): return lax.ppermute(value, axis, [(i, i ^ step) for i in range(count)])  16.3 us
    pallas_call x17, Pallas kernels, call(): pl.pallas_call(kernel, out_shape=[jax.ShapeDtypeStruct(shape, dtype) for...  11.2 us
    ppermute x12, waiting for transfers between devices, swap(): return lax.ppermute(value, axis, [(i, i ^ step) for i in range(count)])  6.06 us
    unnamed x28, local copies, waits for them, and re-layouts  3.26 us
  transfers between devices with their start and end apart: 12, of which 6 were waited for; matrix products, arithmetic and copies ran while one was open for 0% of the time, Pallas kernels for 26%

profile of v6, /device:TPU:0, one launch (start us, length us, event | category | flops | bytes accessed | tf_op | source)
XLA Modules:
  0.0 37.6 jit_solution(14534485807363477090)
XLA Ops:
  0.6 0.0 copy-start.4
  0.6 3.0 %collective-permute-start.5 = (bf16[512,512]{1,0:T(8,128)(2,1)}, bf16[512,512]{1,0:T(8,128)(2,1)S(1)}, u32[]{:S(2)}, u32[]{:S(2)}) collective-permute-start(bf16[512,512]{1,0:T(8,128)(2,1)} %refs_0_.3), channel_id=1, source_target_pairs={{0,2},{1,3},{2,0},{3,1},{4,6},{5,7},{6,4},{7,5},{8,10},{9,11},{10,... | collective-permute-start | bytes 1572872 | tf_op jit(solution)/shard_map/ppermute | solution.py:548
  3.6 2.2 %open.1 = (f32[72,128]{1,0:T(8,128)}, bf16[512,128]{1,0:T(8,128)(2,1)}, bf16[512,128]{1,0:T(8,128)(2,1)}, f32[16,1024]{1,0:T(8,128)}, f32[4,1024]{1,0:T(4,128)}) custom-call(s32[4,4]{1,0:T(4,128)} %refs_0_.2, s32[4,4]{1,0:T(4,128)} %refs_1_.1, bf16[512,512]{1,0:T(8,128)(2,1)} %refs_2_.1, bf16[3,512]{1,0:T(4,128)(2,1)} %dip.1, s32[3,1024]{1,0:T(4,128)} %owner.1, ...), custom_call_target="tpu_custom_call" | custom-call | flops 1000000 | bytes 12000000 | tf_op jit(solution)/shard_map/open/pallas_call | solution.py:500
  5.8 1.6 %collective-permute-start = (f32[72,128]{1,0:T(8,128)}, f32[72,128]{1,0:T(8,128)S(1)}, u32[]{:S(2)}, u32[]{:S(2)}) collective-permute-start(f32[72,128]{1,0:T(8,128)} %get-tuple-element.22.message), channel_id=1, source_target_pairs={{0,4},{4,0},{8,12},{12,8},{1,5},{5,1},{9,13},{13,9},{2,6},{6,2},{1... | collective-permute-start | bytes 110600 | tf_op jit(solution)/shard_map/ppermute | solution.py:548
  7.5 0.0 copy-start
  7.5 0.8 %copy-done = f32[16,1024]{1,0:T(8,128)S(1)} copy-done((f32[16,1024]{1,0:T(8,128)S(1)}, f32[16,1024]{1,0:T(8,128)}, u32[]{:S(2)}) %copy-start) | copy-done | bytes 65560
  8.3 0.0 copy-start.9
  8.3 0.8 %copy-done.9 = f32[72,128]{1,0:T(8,128)S(1)} copy-done((f32[72,128]{1,0:T(8,128)S(1)}, f32[72,128]{1,0:T(8,128)}, u32[]{:S(2)}) %copy-start.9) | copy-done | bytes 36888
  9.1 0.0 copy-start.10
  9.1 0.7 %copy-done.10 = bf16[3,512]{1,0:T(4,128)(2,1)S(1)} copy-done((bf16[3,512]{1,0:T(4,128)(2,1)S(1)}, bf16[3,512]{1,0:T(4,128)(2,1)}, u32[]{:S(2)}) %copy-start.10) | copy-done | bytes 3096
  9.8 0.0 copy-start.6
  9.8 0.0 copy-start.1
  9.8 0.1 prepare.1
  9.8 0.2 collective-permute-done.second
  10.1 2.6 %collective-permute-start.1 = (f32[128,128]{1,0:T(8,128)S(1)}, f32[128,128]{1,0:T(8,128)S(1)}, u32[]{:S(2)}, u32[]{:S(2)}) collective-permute-start(f32[128,128]{1,0:T(8,128)S(1)} %merge.5.first.second), channel_id=1, source_target_pairs={{0,8},{4,12},{8,0},{12,4},{1,9},{5,13},{9,1},{13,5},{2,10},{6,14},... | collective-permute-start | bytes 196616 | tf_op jit(solution)/shard_map/ppermute | solution.py:548
  12.7 0.0 collective-permute-start.4
  12.7 0.0 copy-start.3
  12.7 0.9 %copy-done.3 = s32[32,1024]{1,0:T(8,128)S(1)} copy-done((s32[32,1024]{1,0:T(8,128)S(1)}, s32[32,1024]{1,0:T(8,128)}, u32[]{:S(2)}) %copy-start.3) | copy-done | bytes 131096
  13.6 1.9 %own_gathers.1.done.own_words = s32[160,1024]{1,0:T(8,128)S(1)} custom-call(s32[5,8,8,128]{3,2,1,0:T(8,128)S(1)} %get-tuple-element.25.table.own_table, s32[32,1024]{1,0:T(8,128)S(1)} %copy-done.3), custom_call_target="tpu_custom_call" | custom-call | flops 1000000 | bytes 6000000 | tf_op jit(solution)/shard_map/own_gathers/pallas_call | solution.py:500
  15.5 0.0 copy-start.2
  15.5 0.0 collective-permute-done.1.second
  15.5 0.3 collective-permute-done.5.first
  15.8 0.0 copy-start.5
  15.8 0.3 collective-permute-start.6
  16.1 0.0 copy-done.6
  16.1 2.6 %collective-permute-start.7 = (bf16[512,128]{1,0:T(8,128)(2,1)S(1)}, bf16[512,128]{1,0:T(8,128)(2,1)S(1)}, u32[]{:S(2)}, u32[]{:S(2)}) collective-permute-start(bf16[512,128]{1,0:T(8,128)(2,1)S(1)} %tie.4), channel_id=1, source_target_pairs={{0,8},{4,12},{8,0},{12,4},{1,9},{5,13},{9,1},{13,5},{2,10},{6,14},... | collective-permute-start | bytes 393224 | tf_op jit(solution)/shard_map/ppermute | solution.py:548
  18.7 0.2 collective-permute-start.2
  18.9 1.1 %collective-permute-done.2.second = f32[96,128]{1,0:T(8,128)S(1)} collective-permute-done((f32[96,128]{1,0:T(8,128)S(1)}, f32[96,128]{1,0:T(8,128)S(1)}, u32[]{:S(2)}, u32[]{:S(2)}) %collective-permute-start.2) | collective-permute-done | bytes 49184 | tf_op jit(solution)/shard_map/ppermute | solution.py:548
  19.9 1.6 %collective-permute-start.3 = (f32[112,128]{1,0:T(8,128)S(1)}, f32[112,128]{1,0:T(8,128)S(1)}, u32[]{:S(2)}, u32[]{:S(2)}) collective-permute-start(f32[112,128]{1,0:T(8,128)S(1)} %merge.6.first), channel_id=1, source_target_pairs={{0,2},{1,3},{2,0},{3,1},{4,6},{5,7},{6,4},{7,5},{8,10},{9,11},{10,... | collective-permute-start | bytes 172040 | tf_op jit(solution)/shard_map/ppermute | solution.py:548
  21.5 0.0 copy-done.4
  21.5 0.0 copy-done.1
  21.5 2.7 %pair_forces.1.refs_4_.pair = f32[9,1024]{1,0:T(8,128)S(1)} custom-call(f32[16,1024]{1,0:T(8,128)S(1)} %copy-done.1, s32[160,1024]{1,0:T(8,128)S(1)} %own_gathers.1.done.own_words, s32[5,8,8,128]{3,2,1,0:T(8,128)S(1)} %get-tuple-element.25.table.own_table, f32[160,128]{1,0:T(8,128)S(1)} %get-tuple-element.27.halos, s32[32,1024]{1,0:T(8,128)S(1)} %copy-done.4), custom_call_target="tpu_custom_call" | custom-call | flops 1000000 | bytes 15000000 | tf_op jit(solution)/shard_map/pair_forces/pallas_call | solution.py:500
  24.2 0.0 collective-permute-done.3.second
  24.2 0.0 collective-permute-done.4.refs_1_
  24.2 0.0 collective-permute-done.6.refs_3_
  24.2 0.0 copy-done.2
  24.3 0.8 %field.1 = (f32[16,128]{1,0:T(8,128)S(1)}, bf16[512,2048]{1,0:T(8,128)(2,1)S(1)}) custom-call(f32[144,128]{1,0:T(8,128)S(1)} %merge.7.message, bf16[512,512]{1,0:T(8,128)(2,1)S(1)} %copy-done.2, bf16[512,512]{1,0:T(8,128)(2,1)S(1)} %collective-permute-done.4.refs_1_, bf16[512,512]{1,0:T(8,128)(2,1)S(1)} %tie.3.refs_2_, ...), custom_call_target="tpu_custom_call" | custom-call | flops 1000000 | bytes 5000000 | tf_op jit(solution)/shard_map/field/pallas_call | solution.py:500
  25.1 0.0 copy-start.7
  25.1 0.0 copy-start.8
  25.1 0.0 copy-start.11
  25.1 0.0 copy-start.12
  25.1 0.0 copy-start.13
  25.1 1.6 %collective-permute-start.8 = (f32[16,128]{1,0:T(8,128)S(1)}, f32[16,128]{1,0:T(8,128)S(1)}, u32[]{:S(2)}, u32[]{:S(2)}) collective-permute-start(f32[16,128]{1,0:T(8,128)S(1)} %get-tuple-element.30.first), channel_id=1, source_target_pairs={{0,4},{4,0},{8,12},{12,8},{1,5},{5,1},{9,13},{13,9},{2,6},{6,2},{1... | collective-permute-start | bytes 24584 | tf_op jit(solution)/shard_map/ppermute | solution.py:548
  26.8 0.0 copy-done.5
  26.8 0.4 %collective-permute-start.10 = (bf16[512,128]{1,0:T(8,128)(2,1)S(1)}, bf16[512,128]{1,0:T(8,128)(2,1)S(1)}, u32[]{:S(2)}, u32[]{:S(2)}) collective-permute-start(bf16[512,128]{1,0:T(8,128)(2,1)S(1)} %copy-done.5), channel_id=1, source_target_pairs={{0,4},{4,0},{8,12},{12,8},{1,5},{5,1},{9,13},{13,9},{2,6},{6,2},{1... | collective-permute-start | bytes 393224 | tf_op jit(solution)/shard_map/ppermute | solution.py:548
  27.2 1.6 %collective-permute-done.8.second = f32[16,128]{1,0:T(8,128)S(1)} collective-permute-done((f32[16,128]{1,0:T(8,128)S(1)}, f32[16,128]{1,0:T(8,128)S(1)}, u32[]{:S(2)}, u32[]{:S(2)}) %collective-permute-start.8) | collective-permute-done | bytes 8224 | tf_op jit(solution)/shard_map/ppermute | solution.py:548
  28.9 0.0 collective-permute-done.7.first
  28.9 1.6 %collective-permute-start.9 = (bf16[512,128]{1,0:T(8,128)(2,1)S(1)}, bf16[512,128]{1,0:T(8,128)(2,1)S(1)}, u32[]{:S(2)}, u32[]{:S(2)}) collective-permute-start(bf16[512,128]{1,0:T(8,128)(2,1)S(1)} %tie.5.refs_2_), channel_id=1, source_target_pairs={{0,4},{4,0},{8,12},{12,8},{1,5},{5,1},{9,13},{13,9},{2,6},{6,2},{1... | collective-permute-start | bytes 393224 | tf_op jit(solution)/shard_map/ppermute | solution.py:548
  30.5 0.7 %collective-permute-start.11 = (f32[32,128]{1,0:T(8,128)S(1)}, f32[32,128]{1,0:T(8,128)S(1)}, u32[]{:S(2)}, u32[]{:S(2)}) collective-permute-start(f32[32,128]{1,0:T(8,128)S(1)} %merge.8.second.first), channel_id=1, source_target_pairs={{0,8},{4,12},{8,0},{12,4},{1,9},{5,13},{9,1},{13,5},{2,10},{6,14},... | collective-permute-start | bytes 49160 | tf_op jit(solution)/shard_map/ppermute | solution.py:548
  31.2 2.2 %collective-permute-done.10.refs_1_ = bf16[512,128]{1,0:T(8,128)(2,1)S(1)} collective-permute-done((bf16[512,128]{1,0:T(8,128)(2,1)S(1)}, bf16[512,128]{1,0:T(8,128)(2,1)S(1)}, u32[]{:S(2)}, u32[]{:S(2)}) %collective-permute-start.10) | collective-permute-done | bytes 131104 | tf_op jit(solution)/shard_map/ppermute | solution.py:548
  33.4 1.1 %product.2.refs_1_ = f32[512,512]{1,0:T(8,128)S(1)} custom-call(f32[144,128]{1,0:T(8,128)S(1)} %merge.7.message, bf16[512,2048]{1,0:T(8,128)(2,1)S(1)} %get-tuple-element.28.dens, bf16[512,128]{1,0:T(8,128)(2,1)S(1)} %copy-done.5, bf16[512,128]{1,0:T(8,128)(2,1)S(1)} %collective-permute-done.10.refs_1_, bf16[512,128]{1,0:T(8,128)(2,1)S(1)} %tie.5.refs_2_), custom_call_target="tpu_custom_call" | custom-call | flops 1000000 | bytes 10000000 | tf_op jit(solution)/shard_map/product/pallas_call | solution.py:500
  34.5 0.7 %collective-permute-done.11.second = f32[32,128]{1,0:T(8,128)S(1)} collective-permute-done((f32[32,128]{1,0:T(8,128)S(1)}, f32[32,128]{1,0:T(8,128)S(1)}, u32[]{:S(2)}, u32[]{:S(2)}) %collective-permute-start.11) | collective-permute-done | bytes 16416 | tf_op jit(solution)/shard_map/ppermute | solution.py:548
  35.2 0.0 copy-done.7
  35.2 0.0 copy-done.8
  35.2 0.0 copy-done.11
  35.2 0.0 copy-done.12
  35.2 0.0 copy-done.13
  35.2 1.1 %advance.1 = (f32[3,1024]{1,0:T(4,128)}, f32[3,1024]{1,0:T(4,128)}, f32[3,1024]{1,0:T(4,128)}, f32[4,1024]{1,0:T(4,128)}) custom-call(f32[64,128]{1,0:T(8,128)S(1)} %merge.9.fields, s32[3,1024]{1,0:T(4,128)S(1)} %copy-done.7, f32[16,1024]{1,0:T(8,128)S(1)} %copy-done.1, f32[4,1024]{1,0:T(4,128)S(1)} %copy-done.13, f32[9,1024]{1,0:T(8,128)S(1)} %pair_forces.1.refs_4_.pair, ...), custom_call_target="tpu_custom_call" | custom-call | flops 1000000 | bytes 6000000 | tf_op jit(solution)/shard_map/advance/pallas_call | solution.py:500
  36.3 0.0 collective-permute-done.9.refs_0_
  36.3 1.3 %product.3 = bf16[512,512]{1,0:T(8,128)(2,1)} custom-call(f32[144,128]{1,0:T(8,128)S(1)} %merge.7.message, bf16[512,2048]{1,0:T(8,128)(2,1)S(1)} %get-tuple-element.28.dens, bf16[512,128]{1,0:T(8,128)(2,1)S(1)} %collective-permute-done.9.refs_0_, f32[512,512]{1,0:T(8,128)S(1)} %product.2.refs_1_), custom_call_target="tpu_custom_call" | custom-call | flops 1000000 | bytes 10000000 | tf_op jit(solution)/shard_map/product/pallas_call | solution.py:500
  (9 shorter events, 0.0 us)
Async XLA Ops:
  0.6 20.9 %copy-start.4 = (s32[32,1024]{1,0:T(8,128)S(1)}, s32[32,1024]{1,0:T(8,128)}, u32[]{:S(2)}) copy-start(s32[32,1024]{1,0:T(8,128)} %neighbours.3) | copy-start | bytes 393220
  0.6 15.1 %collective-permute-start.5 = (bf16[512,512]{1,0:T(8,128)(2,1)}, bf16[512,512]{1,0:T(8,128)(2,1)S(1)}, u32[]{:S(2)}, u32[]{:S(2)}) collective-permute-start(bf16[512,512]{1,0:T(8,128)(2,1)} %refs_0_.3), channel_id=1, source_target_pairs={{0,2},{1,3},{2,0},{3,1},{4,6},{5,7},{6,4},{7,5},{8,10},{9,11},{10,... | collective-permute-start | bytes 1572872 | tf_op jit(solution)/shard_map/ppermute | solution.py:548
  5.8 4.2 %collective-permute-start = (f32[72,128]{1,0:T(8,128)}, f32[72,128]{1,0:T(8,128)S(1)}, u32[]{:S(2)}, u32[]{:S(2)}) collective-permute-start(f32[72,128]{1,0:T(8,128)} %get-tuple-element.22.message), channel_id=1, source_target_pairs={{0,4},{4,0},{8,12},{12,8},{1,5},{5,1},{9,13},{13,9},{2,6},{6,2},{1... | collective-permute-start | bytes 110600 | tf_op jit(solution)/shard_map/ppermute | solution.py:548
  7.5 0.8 %copy-start = (f32[16,1024]{1,0:T(8,128)S(1)}, f32[16,1024]{1,0:T(8,128)}, u32[]{:S(2)}) copy-start(f32[16,1024]{1,0:T(8,128)} %get-tuple-element.21.sites) | copy-start | bytes 196612
  8.3 0.8 %copy-start.9 = (f32[72,128]{1,0:T(8,128)S(1)}, f32[72,128]{1,0:T(8,128)}, u32[]{:S(2)}) copy-start(f32[72,128]{1,0:T(8,128)} %get-tuple-element.22.message) | copy-start | bytes 110596
  9.1 0.7 %copy-start.10 = (bf16[3,512]{1,0:T(4,128)(2,1)S(1)}, bf16[3,512]{1,0:T(4,128)(2,1)}, u32[]{:S(2)}) copy-start(bf16[3,512]{1,0:T(4,128)(2,1)} %dip.1) | copy-start | bytes 9220
  9.8 6.3 %copy-start.6 = (bf16[512,128]{1,0:T(8,128)(2,1)S(1)}, bf16[512,128]{1,0:T(8,128)(2,1)}, u32[]{:S(2)}) copy-start(bf16[512,128]{1,0:T(8,128)(2,1)} %get-tuple-element.29.first) | copy-start | bytes 393220
  9.8 11.7 %copy-start.1 = (f32[16,1024]{1,0:T(8,128)S(1)}, f32[16,1024]{1,0:T(8,128)}, u32[]{:S(2)}) copy-start(f32[16,1024]{1,0:T(8,128)} %get-tuple-element.21.sites) | copy-start | bytes 196612
  10.1 5.4 %collective-permute-start.1 = (f32[128,128]{1,0:T(8,128)S(1)}, f32[128,128]{1,0:T(8,128)S(1)}, u32[]{:S(2)}, u32[]{:S(2)}) collective-permute-start(f32[128,128]{1,0:T(8,128)S(1)} %merge.5.first.second), channel_id=1, source_target_pairs={{0,8},{4,12},{8,0},{12,4},{1,9},{5,13},{9,1},{13,5},{2,10},{6,14},... | collective-permute-start | bytes 196616 | tf_op jit(solution)/shard_map/ppermute | solution.py:548
  12.7 11.6 %collective-permute-start.4 = (bf16[512,512]{1,0:T(8,128)(2,1)}, bf16[512,512]{1,0:T(8,128)(2,1)S(1)}, u32[]{:S(2)}, u32[]{:S(2)}) collective-permute-start(bf16[512,512]{1,0:T(8,128)(2,1)} %refs_0_.3), channel_id=1, source_target_pairs={{0,1},{1,0},{2,3},{3,2},{4,5},{5,4},{6,7},{7,6},{8,9},{9,8},{10,11... | collective-permute-start | bytes 1572872 | tf_op jit(solution)/shard_map/ppermute | solution.py:548
  12.7 0.9 %copy-start.3 = (s32[32,1024]{1,0:T(8,128)S(1)}, s32[32,1024]{1,0:T(8,128)}, u32[]{:S(2)}) copy-start(s32[32,1024]{1,0:T(8,128)} %neighbours.3) | copy-start | bytes 393220
  15.5 8.8 %copy-start.2 = (bf16[512,512]{1,0:T(8,128)(2,1)S(1)}, bf16[512,512]{1,0:T(8,128)(2,1)}, u32[]{:S(2)}) copy-start(bf16[512,512]{1,0:T(8,128)(2,1)} %refs_0_.3) | copy-start | bytes 1572868
  15.8 11.0 %copy-start.5 = (bf16[512,128]{1,0:T(8,128)(2,1)S(1)}, bf16[512,128]{1,0:T(8,128)(2,1)}, u32[]{:S(2)}) copy-start(bf16[512,128]{1,0:T(8,128)(2,1)} %get-tuple-element.31.refs_0_) | copy-start | bytes 393220
  15.8 8.4 %collective-permute-start.6 = (bf16[512,512]{1,0:T(8,128)(2,1)S(1)}, bf16[512,512]{1,0:T(8,128)(2,1)S(1)}, u32[]{:S(2)}, u32[]{:S(2)}) collective-permute-start(bf16[512,512]{1,0:T(8,128)(2,1)S(1)} %tie.3.refs_2_), channel_id=1, source_target_pairs={{0,1},{1,0},{2,3},{3,2},{4,5},{5,4},{6,7},{7,6},{8,9},{9,8},{10,11... | collective-permute-start | bytes 1572872 | tf_op jit(solution)/shard_map/ppermute | solution.py:548
  16.1 12.8 %collective-permute-start.7 = (bf16[512,128]{1,0:T(8,128)(2,1)S(1)}, bf16[512,128]{1,0:T(8,128)(2,1)S(1)}, u32[]{:S(2)}, u32[]{:S(2)}) collective-permute-start(bf16[512,128]{1,0:T(8,128)(2,1)S(1)} %tie.4), channel_id=1, source_target_pairs={{0,8},{4,12},{8,0},{12,4},{1,9},{5,13},{9,1},{13,5},{2,10},{6,14},... | collective-permute-start | bytes 393224 | tf_op jit(solution)/shard_map/ppermute | solution.py:548
  18.7 1.2 %collective-permute-start.2 = (f32[96,128]{1,0:T(8,128)S(1)}, f32[96,128]{1,0:T(8,128)S(1)}, u32[]{:S(2)}, u32[]{:S(2)}) collective-permute-start(f32[96,128]{1,0:T(8,128)S(1)} %get-tuple-element.26.first.second), channel_id=1, source_target_pairs={{0,1},{1,0},{2,3},{3,2},{4,5},{5,4},{6,7},{7,6},{8,9},{9,8},{10,11... | collective-permute-start | bytes 147464 | tf_op jit(solution)/shard_map/ppermute | solution.py:548
  19.9 4.2 %collective-permute-start.3 = (f32[112,128]{1,0:T(8,128)S(1)}, f32[112,128]{1,0:T(8,128)S(1)}, u32[]{:S(2)}, u32[]{:S(2)}) collective-permute-start(f32[112,128]{1,0:T(8,128)S(1)} %merge.6.first), channel_id=1, source_target_pairs={{0,2},{1,3},{2,0},{3,1},{4,6},{5,7},{6,4},{7,5},{8,10},{9,11},{10,... | collective-permute-start | bytes 172040 | tf_op jit(solution)/shard_map/ppermute | solution.py:548
  25.1 10.1 %copy-start.7 = (s32[3,1024]{1,0:T(4,128)S(1)}, s32[3,1024]{1,0:T(4,128)}, u32[]{:S(2)}) copy-start(s32[3,1024]{1,0:T(4,128)} %owner.1) | copy-start | bytes 36868
  25.1 10.1 %copy-start.8 = (f32[3,1024]{1,0:T(4,128)S(1)}, f32[3,1024]{1,0:T(4,128)}, u32[]{:S(2)}) copy-start(f32[3,1024]{1,0:T(4,128)} %centres.1) | copy-start | bytes 36868
  25.1 10.1 %copy-start.11 = (f32[3,1024]{1,0:T(4,128)S(1)}, f32[3,1024]{1,0:T(4,128)}, u32[]{:S(2)}) copy-start(f32[3,1024]{1,0:T(4,128)} %velocity.1) | copy-start | bytes 36868
  25.1 10.1 %copy-start.12 = (f32[3,1024]{1,0:T(4,128)S(1)}, f32[3,1024]{1,0:T(4,128)}, u32[]{:S(2)}) copy-start(f32[3,1024]{1,0:T(4,128)} %angmom.1) | copy-start | bytes 36868
  25.1 10.1 %copy-start.13 = (f32[4,1024]{1,0:T(4,128)S(1)}, f32[4,1024]{1,0:T(4,128)}, u32[]{:S(2)}) copy-start(f32[4,1024]{1,0:T(4,128)} %get-tuple-element.32.quat) | copy-start | bytes 49156
  25.1 3.7 %collective-permute-start.8 = (f32[16,128]{1,0:T(8,128)S(1)}, f32[16,128]{1,0:T(8,128)S(1)}, u32[]{:S(2)}, u32[]{:S(2)}) collective-permute-start(f32[16,128]{1,0:T(8,128)S(1)} %get-tuple-element.30.first), channel_id=1, source_target_pairs={{0,4},{4,0},{8,12},{12,8},{1,5},{5,1},{9,13},{13,9},{2,6},{6,2},{1... | collective-permute-start | bytes 24584 | tf_op jit(solution)/shard_map/ppermute | solution.py:548
  26.8 6.6 %collective-permute-start.10 = (bf16[512,128]{1,0:T(8,128)(2,1)S(1)}, bf16[512,128]{1,0:T(8,128)(2,1)S(1)}, u32[]{:S(2)}, u32[]{:S(2)}) collective-permute-start(bf16[512,128]{1,0:T(8,128)(2,1)S(1)} %copy-done.5), channel_id=1, source_target_pairs={{0,4},{4,0},{8,12},{12,8},{1,5},{5,1},{9,13},{13,9},{2,6},{6,2},{1... | collective-permute-start | bytes 393224 | tf_op jit(solution)/shard_map/ppermute | solution.py:548
  28.9 7.4 %collective-permute-start.9 = (bf16[512,128]{1,0:T(8,128)(2,1)S(1)}, bf16[512,128]{1,0:T(8,128)(2,1)S(1)}, u32[]{:S(2)}, u32[]{:S(2)}) collective-permute-start(bf16[512,128]{1,0:T(8,128)(2,1)S(1)} %tie.5.refs_2_), channel_id=1, source_target_pairs={{0,4},{4,0},{8,12},{12,8},{1,5},{5,1},{9,13},{13,9},{2,6},{6,2},{1... | collective-permute-start | bytes 393224 | tf_op jit(solution)/shard_map/ppermute | solution.py:548
  30.5 4.6 %collective-permute-start.11 = (f32[32,128]{1,0:T(8,128)S(1)}, f32[32,128]{1,0:T(8,128)S(1)}, u32[]{:S(2)}, u32[]{:S(2)}) collective-permute-start(f32[32,128]{1,0:T(8,128)S(1)} %merge.8.second.first), channel_id=1, source_target_pairs={{0,8},{4,12},{8,0},{12,4},{1,9},{5,13},{9,1},{13,5},{2,10},{6,14},... | collective-permute-start | bytes 49160 | tf_op jit(solution)/shard_map/ppermute | solution.py:548

commit v7 on v6

--- a/solution.py
+++ b/solution.py
@@ -636,9 +636,10 @@
     )
     for step in steps[1:]:
         small_all[step] = swap(later, "row", rows_n, step)
-    dens_all = relay(dens_all, across, ways, message)
     for step in doublings(ways):
         message = merge(message, swap(message, across, ways, step), summed)
+        if step == 1:
+            dens_all = relay(dens_all, across, ways, message)
     (pair,) = call(
         functools.partial(pair_kernel, rows_n, first),
         "pair_forces",

time: 37.9 us -> 37.8 us (level)
  starting transfers between devices: 16.3 us -> 15.6 us
  waiting for transfers between devices: 6.06 us -> 6.6 us
    ppermute x12, starting transfers between devices: 16.3 us -> 15.6 us  [swap(): return lax.ppermute(value, axis, [(i, i ^ step) for i in range(count)])]
    ppermute x12, waiting for transfers between devices: 6.06 us -> 6.6 us  [swap(): return lax.ppermute(value, axis, [(i, i ^ step) for i in range(count)])]
where the time goes in v7:
time: 37.8 us; the launch traced here: 37.5 us
  starting transfers between devices  15.6 us (41%)
  Pallas kernels  11.2 us (30%)
  waiting for transfers between devices  6.6 us (17%)
  local copies, waits for them, and re-layouts  3.26 us (9%)
  between operations  0.83 us (2%)
    ppermute x12, starting transfers between devices, swap(): return lax.ppermute(value, axis, [(i, i ^ step) for i in range(count)])  15.6 us
    pallas_call x17, Pallas kernels, call(): pl.pallas_call(kernel, out_shape=[jax.ShapeDtypeStruct(shape, dtype) for...  11.2 us
    ppermute x12, waiting for transfers between devices, swap(): return lax.ppermute(value, axis, [(i, i ^ step) for i in range(count)])  6.6 us
    unnamed x28, local copies, waits for them, and re-layouts  3.26 us
  transfers between devices with their start and end apart: 12, of which 6 were waited for; matrix products, arithmetic and copies ran while one was open for 0% of the time, Pallas kernels for 26%

profile of v7, /device:TPU:0, one launch (start us, length us, event | category | flops | bytes accessed | tf_op | source)
XLA Modules:
  0.0 37.5 jit_solution(4684525972489528681)
XLA Ops:
  0.6 0.0 copy-start.2
  0.6 3.0 %collective-permute-start.5 = (bf16[512,512]{1,0:T(8,128)(2,1)}, bf16[512,512]{1,0:T(8,128)(2,1)S(1)}, u32[]{:S(2)}, u32[]{:S(2)}) collective-permute-start(bf16[512,512]{1,0:T(8,128)(2,1)} %refs_0_.3), channel_id=1, source_target_pairs={{0,2},{1,3},{2,0},{3,1},{4,6},{5,7},{6,4},{7,5},{8,10},{9,11},{10,... | collective-permute-start | bytes 1572872 | tf_op jit(solution)/shard_map/ppermute | solution.py:548
  3.6 2.2 %open.1 = (f32[72,128]{1,0:T(8,128)}, bf16[512,128]{1,0:T(8,128)(2,1)}, bf16[512,128]{1,0:T(8,128)(2,1)}, f32[16,1024]{1,0:T(8,128)}, f32[4,1024]{1,0:T(4,128)}) custom-call(s32[4,4]{1,0:T(4,128)} %refs_0_.2, s32[4,4]{1,0:T(4,128)} %refs_1_.1, bf16[512,512]{1,0:T(8,128)(2,1)} %refs_2_.1, bf16[3,512]{1,0:T(4,128)(2,1)} %dip.1, s32[3,1024]{1,0:T(4,128)} %owner.1, ...), custom_call_target="tpu_custom_call" | custom-call | flops 1000000 | bytes 12000000 | tf_op jit(solution)/shard_map/open/pallas_call | solution.py:500
  5.8 1.6 %collective-permute-start = (f32[72,128]{1,0:T(8,128)}, f32[72,128]{1,0:T(8,128)S(1)}, u32[]{:S(2)}, u32[]{:S(2)}) collective-permute-start(f32[72,128]{1,0:T(8,128)} %get-tuple-element.22.message), channel_id=1, source_target_pairs={{0,4},{4,0},{8,12},{12,8},{1,5},{5,1},{9,13},{13,9},{2,6},{6,2},{1... | collective-permute-start | bytes 110600 | tf_op jit(solution)/shard_map/ppermute | solution.py:548
  7.5 0.0 copy-start
  7.5 0.8 %copy-done = f32[16,1024]{1,0:T(8,128)S(1)} copy-done((f32[16,1024]{1,0:T(8,128)S(1)}, f32[16,1024]{1,0:T(8,128)}, u32[]{:S(2)}) %copy-start) | copy-done | bytes 65560
  8.3 0.0 copy-start.9
  8.3 0.8 %copy-done.9 = f32[72,128]{1,0:T(8,128)S(1)} copy-done((f32[72,128]{1,0:T(8,128)S(1)}, f32[72,128]{1,0:T(8,128)}, u32[]{:S(2)}) %copy-start.9) | copy-done | bytes 36888
  9.1 0.0 copy-start.10
  9.1 0.7 %copy-done.10 = bf16[3,512]{1,0:T(4,128)(2,1)S(1)} copy-done((bf16[3,512]{1,0:T(4,128)(2,1)S(1)}, bf16[3,512]{1,0:T(4,128)(2,1)}, u32[]{:S(2)}) %copy-start.10) | copy-done | bytes 3096
  9.8 0.0 copy-start.1
  9.8 0.0 copy-start.4
  9.8 0.1 prepare.1
  9.8 0.2 collective-permute-done.second
  10.1 2.6 %collective-permute-start.1 = (f32[128,128]{1,0:T(8,128)S(1)}, f32[128,128]{1,0:T(8,128)S(1)}, u32[]{:S(2)}, u32[]{:S(2)}) collective-permute-start(f32[128,128]{1,0:T(8,128)S(1)} %merge.5.first.second), channel_id=1, source_target_pairs={{0,8},{4,12},{8,0},{12,4},{1,9},{5,13},{9,1},{13,5},{2,10},{6,14},... | collective-permute-start | bytes 196616 | tf_op jit(solution)/shard_map/ppermute | solution.py:548
  12.7 0.0 copy-start.3
  12.7 0.9 %copy-done.3 = s32[32,1024]{1,0:T(8,128)S(1)} copy-done((s32[32,1024]{1,0:T(8,128)S(1)}, s32[32,1024]{1,0:T(8,128)}, u32[]{:S(2)}) %copy-start.3) | copy-done | bytes 131096
  13.6 0.0 copy-start.6
  13.6 1.9 %own_gathers.1.done.own_words = s32[160,1024]{1,0:T(8,128)S(1)} custom-call(s32[5,8,8,128]{3,2,1,0:T(8,128)S(1)} %get-tuple-element.25.table.own_table, s32[32,1024]{1,0:T(8,128)S(1)} %copy-done.3), custom_call_target="tpu_custom_call" | custom-call | flops 1000000 | bytes 6000000 | tf_op jit(solution)/shard_map/own_gathers/pallas_call | solution.py:500
  15.5 0.0 collective-permute-done.1.second
  15.5 0.1 collective-permute-start.2
  15.6 0.0 copy-done.2
  15.6 0.5 %collective-permute-start.4 = (bf16[512,512]{1,0:T(8,128)(2,1)S(1)}, bf16[512,512]{1,0:T(8,128)(2,1)S(1)}, u32[]{:S(2)}, u32[]{:S(2)}) collective-permute-start(bf16[512,512]{1,0:T(8,128)(2,1)S(1)} %copy-done.2), channel_id=1, source_target_pairs={{0,1},{1,0},{2,3},{3,2},{4,5},{5,4},{6,7},{7,6},{8,9},{9,8},{10,11... | collective-permute-start | bytes 1572872 | tf_op jit(solution)/shard_map/ppermute | solution.py:548
  16.1 0.7 %collective-permute-done.2.second = f32[96,128]{1,0:T(8,128)S(1)} collective-permute-done((f32[96,128]{1,0:T(8,128)S(1)}, f32[96,128]{1,0:T(8,128)S(1)}, u32[]{:S(2)}, u32[]{:S(2)}) %collective-permute-start.2) | collective-permute-done | bytes 49184 | tf_op jit(solution)/shard_map/ppermute | solution.py:548
  16.8 0.0 collective-permute-done.5.first
  16.8 0.0 copy-start.5
  16.8 0.2 collective-permute-start.6
  17.0 0.0 copy-done.6
  17.0 2.4 %collective-permute-start.7 = (bf16[512,128]{1,0:T(8,128)(2,1)S(1)}, bf16[512,128]{1,0:T(8,128)(2,1)S(1)}, u32[]{:S(2)}, u32[]{:S(2)}) collective-permute-start(bf16[512,128]{1,0:T(8,128)(2,1)S(1)} %tie.4), channel_id=1, source_target_pairs={{0,8},{4,12},{8,0},{12,4},{1,9},{5,13},{9,1},{13,5},{2,10},{6,14},... | collective-permute-start | bytes 393224 | tf_op jit(solution)/shard_map/ppermute | solution.py:548
  19.5 0.7 %collective-permute-start.3 = (f32[112,128]{1,0:T(8,128)S(1)}, f32[112,128]{1,0:T(8,128)S(1)}, u32[]{:S(2)}, u32[]{:S(2)}) collective-permute-start(f32[112,128]{1,0:T(8,128)S(1)} %merge.6.first.second), channel_id=1, source_target_pairs={{0,2},{1,3},{2,0},{3,1},{4,6},{5,7},{6,4},{7,5},{8,10},{9,11},{10,... | collective-permute-start | bytes 172040 | tf_op jit(solution)/shard_map/ppermute | solution.py:548
  20.2 0.0 copy-done.1
  20.2 0.0 copy-done.4
  20.2 2.7 %pair_forces.1.refs_4_.pair = f32[9,1024]{1,0:T(8,128)S(1)} custom-call(f32[16,1024]{1,0:T(8,128)S(1)} %copy-done.1, s32[160,1024]{1,0:T(8,128)S(1)} %own_gathers.1.done.own_words, s32[5,8,8,128]{3,2,1,0:T(8,128)S(1)} %get-tuple-element.25.table.own_table, f32[160,128]{1,0:T(8,128)S(1)} %get-tuple-element.27.halos, s32[32,1024]{1,0:T(8,128)S(1)} %copy-done.4), custom_call_target="tpu_custom_call" | custom-call | flops 1000000 | bytes 15000000 | tf_op jit(solution)/shard_map/pair_forces/pallas_call | solution.py:500
  22.9 0.7 %collective-permute-done.3.second = f32[112,128]{1,0:T(8,128)S(1)} collective-permute-done((f32[112,128]{1,0:T(8,128)S(1)}, f32[112,128]{1,0:T(8,128)S(1)}, u32[]{:S(2)}, u32[]{:S(2)}) %collective-permute-start.3) | collective-permute-done | bytes 57376 | tf_op jit(solution)/shard_map/ppermute | solution.py:548
  23.7 0.0 collective-permute-done.4.refs_1_
  23.7 0.0 collective-permute-done.6.refs_3_
  23.7 0.8 %field.1 = (f32[16,128]{1,0:T(8,128)S(1)}, bf16[512,2048]{1,0:T(8,128)(2,1)S(1)}) custom-call(f32[144,128]{1,0:T(8,128)S(1)} %merge.7.message, bf16[512,512]{1,0:T(8,128)(2,1)S(1)} %copy-done.2, bf16[512,512]{1,0:T(8,128)(2,1)S(1)} %collective-permute-done.4.refs_1_, bf16[512,512]{1,0:T(8,128)(2,1)S(1)} %tie.3.refs_2_, ...), custom_call_target="tpu_custom_call" | custom-call | flops 1000000 | bytes 5000000 | tf_op jit(solution)/shard_map/field/pallas_call | solution.py:500
  24.5 0.0 copy-start.7
  24.5 0.0 copy-start.8
  24.5 0.0 copy-start.11
  24.5 0.0 copy-start.12
  24.5 0.0 copy-start.13
  24.6 2.2 %collective-permute-start.8 = (f32[16,128]{1,0:T(8,128)S(1)}, f32[16,128]{1,0:T(8,128)S(1)}, u32[]{:S(2)}, u32[]{:S(2)}) collective-permute-start(f32[16,128]{1,0:T(8,128)S(1)} %get-tuple-element.30.first), channel_id=1, source_target_pairs={{0,4},{4,0},{8,12},{12,8},{1,5},{5,1},{9,13},{13,9},{2,6},{6,2},{1... | collective-permute-start | bytes 24584 | tf_op jit(solution)/shard_map/ppermute | solution.py:548
  26.7 0.0 copy-done.5
  26.7 0.1 collective-permute-start.10
  26.8 1.6 %collective-permute-done.8.second = f32[16,128]{1,0:T(8,128)S(1)} collective-permute-done((f32[16,128]{1,0:T(8,128)S(1)}, f32[16,128]{1,0:T(8,128)S(1)}, u32[]{:S(2)}, u32[]{:S(2)}) %collective-permute-start.8) | collective-permute-done | bytes 8224 | tf_op jit(solution)/shard_map/ppermute | solution.py:548
  28.5 0.0 collective-permute-done.7.first
  28.5 1.9 %collective-permute-start.9 = (bf16[512,128]{1,0:T(8,128)(2,1)S(1)}, bf16[512,128]{1,0:T(8,128)(2,1)S(1)}, u32[]{:S(2)}, u32[]{:S(2)}) collective-permute-start(bf16[512,128]{1,0:T(8,128)(2,1)S(1)} %tie.5.refs_2_), channel_id=1, source_target_pairs={{0,4},{4,0},{8,12},{12,8},{1,5},{5,1},{9,13},{13,9},{2,6},{6,2},{1... | collective-permute-start | bytes 393224 | tf_op jit(solution)/shard_map/ppermute | solution.py:548
  30.4 0.3 collective-permute-start.11
  30.7 2.1 %collective-permute-done.10.refs_1_ = bf16[512,128]{1,0:T(8,128)(2,1)S(1)} collective-permute-done((bf16[512,128]{1,0:T(8,128)(2,1)S(1)}, bf16[512,128]{1,0:T(8,128)(2,1)S(1)}, u32[]{:S(2)}, u32[]{:S(2)}) %collective-permute-start.10) | collective-permute-done | bytes 131104 | tf_op jit(solution)/shard_map/ppermute | solution.py:548
  32.7 1.1 %product.2.refs_1_ = f32[512,512]{1,0:T(8,128)S(1)} custom-call(f32[144,128]{1,0:T(8,128)S(1)} %merge.7.message, bf16[512,2048]{1,0:T(8,128)(2,1)S(1)} %get-tuple-element.28.dens, bf16[512,128]{1,0:T(8,128)(2,1)S(1)} %copy-done.5, bf16[512,128]{1,0:T(8,128)(2,1)S(1)} %collective-permute-done.10.refs_1_, bf16[512,128]{1,0:T(8,128)(2,1)S(1)} %tie.5.refs_2_), custom_call_target="tpu_custom_call" | custom-call | flops 1000000 | bytes 10000000 | tf_op jit(solution)/shard_map/product/pallas_call | solution.py:500
  33.8 1.2 %collective-permute-done.11.second = f32[32,128]{1,0:T(8,128)S(1)} collective-permute-done((f32[32,128]{1,0:T(8,128)S(1)}, f32[32,128]{1,0:T(8,128)S(1)}, u32[]{:S(2)}, u32[]{:S(2)}) %collective-permute-start.11) | collective-permute-done | bytes 16416 | tf_op jit(solution)/shard_map/ppermute | solution.py:548
  35.0 0.0 copy-done.7
  35.0 0.0 copy-done.8
  35.0 0.0 copy-done.11
  35.1 0.0 copy-done.12
  35.1 0.0 copy-done.13
  35.1 1.1 %advance.1 = (f32[3,1024]{1,0:T(4,128)}, f32[3,1024]{1,0:T(4,128)}, f32[3,1024]{1,0:T(4,128)}, f32[4,1024]{1,0:T(4,128)}) custom-call(f32[64,128]{1,0:T(8,128)S(1)} %merge.9.fields, s32[3,1024]{1,0:T(4,128)S(1)} %copy-done.7, f32[16,1024]{1,0:T(8,128)S(1)} %copy-done.1, f32[4,1024]{1,0:T(4,128)S(1)} %copy-done.13, f32[9,1024]{1,0:T(8,128)S(1)} %pair_forces.1.refs_4_.pair, ...), custom_call_target="tpu_custom_call" | custom-call | flops 1000000 | bytes 6000000 | tf_op jit(solution)/shard_map/advance/pallas_call | solution.py:500
  36.1 0.0 collective-permute-done.9.refs_0_
  36.1 1.3 %product.3 = bf16[512,512]{1,0:T(8,128)(2,1)} custom-call(f32[144,128]{1,0:T(8,128)S(1)} %merge.7.message, bf16[512,2048]{1,0:T(8,128)(2,1)S(1)} %get-tuple-element.28.dens, bf16[512,128]{1,0:T(8,128)(2,1)S(1)} %collective-permute-done.9.refs_0_, f32[512,512]{1,0:T(8,128)S(1)} %product.2.refs_1_), custom_call_target="tpu_custom_call" | custom-call | flops 1000000 | bytes 10000000 | tf_op jit(solution)/shard_map/product/pallas_call | solution.py:500
  (9 shorter events, 0.0 us)
Async XLA Ops:
  0.6 14.9 %copy-start.2 = (bf16[512,512]{1,0:T(8,128)(2,1)S(1)}, bf16[512,512]{1,0:T(8,128)(2,1)}, u32[]{:S(2)}) copy-start(bf16[512,512]{1,0:T(8,128)(2,1)} %refs_0_.3) | copy-start | bytes 1572868
  0.6 16.1 %collective-permute-start.5 = (bf16[512,512]{1,0:T(8,128)(2,1)}, bf16[512,512]{1,0:T(8,128)(2,1)S(1)}, u32[]{:S(2)}, u32[]{:S(2)}) collective-permute-start(bf16[512,512]{1,0:T(8,128)(2,1)} %refs_0_.3), channel_id=1, source_target_pairs={{0,2},{1,3},{2,0},{3,1},{4,6},{5,7},{6,4},{7,5},{8,10},{9,11},{10,... | collective-permute-start | bytes 1572872 | tf_op jit(solution)/shard_map/ppermute | solution.py:548
  5.8 4.2 %collective-permute-start = (f32[72,128]{1,0:T(8,128)}, f32[72,128]{1,0:T(8,128)S(1)}, u32[]{:S(2)}, u32[]{:S(2)}) collective-permute-start(f32[72,128]{1,0:T(8,128)} %get-tuple-element.22.message), channel_id=1, source_target_pairs={{0,4},{4,0},{8,12},{12,8},{1,5},{5,1},{9,13},{13,9},{2,6},{6,2},{1... | collective-permute-start | bytes 110600 | tf_op jit(solution)/shard_map/ppermute | solution.py:548
  7.5 0.8 %copy-start = (f32[16,1024]{1,0:T(8,128)S(1)}, f32[16,1024]{1,0:T(8,128)}, u32[]{:S(2)}) copy-start(f32[16,1024]{1,0:T(8,128)} %get-tuple-element.21.sites) | copy-start | bytes 196612
  8.3 0.8 %copy-start.9 = (f32[72,128]{1,0:T(8,128)S(1)}, f32[72,128]{1,0:T(8,128)}, u32[]{:S(2)}) copy-start(f32[72,128]{1,0:T(8,128)} %get-tuple-element.22.message) | copy-start | bytes 110596
  9.1 0.7 %copy-start.10 = (bf16[3,512]{1,0:T(4,128)(2,1)S(1)}, bf16[3,512]{1,0:T(4,128)(2,1)}, u32[]{:S(2)}) copy-start(bf16[3,512]{1,0:T(4,128)(2,1)} %dip.1) | copy-start | bytes 9220
  9.8 10.4 %copy-start.1 = (f32[16,1024]{1,0:T(8,128)S(1)}, f32[16,1024]{1,0:T(8,128)}, u32[]{:S(2)}) copy-start(f32[16,1024]{1,0:T(8,128)} %get-tuple-element.21.sites) | copy-start | bytes 196612
  9.8 10.4 %copy-start.4 = (s32[32,1024]{1,0:T(8,128)S(1)}, s32[32,1024]{1,0:T(8,128)}, u32[]{:S(2)}) copy-start(s32[32,1024]{1,0:T(8,128)} %neighbours.3) | copy-start | bytes 393220
  10.1 5.4 %collective-permute-start.1 = (f32[128,128]{1,0:T(8,128)S(1)}, f32[128,128]{1,0:T(8,128)S(1)}, u32[]{:S(2)}, u32[]{:S(2)}) collective-permute-start(f32[128,128]{1,0:T(8,128)S(1)} %merge.5.first.second), channel_id=1, source_target_pairs={{0,8},{4,12},{8,0},{12,4},{1,9},{5,13},{9,1},{13,5},{2,10},{6,14},... | collective-permute-start | bytes 196616 | tf_op jit(solution)/shard_map/ppermute | solution.py:548
  12.7 0.9 %copy-start.3 = (s32[32,1024]{1,0:T(8,128)S(1)}, s32[32,1024]{1,0:T(8,128)}, u32[]{:S(2)}) copy-start(s32[32,1024]{1,0:T(8,128)} %neighbours.3) | copy-start | bytes 393220
  13.6 3.5 %copy-start.6 = (bf16[512,128]{1,0:T(8,128)(2,1)S(1)}, bf16[512,128]{1,0:T(8,128)(2,1)}, u32[]{:S(2)}) copy-start(bf16[512,128]{1,0:T(8,128)(2,1)} %get-tuple-element.29.first) | copy-start | bytes 393220
  15.5 1.3 %collective-permute-start.2 = (f32[96,128]{1,0:T(8,128)S(1)}, f32[96,128]{1,0:T(8,128)S(1)}, u32[]{:S(2)}, u32[]{:S(2)}) collective-permute-start(f32[96,128]{1,0:T(8,128)S(1)} %get-tuple-element.26.first), channel_id=1, source_target_pairs={{0,1},{1,0},{2,3},{3,2},{4,5},{5,4},{6,7},{7,6},{8,9},{9,8},{10,11... | collective-permute-start | bytes 147464 | tf_op jit(solution)/shard_map/ppermute | solution.py:548
  15.6 8.1 %collective-permute-start.4 = (bf16[512,512]{1,0:T(8,128)(2,1)S(1)}, bf16[512,512]{1,0:T(8,128)(2,1)S(1)}, u32[]{:S(2)}, u32[]{:S(2)}) collective-permute-start(bf16[512,512]{1,0:T(8,128)(2,1)S(1)} %copy-done.2), channel_id=1, source_target_pairs={{0,1},{1,0},{2,3},{3,2},{4,5},{5,4},{6,7},{7,6},{8,9},{9,8},{10,11... | collective-permute-start | bytes 1572872 | tf_op jit(solution)/shard_map/ppermute | solution.py:548
  16.8 9.9 %copy-start.5 = (bf16[512,128]{1,0:T(8,128)(2,1)S(1)}, bf16[512,128]{1,0:T(8,128)(2,1)}, u32[]{:S(2)}) copy-start(bf16[512,128]{1,0:T(8,128)(2,1)} %get-tuple-element.31.refs_0_) | copy-start | bytes 393220
  16.8 6.8 %collective-permute-start.6 = (bf16[512,512]{1,0:T(8,128)(2,1)S(1)}, bf16[512,512]{1,0:T(8,128)(2,1)S(1)}, u32[]{:S(2)}, u32[]{:S(2)}) collective-permute-start(bf16[512,512]{1,0:T(8,128)(2,1)S(1)} %tie.3.refs_2_), channel_id=1, source_target_pairs={{0,1},{1,0},{2,3},{3,2},{4,5},{5,4},{6,7},{7,6},{8,9},{9,8},{10,11... | collective-permute-start | bytes 1572872 | tf_op jit(solution)/shard_map/ppermute | solution.py:548
  17.0 11.4 %collective-permute-start.7 = (bf16[512,128]{1,0:T(8,128)(2,1)S(1)}, bf16[512,128]{1,0:T(8,128)(2,1)S(1)}, u32[]{:S(2)}, u32[]{:S(2)}) collective-permute-start(bf16[512,128]{1,0:T(8,128)(2,1)S(1)} %tie.4), channel_id=1, source_target_pairs={{0,8},{4,12},{8,0},{12,4},{1,9},{5,13},{9,1},{13,5},{2,10},{6,14},... | collective-permute-start | bytes 393224 | tf_op jit(solution)/shard_map/ppermute | solution.py:548
  19.5 4.2 %collective-permute-start.3 = (f32[112,128]{1,0:T(8,128)S(1)}, f32[112,128]{1,0:T(8,128)S(1)}, u32[]{:S(2)}, u32[]{:S(2)}) collective-permute-start(f32[112,128]{1,0:T(8,128)S(1)} %merge.6.first.second), channel_id=1, source_target_pairs={{0,2},{1,3},{2,0},{3,1},{4,6},{5,7},{6,4},{7,5},{8,10},{9,11},{10,... | collective-permute-start | bytes 172040 | tf_op jit(solution)/shard_map/ppermute | solution.py:548
  24.5 10.5 %copy-start.7 = (s32[3,1024]{1,0:T(4,128)S(1)}, s32[3,1024]{1,0:T(4,128)}, u32[]{:S(2)}) copy-start(s32[3,1024]{1,0:T(4,128)} %owner.1) | copy-start | bytes 36868
  24.5 10.5 %copy-start.8 = (f32[3,1024]{1,0:T(4,128)S(1)}, f32[3,1024]{1,0:T(4,128)}, u32[]{:S(2)}) copy-start(f32[3,1024]{1,0:T(4,128)} %centres.1) | copy-start | bytes 36868
  24.5 10.5 %copy-start.11 = (f32[3,1024]{1,0:T(4,128)S(1)}, f32[3,1024]{1,0:T(4,128)}, u32[]{:S(2)}) copy-start(f32[3,1024]{1,0:T(4,128)} %velocity.1) | copy-start | bytes 36868
  24.5 10.5 %copy-start.12 = (f32[3,1024]{1,0:T(4,128)S(1)}, f32[3,1024]{1,0:T(4,128)}, u32[]{:S(2)}) copy-start(f32[3,1024]{1,0:T(4,128)} %angmom.1) | copy-start | bytes 36868
  24.5 10.5 %copy-start.13 = (f32[4,1024]{1,0:T(4,128)S(1)}, f32[4,1024]{1,0:T(4,128)}, u32[]{:S(2)}) copy-start(f32[4,1024]{1,0:T(4,128)} %get-tuple-element.32.quat) | copy-start | bytes 49156
  24.6 3.9 %collective-permute-start.8 = (f32[16,128]{1,0:T(8,128)S(1)}, f32[16,128]{1,0:T(8,128)S(1)}, u32[]{:S(2)}, u32[]{:S(2)}) collective-permute-start(f32[16,128]{1,0:T(8,128)S(1)} %get-tuple-element.30.first), channel_id=1, source_target_pairs={{0,4},{4,0},{8,12},{12,8},{1,5},{5,1},{9,13},{13,9},{2,6},{6,2},{1... | collective-permute-start | bytes 24584 | tf_op jit(solution)/shard_map/ppermute | solution.py:548
  26.7 6.0 %collective-permute-start.10 = (bf16[512,128]{1,0:T(8,128)(2,1)S(1)}, bf16[512,128]{1,0:T(8,128)(2,1)S(1)}, u32[]{:S(2)}, u32[]{:S(2)}) collective-permute-start(bf16[512,128]{1,0:T(8,128)(2,1)S(1)} %copy-done.5), channel_id=1, source_target_pairs={{0,4},{4,0},{8,12},{12,8},{1,5},{5,1},{9,13},{13,9},{2,6},{6,2},{1... | collective-permute-start | bytes 393224 | tf_op jit(solution)/shard_map/ppermute | solution.py:548
  28.5 7.7 %collective-permute-start.9 = (bf16[512,128]{1,0:T(8,128)(2,1)S(1)}, bf16[512,128]{1,0:T(8,128)(2,1)S(1)}, u32[]{:S(2)}, u32[]{:S(2)}) collective-permute-start(bf16[512,128]{1,0:T(8,128)(2,1)S(1)} %tie.5.refs_2_), channel_id=1, source_target_pairs={{0,4},{4,0},{8,12},{12,8},{1,5},{5,1},{9,13},{13,9},{2,6},{6,2},{1... | collective-permute-start | bytes 393224 | tf_op jit(solution)/shard_map/ppermute | solution.py:548
  30.4 4.6 %collective-permute-start.11 = (f32[32,128]{1,0:T(8,128)S(1)}, f32[32,128]{1,0:T(8,128)S(1)}, u32[]{:S(2)}, u32[]{:S(2)}) collective-permute-start(f32[32,128]{1,0:T(8,128)S(1)} %merge.8.second.first), channel_id=1, source_target_pairs={{0,8},{4,12},{8,0},{12,4},{1,9},{5,13},{9,1},{13,5},{2,10},{6,14},... | collective-permute-start | bytes 49160 | tf_op jit(solution)/shard_map/ppermute | solution.py:548
